TPU v7x, 32 devices: a whole 2x2x4 slice. The times are simulated.
32 devices in a mesh: parts: 2 (over x), tensor: 8 (over z, y), dp: 2 (over core).
Axes of the slice: x: 2, y: 2, z: 4, core: 2. Of those that a mesh axis runs over, the one named last changes fastest.
Arguments:
- train_inputs: bfloat16 [24, 1024, 28672], P(('parts', 'dp'), None, 'tensor'), parts along dimension 0, may hold values from -6 to 6
- train_outgrads: bfloat16 [24, 1024, 8192], P(('parts', 'dp'), None, 'tensor'), parts along dimension 0, may hold values from -6 to 6
- test_inputs: bfloat16 [8, 1024, 28672], P(('parts', 'dp'), None, 'tensor'), parts along dimension 0, may hold values from -6 to 6
- test_outgrads: bfloat16 [8, 1024, 8192], P(('parts', 'dp'), None, 'tensor'), parts along dimension 0, may hold values from -6 to 6
- train_counts: int32 [24], P(('parts', 'dp')), parts along dimension 0, may hold values from 256 to 1024, as said below
- test_counts: int32 [8], P(('parts', 'dp')), parts along dimension 0, may hold values from 256 to 1024, as said below
- proj_in: bfloat16 [64, 28672], P(None, 'tensor'), may hold values from -0.03125 to 0.03125
- proj_out: bfloat16 [64, 8192], P(None, 'tensor'), may hold values from -0.0625 to 0.0625
- fisher_prior: float32 [8192, 4096], P(('parts', 'tensor')), parts along dimension 0, as said below
Outputs:
- scores: float32 [8, 12], P(('parts', 'dp')), parts along dimension 0
- preconditioned: float32 [8, 4096], P(('parts', 'dp'), 'tensor'), parts along dimension 0
There are 2 independent parts, one for each index of `parts`. A program takes and returns all parts, laid end to end along the dimension named above; an argument that names none is the same for every part. Nothing has to cross between parts.
Inputs may be any that keep to these rules, and one draw needn't show every extreme that they name: `train_counts`: in each aligned block of 6 training sequences one has all 1024 tokens live. `test_counts`: in each aligned block of 2 test sequences one has all 1024 tokens live. `fisher_prior`: symmetric and positive definite.
All inputs are finite; a program needn't handle non-finite values.
Results may differ from a plain program's by a relative error of at most 0.0003.
Values sent between devices are 32-bit elements; how exact they have to be, the bound alone decides.
No kernel may reach another device: no remote copies, remote signals or barrier semaphores. Data moves between devices by JAX's collectives and lax.ppermute only.
A program may use at most 192 MiB of HBM per device.

v0:
```python
import math

import jax
import jax.numpy as jnp
from jax import lax
from jax.sharding import PartitionSpec as P

RANK = 64
ITERS = 6


def project(data, basis):
    rows = data.reshape(-1, data.shape[-1])
    return lax.dot_general(
        rows, basis, (((1,), (1,)), ((), ())), preferred_element_type=jnp.float32
    )


def outer_sums(left, right, counts, length):
    examples = counts.shape[0]
    left = left.reshape(examples, length, -1)
    right = right.reshape(examples, length, -1)
    live = (jnp.arange(length, dtype=jnp.int32)[None, :] < counts[:, None]).astype(jnp.float32)
    grads = jnp.einsum(
        "etr,ets->ers", left * live[:, :, None], right, precision=lax.Precision.HIGHEST
    )
    return grads.reshape(examples, -1) * (1.0 / math.sqrt(length))


def per_device(
    train_inputs,
    train_outgrads,
    test_inputs,
    test_outgrads,
    train_counts,
    test_counts,
    proj_in,
    proj_out,
    fisher_prior,
):
    high = lax.Precision.HIGHEST
    length = train_inputs.shape[1]
    left_train = project(train_outgrads, proj_out)
    right_train = project(train_inputs, proj_in)
    left_test = project(test_outgrads, proj_out)
    right_test = project(test_inputs, proj_in)
    left_train, right_train, left_test, right_test = lax.psum(
        (left_train, right_train, left_test, right_test), "tensor"
    )
    train_grads = outer_sums(left_train, right_train, train_counts, length)
    test_grads = outer_sums(left_test, right_test, test_counts, length)
    every_train = lax.all_gather(train_grads, "dp", axis=0, tiled=True)
    total_train = every_train.shape[0]
    own_rows = fisher_prior.shape[0]
    start = lax.axis_index("tensor") * own_rows
    own_train = lax.dynamic_slice_in_dim(every_train, start, own_rows, 1)
    fisher_rows = fisher_prior + jnp.dot(own_train.T, every_train, precision=high) / total_train
    residue = lax.dynamic_slice_in_dim(test_grads, start, own_rows, 1)
    search = residue
    solution = jnp.zeros_like(residue)
    norm_now = jnp.sum(test_grads * test_grads, axis=1)
    for step in range(ITERS):
        image = lax.dot_general(
            lax.all_gather(search, "tensor", axis=1, tiled=True),
            fisher_rows,
            (((1,), (1,)), ((), ())),
            precision=high,
        )
        curve, cross, square = lax.psum(
            (
                jnp.sum(search * image, axis=1),
                jnp.sum(residue * image, axis=1),
                jnp.sum(image * image, axis=1),
            ),
            "tensor",
        )
        alpha = norm_now / curve
        solution = solution + alpha[:, None] * search
        residue = residue - alpha[:, None] * image
        norm_next = norm_now - 2.0 * alpha * cross + alpha * alpha * square
        search = residue + (norm_next / norm_now)[:, None] * search
        norm_now = norm_next
    partial_value = jnp.dot(solution, own_train.T, precision=high)
    scores = lax.psum(partial_value, "tensor") / RANK
    return (scores, solution)


def solution(mesh):
    in_specs = (
        P(("parts", "dp"), None, "tensor"),
        P(("parts", "dp"), None, "tensor"),
        P(("parts", "dp"), None, "tensor"),
        P(("parts", "dp"), None, "tensor"),
        P(("parts", "dp")),
        P(("parts", "dp")),
        P(None, "tensor"),
        P(None, "tensor"),
        P(("parts", "tensor"), None),
    )
    out_specs = (P(("parts", "dp"), None), P(("parts", "dp"), "tensor"))
    return jax.shard_map(
        per_device, mesh=mesh, in_specs=in_specs, out_specs=out_specs, check_vma=False
    )
```

profile of v0, /device:TPU:0, one launch (start us, length us, event | category | flops | bytes accessed | tf_op | source)
XLA Modules:
  0.0 627.4 jit_solution(14249428662126695028)
XLA Ops:
  8.2 10.5 %fusion.20 = f32[2048,64]{0,1:T(8,128)} fusion(bf16[2048,3584]{1,0:T(8,128)(2,1)} %bitcast.41, bf16[64,3584]{1,0:T(8,128)(2,1)S(1)} %copy-done), kind=kOutput, calls=%fused_computation.59 | convolution fusion | flops 939524096 | bytes 15663104 | tf_op jit(solution)/shard_map/dot_general | solution.py:14
  18.7 22.1 %fusion.22 = f32[6144,64]{0,1:T(8,128)} fusion(bf16[6144,3584]{1,0:T(8,128)(2,1)} %bitcast.40, bf16[64,3584]{1,0:T(8,128)(2,1)S(1)} %copy-done), kind=kOutput, calls=%fused_computation.61 | convolution fusion | flops 2818572288 | bytes 46071808 | tf_op jit(solution)/shard_map/dot_general | solution.py:14
  45.8 8.6 %fusion.21 = f32[6144,64]{0,1:T(8,128)S(1)} fusion(bf16[6144,1024]{1,0:T(8,128)(2,1)} %bitcast.42, bf16[64,1024]{1,0:T(8,128)(2,1)S(1)} %copy-done.6), kind=kOutput, calls=%fused_computation.60 | convolution fusion | flops 805306368 | bytes 14286848 | tf_op jit(solution)/shard_map/dot_general | solution.py:14
  57.9 173.4 %all-reduce.8.cloned.1.call-done = (f32[2,1024,64]{1,2,0:T(8,128)}, f32[2,1024,64]{1,2,0:T(8,128)}, f32[6,1024,64]{1,2,0:T(8,128)}, f32[6,1024,64]{1,0,2:T(8,128)}) async-done(((f32[2,1024,64]{1,2,0:T(8,128)}, f32[2,1024,64]{1,2,0:T(8,128)}, f32[6,1024,64]{1,2,0:T(8,128)}, f32[6,1024,64]{1,0,2:T(8,128)}), (f32[2,1024,64]{1,2,0:T(8,128)}, f32[2,1024,64]{1,2,0:T(8,128)}, f32[6,1024,64]{1,2,0:T(8,128)}, ...) | async-done | bytes 4194320 | tf_op jit(solution)/shard_map/psum | solution.py:47
  233.3 30.6 %all_gather.21 = f32[2,4096]{1,0:T(2,128)S(1)} all-gather(f32[2,512]{1,0:T(2,128)S(1)} %constant_dynamic-slice_fusion), channel_id=1, replica_groups=mesh['parts'=2,'tensor'=8,'dp'=2] {'tensor'}, dimensions={1}, use_global_device_ids=true | all-gather | bytes 36864 | tf_op jit(solution)/shard_map/all_gather | solution.py:64
  271.7 9.5 %multiply_add_fusion = f32[512,4096]{1,0:T(8,128)S(1)} fusion(f32[512,4096]{1,0:T(8,128)} %param.17, f32[12,4096]{1,0:T(8,128)S(1)} %reshape.98, s32[]{:T(128)S(6)} %select_n.4), kind=kOutput, calls=%fused_computation | convolution fusion | flops 306184192 | bytes 17072132 | tf_op jit(solution)/shard_map/dot_general | solution.py:57
  284.4 7.1 %multiply_reduce_fusion.14 = (f32[2]{0:T(128)S(1)}, f32[2]{0:T(128)S(1)}, f32[2,512]{1,0:T(2,128)S(1)}) fusion(f32[2,512]{1,0:T(2,128)S(1)} %constant_dynamic-slice_fusion, f32[2,4096]{1,0:T(2,128)S(1)} %all_gather.21, f32[512,4096]{1,0:T(8,128)S(1)} %multiply_add_fusion), kind=kOutput, calls=%fused_computation.43 | convolution fusion | flops 50335740 | bytes 8429584 | tf_op jit(solution)/shard_map/dot_general | solution.py:63
  291.5 19.6 %all-reduce.4 = (f32[2]{0:T(128)S(1)}, f32[2]{0:T(128)S(1)}) all-reduce(f32[2]{0:T(128)S(1)} %get-tuple-element.15, f32[2]{0:T(128)S(1)} %get-tuple-element.14), channel_id=1, replica_groups=mesh['parts'=2,'tensor'=8,'dp'=2] {'tensor'}, use_global_device_ids=true, to_apply=%region_8.0 | all-reduce | flops 4 | bytes 32 | tf_op jit(solution)/shard_map/psum | solution.py:69
  311.1 30.4 %all_gather.23 = f32[2,4096]{1,0:T(2,128)S(1)} all-gather(f32[2,512]{1,0:T(2,128)S(1)} %multiply_add_fusion.6), channel_id=1, replica_groups=mesh['parts'=2,'tensor'=8,'dp'=2] {'tensor'}, dimensions={1}, use_global_device_ids=true | all-gather | bytes 36864 | tf_op jit(solution)/shard_map/all_gather | solution.py:64
  341.5 9.4 %multiply_reduce_fusion.11 = (f32[2]{0:T(128)S(1)}, f32[2]{0:T(128)S(1)}, f32[2]{0:T(128)S(1)}, f32[2,512]{1,0:T(2,128)S(1)}) fusion(f32[2,512]{1,0:T(2,128)S(1)} %constant_dynamic-slice_fusion, f32[2,512]{1,0:T(2,128)S(1)} %get-tuple-element.57, f32[2]{0:T(128)S(1)} %get-tuple-element.54, f32[2,512]{1,0:T(2,128)S(1)} %multiply_add_fusion.6, ...), kind=kOutput, calls=%fused_computation.38 | convolution fusion | flops 50339832 | bytes 8437792 | tf_op jit(solution)/shard_map/dot_general | solution.py:63
  350.9 17.1 %all-reduce.3 = (f32[2]{0:T(128)S(1)}, f32[2]{0:T(128)S(1)}, f32[2]{0:T(128)S(1)}) all-reduce(f32[2]{0:T(128)S(1)} %get-tuple-element.13, f32[2]{0:T(128)S(1)} %get-tuple-element.12, f32[2]{0:T(128)S(1)} %get-tuple-element.11), channel_id=1, replica_groups=mesh['parts'=2,'tensor'=8,'dp'=2] {'tensor'}, use_global_device_ids=true, to_apply=%region_10.0 | all-reduce | flops 6 | bytes 48 | tf_op jit(solution)/shard_map/psum | solution.py:69
  368.1 30.4 %all_gather.24 = f32[2,4096]{1,0:T(2,128)S(1)} all-gather(f32[2,512]{1,0:T(2,128)S(1)} %get-tuple-element.47), channel_id=1, replica_groups=mesh['parts'=2,'tensor'=8,'dp'=2] {'tensor'}, dimensions={1}, use_global_device_ids=true | all-gather | bytes 36864 | tf_op jit(solution)/shard_map/all_gather | solution.py:64
  398.5 9.4 %multiply_reduce_fusion.8 = (f32[2]{0:T(128)S(1)}, f32[2]{0:T(128)S(1)}, f32[2]{0:T(128)S(1)}, f32[2,512]{1,0:T(2,128)S(1)}) fusion(f32[2,512]{1,0:T(2,128)S(1)} %get-tuple-element.48, f32[2,512]{1,0:T(2,128)S(1)} %get-tuple-element.47, f32[2,4096]{1,0:T(2,128)S(1)} %all_gather.24, f32[512,4096]{1,0:T(8,128)} %copy-done.2), kind=kOutput, calls=%fused_computation.33 | convolution fusion | flops 50337784 | bytes 8433688 | tf_op jit(solution)/shard_map/dot_general | solution.py:63
  407.9 19.1 %all-reduce.2 = (f32[2]{0:T(128)S(1)}, f32[2]{0:T(128)S(1)}, f32[2]{0:T(128)S(1)}) all-reduce(f32[2]{0:T(128)S(1)} %get-tuple-element.10, f32[2]{0:T(128)S(1)} %get-tuple-element.9, f32[2]{0:T(128)S(1)} %get-tuple-element.8), channel_id=1, replica_groups=mesh['parts'=2,'tensor'=8,'dp'=2] {'tensor'}, use_global_device_ids=true, to_apply=%region_16.0 | all-reduce | flops 6 | bytes 48 | tf_op jit(solution)/shard_map/psum | solution.py:69
  427.1 30.4 %all_gather.25 = f32[2,4096]{1,0:T(2,128)S(1)} all-gather(f32[2,512]{1,0:T(2,128)S(1)} %get-tuple-element.42), channel_id=1, replica_groups=mesh['parts'=2,'tensor'=8,'dp'=2] {'tensor'}, dimensions={1}, use_global_device_ids=true | all-gather | bytes 36864 | tf_op jit(solution)/shard_map/all_gather | solution.py:64
  457.5 9.4 %multiply_reduce_fusion.5 = (f32[2]{0:T(128)S(1)}, f32[2]{0:T(128)S(1)}, f32[2]{0:T(128)S(1)}, f32[2,512]{1,0:T(2,128)S(1)}) fusion(f32[2,512]{1,0:T(2,128)S(1)} %get-tuple-element.43, f32[2,512]{1,0:T(2,128)S(1)} %get-tuple-element.42, f32[2,4096]{1,0:T(2,128)S(1)} %all_gather.25, f32[512,4096]{1,0:T(8,128)} %copy-done.2), kind=kOutput, calls=%fused_computation.28 | convolution fusion | flops 50337784 | bytes 8433688 | tf_op jit(solution)/shard_map/dot_general | solution.py:63
  466.8 17.1 %all-reduce.1 = (f32[2]{0:T(128)S(1)}, f32[2]{0:T(128)S(1)}, f32[2]{0:T(128)S(1)}) all-reduce(f32[2]{0:T(128)S(1)} %get-tuple-element.7, f32[2]{0:T(128)S(1)} %get-tuple-element.6, f32[2]{0:T(128)S(1)} %get-tuple-element.5), channel_id=1, replica_groups=mesh['parts'=2,'tensor'=8,'dp'=2] {'tensor'}, use_global_device_ids=true, to_apply=%region_22.0 | all-reduce | flops 6 | bytes 48 | tf_op jit(solution)/shard_map/psum | solution.py:69
  484.1 30.7 %all_gather.26 = f32[2,4096]{1,0:T(2,128)S(1)} all-gather(f32[2,512]{1,0:T(2,128)S(1)} %get-tuple-element.37), channel_id=1, replica_groups=mesh['parts'=2,'tensor'=8,'dp'=2] {'tensor'}, dimensions={1}, use_global_device_ids=true | all-gather | bytes 36864 | tf_op jit(solution)/shard_map/all_gather | solution.py:64
  514.7 9.4 %multiply_reduce_fusion.2 = (f32[2]{0:T(128)S(1)}, f32[2]{0:T(128)S(1)}, f32[2]{0:T(128)S(1)}, f32[2,512]{1,0:T(2,128)S(1)}) fusion(f32[2,512]{1,0:T(2,128)S(1)} %get-tuple-element.38, f32[2,512]{1,0:T(2,128)S(1)} %get-tuple-element.37, f32[2,4096]{1,0:T(2,128)S(1)} %all_gather.26, f32[512,4096]{1,0:T(8,128)} %copy-done.2), kind=kOutput, calls=%fused_computation.23 | convolution fusion | flops 50337784 | bytes 8433688 | tf_op jit(solution)/shard_map/dot_general | solution.py:63
  524.1 19.1 %all-reduce = (f32[2]{0:T(128)S(1)}, f32[2]{0:T(128)S(1)}, f32[2]{0:T(128)S(1)}) all-reduce(f32[2]{0:T(128)S(1)} %get-tuple-element.3, f32[2]{0:T(128)S(1)} %get-tuple-element.4, f32[2]{0:T(128)S(1)} %get-tuple-element.2), channel_id=1, replica_groups=mesh['parts'=2,'tensor'=8,'dp'=2] {'tensor'}, use_global_device_ids=true, to_apply=%region_32.0 | all-reduce | flops 6 | bytes 48 | tf_op jit(solution)/shard_map/psum | solution.py:69
  543.4 30.4 %all_gather.27 = f32[2,4096]{1,0:T(2,128)S(1)} all-gather(f32[2,512]{1,0:T(2,128)S(1)} %multiply_add_fusion.2), channel_id=1, replica_groups=mesh['parts'=2,'tensor'=8,'dp'=2] {'tensor'}, dimensions={1}, use_global_device_ids=true | all-gather | bytes 36864 | tf_op jit(solution)/shard_map/all_gather | solution.py:64
  573.8 9.3 %fusion.5 = f32[2]{0:T(128)S(1)} fusion(f32[2,512]{1,0:T(2,128)S(1)} %multiply_add_fusion.2, f32[2,4096]{1,0:T(2,128)S(1)} %all_gather.27, f32[512,4096]{1,0:T(8,128)} %copy-done.2), kind=kOutput, calls=%fused_computation.7 | convolution fusion | flops 50333696 | bytes 8425480 | tf_op jit(solution)/shard_map/dot_general | solution.py:63
  583.1 17.1 %psum.161 = f32[2]{0:T(128)S(1)} all-reduce(f32[2]{0:T(128)S(1)} %fusion.5), channel_id=1, replica_groups=mesh['parts'=2,'tensor'=8,'dp'=2] {'tensor'}, use_global_device_ids=true, to_apply=%region_34.0 | all-reduce | flops 2 | bytes 16 | tf_op jit(solution)/shard_map/psum | solution.py:69
  600.4 19.1 %psum.162 = f32[2,12]{1,0:T(2,128)S(1)} all-reduce(f32[2,12]{1,0:T(2,128)S(1)} %fusion.9), channel_id=1, replica_groups=mesh['parts'=2,'tensor'=8,'dp'=2] {'tensor'}, use_global_device_ids=true, to_apply=%region_35.0 | all-reduce | flops 24 | bytes 192 | tf_op jit(solution)/shard_map/psum | solution.py:84
  (50 shorter events, 23.7 us)
Async XLA Ops:
  7.2 1.0 copy-start
  7.2 224.1 %all-reduce.8.cloned.1.call-start = ((), (), s32[]{:S(2)}) async-start(), calls=%async_computation | async-start | bytes 9437184 | tf_op jit(solution)/shard_map/psum | solution.py:47
  18.7 24.9 %copy-start.3 = (bf16[2,1024,1024]{2,1,0:T(8,128)(2,1)S(1)}, bf16[2,1024,1024]{2,1,0:T(8,128)(2,1)}, u32[]{:S(2)}) copy-start(bf16[2,1024,1024]{2,1,0:T(8,128)(2,1)} %param.12) | copy-start | bytes 12582916
  18.7 24.9 %copy-start.6 = (bf16[64,1024]{1,0:T(8,128)(2,1)S(1)}, bf16[64,1024]{1,0:T(8,128)(2,1)}, u32[]{:S(2)}) copy-start(bf16[64,1024]{1,0:T(8,128)(2,1)} %param.16) | copy-start | bytes 393220
  45.8 10.8 %copy-start.4 = (f32[2048,64]{0,1:T(8,128)S(1)}, f32[2048,64]{0,1:T(8,128)}, u32[]{:S(2)}) copy-start(f32[2048,64]{0,1:T(8,128)} %fusion.20) | copy-start | bytes 1572868
  45.8 10.8 %copy-start.5 = (f32[2048,64]{0,1:T(8,128)S(1)}, f32[2048,64]{0,1:T(8,128)}, u32[]{:S(2)}) copy-start(f32[2048,64]{0,1:T(8,128)} %fusion.19) | copy-start | bytes 1572868
  54.4 3.4 copy-start.9
  54.4 3.4 copy-start.8
  281.2 3.2 copy-start.2
  514.7 105.4 %copy-start.1 = (bf16[64,3584]{1,0:T(8,128)(2,1)S(1)}, bf16[64,3584]{1,0:T(8,128)(2,1)}, u32[]{:S(2)}) copy-start(bf16[64,3584]{1,0:T(8,128)(2,1)} %param.15) | copy-start | bytes 1376260
  600.3 19.9 %copy-start.7 = (f32[2,512]{1,0:T(2,128)}, f32[2,512]{1,0:T(2,128)S(1)}, u32[]{:S(2)}) copy-start(f32[2,512]{1,0:T(2,128)S(1)} %multiply_add_fusion.1) | copy-start | bytes 12292
Sparse Core Ops, SparseCore 0:
  57.9 173.4 all-reduce.7
where the time goes:
time: 636 us; the launch traced here: 627 us
  blocking collectives  313 us (49%)
  waiting for transfers between devices  173 us (27%)
  matrix products  113 us (18%)
  between operations  14.6 us (2%)
  local copies, waits for them, and re-layouts  10.5 us (2%)
    all_gather x6, blocking collectives, per_device(): lax.all_gather(search, 'tensor', axis=1, tiled=True)  183 us
    psum x1, waiting for transfers between devices, per_device(): lax.psum((left_train, right_train, left_test, right_test), 'tensor')  173 us
    psum x6, blocking collectives, per_device(): lax.psum((jnp.sum(search * image, axis=1), jnp.sum(residue * image, axis=...  109 us
    dot_general x6, matrix products, per_device(): lax.dot_general(lax.all_gather(search, 'tensor', axis=1, tiled=True), fis...  53.8 us
    dot_general x4, matrix products, project(): lax.dot_general(rows, basis, (((1,), (1,)), ((), ())), preferred_element_...  43.4 us
    psum x1, blocking collectives, per_device(): scores = lax.psum(partial_value, 'tensor') / RANK  19.1 us
  transfers between devices with their start and end apart: 1, of which 1 were waited for; matrix products, arithmetic and copies ran while one was open for 0% of the time, Pallas kernels for 0%

commit v1 on v0

v1 whole, which is shorter than its diff:
```python
import functools
import math

import jax
import jax.numpy as jnp
from jax import lax
from jax.experimental import pallas as pl
from jax.experimental.pallas import tpu as pltpu
from jax.sharding import PartitionSpec as P

RANK = 64
ITERS = 6
LANES = 128
CHUNKS = (256, 256, 256, 256)
TILE = 256
SLOTS = 3

HIGH = lax.Precision.HIGHEST
VMEM = pl.BlockSpec(memory_space=pltpu.VMEM)
SMEM = pl.BlockSpec(memory_space=pltpu.SMEM)
ANY = pl.BlockSpec(memory_space=pl.ANY)


def project(data, basis):
    rows = data.reshape(-1, data.shape[-1])
    return lax.dot_general(
        rows, basis, (((1,), (1,)), ((), ())), preferred_element_type=jnp.float32
    )


def outer_sums(left, right, counts, length):
    examples = counts.shape[0]
    left = left.reshape(examples, length, -1)
    right = right.reshape(examples, length, -1)
    live = (jnp.arange(length, dtype=jnp.int32)[None, :] < counts[:, None]).astype(jnp.float32)
    grads = jnp.einsum("etr,ets->ers", left * live[:, :, None], right, precision=HIGH)
    return grads.reshape(examples, -1) * (1.0 / math.sqrt(length))


def plain(
    train_inputs,
    train_outgrads,
    test_inputs,
    test_outgrads,
    train_counts,
    test_counts,
    proj_in,
    proj_out,
    fisher_prior,
):
    length = train_inputs.shape[1]
    left_train = project(train_outgrads, proj_out)
    right_train = project(train_inputs, proj_in)
    left_test = project(test_outgrads, proj_out)
    right_test = project(test_inputs, proj_in)
    left_train, right_train, left_test, right_test = lax.psum(
        (left_train, right_train, left_test, right_test), "tensor"
    )
    train_grads = outer_sums(left_train, right_train, train_counts, length)
    test_grads = outer_sums(left_test, right_test, test_counts, length)
    every_train = lax.all_gather(train_grads, "dp", axis=0, tiled=True)
    total_train = every_train.shape[0]
    own_rows = fisher_prior.shape[0]
    start = lax.axis_index("tensor") * own_rows
    own_train = lax.dynamic_slice_in_dim(every_train, start, own_rows, 1)
    fisher_rows = fisher_prior + jnp.dot(own_train.T, every_train, precision=HIGH) / total_train
    residue = test_grads
    search = test_grads
    solution = jnp.zeros_like(test_grads)
    norm_now = jnp.sum(test_grads * test_grads, axis=1)
    for step in range(ITERS):
        part = lax.dot_general(search, fisher_rows, (((1,), (1,)), ((), ())), precision=HIGH)
        image = lax.all_gather(part, "tensor", axis=1, tiled=True)
        alpha = norm_now / jnp.sum(search * image, axis=1)
        solution = solution + alpha[:, None] * search
        residue = residue - alpha[:, None] * image
        norm_next = jnp.sum(residue * residue, axis=1)
        search = residue + (norm_next / norm_now)[:, None] * search
        norm_now = norm_next
    scores = jnp.dot(solution, every_train.T, precision=HIGH) / RANK
    return (scores, lax.dynamic_slice_in_dim(solution, start, own_rows, 1))


def project_kernel(
    flip, first, size, tile, train_count, test_count, train_in, train_out, test_in, test_out,
    basis_in, basis_out, out, held_in, held_out, sems,
):
    low = lax.rem(lax.axis_index("tensor"), 2)
    low = 1 - low if flip else low
    each = size // tile
    total = 4 * each
    last = train_in.shape[0] // 2

    def place(k):
        return k // each, first + lax.rem(k, each) * tile

    def live(k):
        i, row = place(k)
        count = jnp.where(
            i < last, train_count[jnp.minimum(2 * i + low, 2 * last - 1)], test_count[low]
        )
        return count > row

    def copies(k, train):
        i, row = place(k)
        slot = lax.rem(k, SLOTS)
        rows = pl.ds(row, tile)
        wide, narrow, e = (train_in, train_out, 2 * i + low) if train else (test_in, test_out, low)
        return (
            pltpu.make_async_copy(wide.at[e, rows], held_in.at[slot], sems.at[slot, 0]),
            pltpu.make_async_copy(narrow.at[e, rows], held_out.at[slot], sems.at[slot, 1]),
        )

    def start(k):
        i, _ = place(k)

        @pl.when(live(k) & (i < last))
        def _():
            for copy in copies(k, True):
                copy.start()

        @pl.when(live(k) & (i == last))
        def _():
            for copy in copies(k, False):
                copy.start()

    for k in range(SLOTS - 1):
        start(jnp.int32(k))

    @pl.loop(0, total)
    def _(k):
        i, row = place(k)
        slot = lax.rem(k, SLOTS)

        @pl.when(k + SLOTS - 1 < total)
        def _():
            start(k + SLOTS - 1)

        there = pl.ds(row - first, tile)

        @pl.when(live(k))
        def _():
            for copy in copies(k, False):
                copy.wait()
            out[i, there, :] = jnp.dot(
                held_out[slot], basis_out[...], preferred_element_type=jnp.float32
            ) + jnp.dot(held_in[slot], basis_in[...], preferred_element_type=jnp.float32)

        @pl.when(jnp.logical_not(live(k)))
        def _():
            out[i, there, :] = jnp.zeros((tile, LANES), jnp.float32)


def project_rows(flip, first, size, tile, operands):
    wide, narrow = operands[2], operands[3]
    return pl.pallas_call(
        functools.partial(project_kernel, flip, first, size, tile),
        out_shape=jax.ShapeDtypeStruct((4, size, LANES), jnp.float32),
        in_specs=[SMEM, SMEM, ANY, ANY, ANY, ANY, VMEM, VMEM],
        out_specs=VMEM,
        scratch_shapes=[
            pltpu.VMEM((SLOTS, tile, wide.shape[2]), wide.dtype),
            pltpu.VMEM((SLOTS, tile, narrow.shape[2]), narrow.dtype),
            pltpu.SemaphoreType.DMA((SLOTS, 2)),
        ],
        compiler_params=pltpu.CompilerParams(vmem_limit_bytes=24 * 2**20),
        cost_estimate=pl.CostEstimate(
            flops=2 * 4 * size * 4608 * 64, bytes_accessed=4 * size * 4608 * 2, transcendentals=0
        ),
        name=f"project_{'send' if flip else 'keep'}_{first}",
    )(*operands)


def gram_kernel(count, rows, out, held):
    live = lax.broadcasted_iota(jnp.int32, rows.shape, 0) < count[0]
    vectors = jnp.where(live, rows[...], 0.0)
    held[...] = lax.dot_general(
        vectors[:, :RANK], vectors[:, RANK:], (((0,), (0,)), ((), ())), precision=HIGH,
        preferred_element_type=jnp.float32,
    ) * (1.0 / math.sqrt(rows.shape[0]))
    half = RANK // 2
    grad = jnp.concatenate(
        [held[pl.ds(0, half, stride=2), :], held[pl.ds(1, half, stride=2), :]], axis=1
    )
    for i in range(out.shape[0]):
        out[i] = grad


def gram(count, rows, n):
    return pl.pallas_call(
        gram_kernel,
        out_shape=jax.ShapeDtypeStruct((n, RANK // 2, LANES), jnp.float32),
        in_specs=[SMEM, VMEM],
        out_specs=VMEM,
        scratch_shapes=[pltpu.VMEM((RANK, RANK), jnp.float32)],
        name="gram",
    )(count, rows)


def pair_sums(x):
    x = jnp.sum(x, axis=-1, keepdims=True)
    upper = lax.broadcasted_iota(jnp.int32, x.shape, x.ndim - 2) < 4
    first = jnp.sum(jnp.where(upper, x, 0.0), axis=-2, keepdims=True)
    second = jnp.sum(jnp.where(upper, 0.0, x), axis=-2, keepdims=True)
    return jnp.where(upper, first, second)


def inner(a, b):
    return pair_sums(jnp.sum(a * b, axis=0))


def weights_of(grads, vector):
    return pair_sums(
        jnp.stack([jnp.sum(grads[i] * vector, axis=0) for i in range(grads.shape[0])])
    )


def fisher_rows(prior, grads, vector, weights, image):
    me = lax.axis_index("tensor")
    ones = jnp.ones((8, LANES), jnp.float32)

    @pl.loop(0, prior.shape[0] // LANES)
    def _(block):
        rows = pl.ds(pl.multiple_of(block * LANES, LANES), LANES)
        sums = [jnp.zeros((LANES, LANES), jnp.float32)] * 2
        for c in range(prior.shape[1] // LANES):
            piece = prior[rows, pl.ds(c * LANES, LANES)]
            for j in range(2):
                sums[j] = sums[j] + piece * vector[c // 4, pl.ds(j * 4 + c % 4, 1), :]
        for j in range(2):
            line = lax.dot_general(
                ones, sums[j], (((1,), (1,)), ((), ())), precision=HIGH,
                preferred_element_type=jnp.float32,
            )
            image[pl.ds(j * 4 + block, 1), :] = line[:1]

    total = grads.shape[0]
    low = weights[0] * grads[0, me]
    for i in range(1, total):
        low = low + weights[i] * grads[i, me]
    image[...] = image[...] + low * (1.0 / total)


def begin_kernel(own, other, prior, grads, search, payload, image):
    me = lax.axis_index("dp")
    per = other.shape[0]
    for i in range(per):
        for s in range(8):
            for half in range(2):
                grads[me * per + i, s, pl.ds(half * 4, 4), :] = own[i, pl.ds(s * 4, 4), :]
                grads[(1 - me) * per + i, s, pl.ds(half * 4, 4), :] = other[i, pl.ds(s * 4, 4), :]
    for j in range(2):
        for s in range(8):
            search[s, pl.ds(j * 4, 4), :] = own[per + j, pl.ds(s * 4, 4), :]
    fisher_rows(prior, grads, search, weights_of(grads, search[...]), image)
    for s in range(8):
        payload[s] = image[...]


def advance(first, images, solution, residue, search, new_solution, new_residue, new_search):
    old = search[...]
    rest = old if first else residue[...]
    image = images[...]
    norm = inner(rest, rest)
    alpha = norm / inner(old, image)
    new_solution[...] = alpha * old if first else solution[...] + alpha * old
    rest = rest - alpha * image
    new_residue[...] = rest
    norm_next = inner(rest, rest)
    new_search[...] = rest + (norm_next / norm) * old
    return norm_next


def step_kernel(
    images, solution, residue, search, grads, prior,
    new_solution, new_residue, new_search, payload, image,
):
    advance(False, images, solution, residue, search, new_solution, new_residue, new_search)
    fisher_rows(prior, grads, new_search, weights_of(grads, new_search[...]), image)
    for s in range(8):
        payload[s] = image[...]


def first_kernel(
    images, search, grads, prior, new_solution, new_residue, new_search, payload, image
):
    advance(True, images, None, None, search, new_solution, new_residue, new_search)
    fisher_rows(prior, grads, new_search, weights_of(grads, new_search[...]), image)
    for s in range(8):
        payload[s] = image[...]


def last_kernel(
    images, solution, residue, search, grads, prior,
    own, payload, values, new_solution, new_residue, new_search, image,
):
    me = lax.axis_index("tensor")
    norm = advance(False, images, solution, residue, search, new_solution, new_residue, new_search)
    weights = weights_of(grads, new_search[...])
    fisher_rows(prior, grads, new_search, weights, image)
    curve = pair_sums(new_search[me] * image[...])
    for s in range(8):
        payload[s] = jnp.broadcast_to(curve, (8, LANES))
    own[0] = new_solution[me]
    own[1] = new_search[me]
    own[2] = jnp.broadcast_to(norm, (8, LANES))
    values[0] = jnp.broadcast_to(weights_of(grads, new_solution[...]), values.shape[1:])
    values[1] = jnp.broadcast_to(weights, values.shape[1:])


def end_kernel(curves, own, values, scores, solution):
    alpha = own[2] / jnp.sum(curves[...], axis=0)
    done = own[0] + alpha * own[1]
    for j in range(2):
        for c in range(4):
            solution[pl.ds(j, 1), pl.ds(c * LANES, LANES)] = done[j * 4 + c : j * 4 + c + 1]
    total = values.shape[1]
    lane = lax.broadcasted_iota(jnp.int32, (8, LANES), 1)
    table = jnp.zeros((8, LANES), jnp.float32)
    for i in range(total):
        table = jnp.where(lane == i, (values[0, i] + alpha * values[1, i]) / RANK, table)
    for j in range(2):
        scores[pl.ds(j, 1), :] = table[j * 4 : j * 4 + 1, :total]


def call(kernel, shapes, operands, scratch=(), limit=16):
    return pl.pallas_call(
        kernel,
        out_shape=[jax.ShapeDtypeStruct(s, jnp.float32) for s in shapes],
        in_specs=[VMEM] * len(operands),
        out_specs=[VMEM] * len(shapes),
        scratch_shapes=[pltpu.VMEM(s, jnp.float32) for s in scratch],
        compiler_params=pltpu.CompilerParams(vmem_limit_bytes=limit * 2**20),
        name=kernel.__name__,
    )(*operands)


def flipped(n, bit):
    return [(i, i ^ bit) for i in range(n)]


def per_device(
    train_inputs,
    train_outgrads,
    test_inputs,
    test_outgrads,
    train_counts,
    test_counts,
    proj_in,
    proj_out,
    fisher_prior,
):
    n = 8
    me = lax.axis_index("tensor")
    near, far = (me >> 1) & 1, me >> 2
    length = train_inputs.shape[1]
    basis_out = jnp.concatenate([proj_out, jnp.zeros_like(proj_out)], 0).T
    basis_in = jnp.concatenate([jnp.zeros_like(proj_in), proj_in], 0).T
    operands = (
        train_counts, test_counts, train_inputs, train_outgrads, test_inputs, test_outgrads,
        basis_in, basis_out,
    )
    firsts = [sum(CHUNKS[:c]) for c in range(len(CHUNKS))]
    arrived = []
    for first, size in zip(firsts, CHUNKS):
        sent = project_rows(True, first, size, min(TILE, size), operands)
        arrived.append(lax.ppermute(sent, "tensor", flipped(n, 1)))
    kept = project_rows(False, 0, length, TILE, operands)
    whole = []
    for first, size, got in zip(firsts, CHUNKS, arrived):
        pair = (kept[:, first : first + size] + got).reshape(2, 2, size, LANES)
        ours = lax.dynamic_index_in_dim(pair, near, 1, False)
        theirs = lax.dynamic_index_in_dim(pair, 1 - near, 1, False)
        quad = ours + lax.ppermute(theirs, "tensor", flipped(n, 2))
        ours = lax.dynamic_index_in_dim(quad, far, 0, False)
        theirs = lax.dynamic_index_in_dim(quad, 1 - far, 0, False)
        whole.append(ours + lax.ppermute(theirs, "tensor", flipped(n, 4)))
    counts = jnp.concatenate([train_counts, test_counts])
    grad = gram(lax.dynamic_slice_in_dim(counts, me, 1), jnp.concatenate(whole), n)
    own = lax.all_to_all(grad, "tensor", 0, 0, tiled=True)
    per = train_inputs.shape[0]
    other = lax.ppermute(own[:per], "dp", flipped(2, 1))
    state = (8, 8, LANES)
    piece = (8, LANES)
    total = 2 * per
    grads, search, payload = call(
        begin_kernel, [(total, 8, 8, LANES), state, state], (own, other, fisher_prior), [piece]
    )
    swap = lambda x: lax.all_to_all(x, "tensor", 0, 0, tiled=True)
    solution, residue, search, payload = call(
        first_kernel, [state] * 4, (swap(payload), search, grads, fisher_prior), [piece]
    )
    for _ in range(ITERS - 3):
        solution, residue, search, payload = call(
            step_kernel,
            [state] * 4,
            (swap(payload), solution, residue, search, grads, fisher_prior),
            [piece],
        )
    ours, payload, values = call(
        last_kernel,
        [(3, 8, LANES), state, (2, total, 8, LANES)],
        (swap(payload), solution, residue, search, grads, fisher_prior),
        [state, state, state, piece],
    )
    return tuple(
        call(
            end_kernel,
            [(2, total), (2, fisher_prior.shape[0])],
            (swap(payload), ours, values),
        )
    )


def solution(mesh):
    in_specs = (
        P(("parts", "dp"), None, "tensor"),
        P(("parts", "dp"), None, "tensor"),
        P(("parts", "dp"), None, "tensor"),
        P(("parts", "dp"), None, "tensor"),
        P(("parts", "dp")),
        P(("parts", "dp")),
        P(None, "tensor"),
        P(None, "tensor"),
        P(("parts", "tensor"), None),
    )
    out_specs = (P(("parts", "dp"), None), P(("parts", "dp"), "tensor"))
    body = per_device if mesh.shape["tensor"] == 8 and mesh.shape["dp"] == 2 else plain
    return jax.shard_map(
        body, mesh=mesh, in_specs=in_specs, out_specs=out_specs, check_vma=False
    )
```

time: 636 us -> 207 us (0.33); the launches traced: 627 us -> 206 us
  blocking collectives: 313 us -> 66.8 us
  waiting for transfers between devices: 173 us -> 42.4 us
  matrix products: 113 us -> 0 us
  Pallas kernels: 0 us -> 53.3 us
  local copies, waits for them, and re-layouts: 10.5 us -> 25.3 us
  starting transfers between devices: 0.04 us -> 14.1 us
  between operations: 14.6 us -> 0.92 us
    all_gather x7 -> x0, blocking collectives: 185 us -> none  [the longest x6 183 us: per_device(): lax.all_gather(search, 'tensor', axis=1, tiled=True)]
    psum x1 -> x0, waiting for transfers between devices: 173 us -> none  [per_device(): lax.psum((left_train, right_train, left_test, right_test), 'tensor')]
    psum x7 -> x0, blocking collectives: 128 us -> none  [the longest x6 109 us: per_device(): lax.psum((jnp.sum(search * image, axis=1), jnp.sum(residue * image, axis=...]
    dot_general x14 -> x0, matrix products: 113 us -> none  [the longest x6 53.8 us: per_device(): lax.dot_general(lax.all_gather(search, 'tensor', axis=1, tiled=True), fis...]
    all_to_all x0 -> x7, blocking collectives: none -> 66.8 us  [the longest x6 54.4 us: per_device(): swap = lambda x: lax.all_to_all(x, 'tensor', 0, 0, tiled=True)]
    pallas_call x0 -> x13, Pallas kernels: none -> 53.3 us  [the longest x5 33 us: project_rows(): pl.pallas_call(functools.partial(project_kernel, flip, first, size, tile)...]
    ppermute x0 -> x13, waiting for transfers between devices: none -> 42.4 us  [the longest x4 21 us: per_device(): quad = ours + lax.ppermute(theirs, 'tensor', flipped(n, 2))]
    unnamed x22, local copies, waits for them, and re-layouts: 4.35 us -> 24.1 us
  transfers between devices with their start and end apart: 1 -> 13, of which waited for: 1 -> 8; matrix products, arithmetic and copies ran while one was open for 0% -> 0% of each run, Pallas kernels for 0% -> 13%
where the time goes in v1:
time: 207 us; the launch traced here: 206 us
  blocking collectives  66.8 us (32%)
  Pallas kernels  53.3 us (26%)
  waiting for transfers between devices  42.4 us (20%)
  local copies, waits for them, and re-layouts  25.3 us (12%)
  starting transfers between devices  14.1 us (7%)
  other arithmetic  2.87 us (1%)
    all_to_all x6, blocking collectives, per_device(): swap = lambda x: lax.all_to_all(x, 'tensor', 0, 0, tiled=True)  54.4 us
    pallas_call x5, Pallas kernels, project_rows(): pl.pallas_call(functools.partial(project_kernel, flip, first, size, tile)...  33 us
    unnamed x22, local copies, waits for them, and re-layouts  24.1 us
    ppermute x4, waiting for transfers between devices, per_device(): quad = ours + lax.ppermute(theirs, 'tensor', flipped(n, 2))  21 us
    pallas_call x7, Pallas kernels, call(): pl.pallas_call(kernel, out_shape=[jax.ShapeDtypeStruct(s, jnp.float32) fo...  17.3 us
    all_to_all x1, blocking collectives, per_device(): own = lax.all_to_all(grad, 'tensor', 0, 0, tiled=True)  12.4 us
    ppermute x4, waiting for transfers between devices, per_device(): whole.append(ours + lax.ppermute(theirs, 'tensor', flipped(n, 4)))  10.4 us
    ppermute x4, waiting for transfers between devices, per_device(): arrived.append(lax.ppermute(sent, 'tensor', flipped(n, 1)))  9.78 us
  transfers between devices with their start and end apart: 13, of which 8 were waited for; matrix products, arithmetic and copies ran while one was open for 0% of the time, Pallas kernels for 13%

profile of v1, /device:TPU:0, one launch (start us, length us, event | category | flops | bytes accessed | tf_op | source)
XLA Modules:
  0.0 205.7 jit_solution(4850872170639668626)
XLA Ops:
  3.6 4.6 %copy-done = bf16[6,1024,1024]{2,1,0:T(8,128)(2,1)S(1)} copy-done((bf16[6,1024,1024]{2,1,0:T(8,128)(2,1)S(1)}, bf16[6,1024,1024]{2,1,0:T(8,128)(2,1)}, u32[]{:S(2)}) %copy-start) | copy-done | bytes 12582936
  11.7 5.3 %project_send_0.1 = f32[4,256,128]{2,1,0:T(8,128)S(1)} custom-call(s32[6]{0:T(128)S(1)} %copy-done.8, s32[2]{0:T(128)S(1)} %copy-done.6, bf16[6,1024,3584]{2,1,0:T(8,128)(2,1)} %train_in.9, bf16[6,1024,1024]{2,1,0:T(8,128)(2,1)S(1)} %copy-done, bf16[2,1024,3584]{2,1,0:T(8,128)(2,1)} %test_in.9, bf16[2,1024,1024]{2,1,0:T(8,128)(2,1)S(1)} %copy-done.4, ...), custom_call_target="tpu_custom_call" | custom-call | flops 603979776 | bytes 9437184 | tf_op jit(solution)/shard_map/project_send_0/pallas_call | solution.py:156
  17.0 3.0 %collective-permute-start = (f32[4,256,128]{2,1,0:T(8,128)S(1)}, f32[4,256,128]{2,1,0:T(8,128)}, u32[]{:S(2)}, u32[]{:S(2)}) collective-permute-start(f32[4,256,128]{2,1,0:T(8,128)S(1)} %project_send_0.1), channel_id=1, source_target_pairs={{0,2},{2,0},{4,6},{6,4},{8,10},{10,8},{12,14},{14,12},{1,3},{3,1},... | collective-permute-start | bytes 1572872 | tf_op jit(solution)/shard_map/ppermute | solution.py:367
  20.0 5.3 %project_send_256.1 = f32[4,256,128]{2,1,0:T(8,128)S(1)} custom-call(s32[6]{0:T(128)S(1)} %copy-done.8, s32[2]{0:T(128)S(1)} %copy-done.6, bf16[6,1024,3584]{2,1,0:T(8,128)(2,1)} %train_in.9, bf16[6,1024,1024]{2,1,0:T(8,128)(2,1)S(1)} %copy-done, bf16[2,1024,3584]{2,1,0:T(8,128)(2,1)} %test_in.9, bf16[2,1024,1024]{2,1,0:T(8,128)(2,1)S(1)} %copy-done.4, ...), custom_call_target="tpu_custom_call" | custom-call | flops 603979776 | bytes 9437184 | tf_op jit(solution)/shard_map/project_send_256/pallas_call | solution.py:156
  25.4 4.5 %project_send_512.1 = f32[4,256,128]{2,1,0:T(8,128)S(1)} custom-call(s32[6]{0:T(128)S(1)} %copy-done.8, s32[2]{0:T(128)S(1)} %copy-done.6, bf16[6,1024,3584]{2,1,0:T(8,128)(2,1)} %train_in.9, bf16[6,1024,1024]{2,1,0:T(8,128)(2,1)S(1)} %copy-done, bf16[2,1024,3584]{2,1,0:T(8,128)(2,1)} %test_in.9, bf16[2,1024,1024]{2,1,0:T(8,128)(2,1)S(1)} %copy-done.4, ...), custom_call_target="tpu_custom_call" | custom-call | flops 603979776 | bytes 9437184 | tf_op jit(solution)/shard_map/project_send_512/pallas_call | solution.py:156
  30.5 4.5 %project_send_768.1 = f32[4,256,128]{2,1,0:T(8,128)S(1)} custom-call(s32[6]{0:T(128)S(1)} %copy-done.8, s32[2]{0:T(128)S(1)} %copy-done.6, bf16[6,1024,3584]{2,1,0:T(8,128)(2,1)} %train_in.9, bf16[6,1024,1024]{2,1,0:T(8,128)(2,1)S(1)} %copy-done, bf16[2,1024,3584]{2,1,0:T(8,128)(2,1)} %test_in.9, bf16[2,1024,1024]{2,1,0:T(8,128)(2,1)S(1)} %copy-done.4, ...), custom_call_target="tpu_custom_call" | custom-call | flops 603979776 | bytes 9437184 | tf_op jit(solution)/shard_map/project_send_768/pallas_call | solution.py:156
  35.8 4.6 %copy-done.1 = bf16[6,1024,1024]{2,1,0:T(8,128)(2,1)S(1)} copy-done((bf16[6,1024,1024]{2,1,0:T(8,128)(2,1)S(1)}, bf16[6,1024,1024]{2,1,0:T(8,128)(2,1)}, u32[]{:S(2)}) %copy-start.1) | copy-done | bytes 12582936
  42.6 13.4 %project_keep_0.1 = f32[4,1024,128]{2,1,0:T(8,128)S(1)} custom-call(s32[6]{0:T(128)S(1)} %copy-done.9, s32[2]{0:T(128)S(1)} %copy-done.7, bf16[6,1024,3584]{2,1,0:T(8,128)(2,1)} %train_in.9, bf16[6,1024,1024]{2,1,0:T(8,128)(2,1)S(1)} %copy-done.1, bf16[2,1024,3584]{2,1,0:T(8,128)(2,1)} %test_in.9, bf16[2,1024,1024]{2,1,0:T(8,128)(2,1)S(1)} %copy-done.5, ...), custom_call_target="tpu_custom_call" | custom-call | flops 2415919104 | bytes 37748736 | tf_op jit(solution)/shard_map/project_keep_0/pallas_call | solution.py:156
  56.0 9.8 %collective-permute-done.9 = f32[4,256,128]{2,1,0:T(8,128)} collective-permute-done((f32[4,256,128]{2,1,0:T(8,128)S(1)}, f32[4,256,128]{2,1,0:T(8,128)}, u32[]{:S(2)}, u32[]{:S(2)}) %collective-permute-start.9) | collective-permute-done | bytes 524320 | tf_op jit(solution)/shard_map/ppermute | solution.py:367
  71.9 4.9 %collective-permute-done.1 = f32[2,256,128]{2,1,0:T(8,128)S(1)} collective-permute-done((f32[2,256,128]{2,1,0:T(8,128)S(1)}, f32[2,256,128]{2,1,0:T(8,128)S(1)}, u32[]{:S(2)}, u32[]{:S(2)}) %collective-permute-start.1) | collective-permute-done | bytes 262176 | tf_op jit(solution)/shard_map/ppermute | solution.py:374
  79.8 6.9 %collective-permute-done.4 = f32[2,256,128]{2,1,0:T(8,128)S(1)} collective-permute-done((f32[2,256,128]{2,1,0:T(8,128)S(1)}, f32[2,256,128]{2,1,0:T(8,128)S(1)}, u32[]{:S(2)}, u32[]{:S(2)}) %collective-permute-start.4) | collective-permute-done | bytes 262176 | tf_op jit(solution)/shard_map/ppermute | solution.py:374
  88.7 5.1 %collective-permute-done.7 = f32[2,256,128]{2,1,0:T(8,128)S(1)} collective-permute-done((f32[2,256,128]{2,1,0:T(8,128)S(1)}, f32[2,256,128]{2,1,0:T(8,128)S(1)}, u32[]{:S(2)}, u32[]{:S(2)}) %collective-permute-start.7) | collective-permute-done | bytes 262176 | tf_op jit(solution)/shard_map/ppermute | solution.py:374
  94.8 4.0 %collective-permute-done.10 = f32[2,256,128]{2,1,0:T(8,128)S(1)} collective-permute-done((f32[2,256,128]{2,1,0:T(8,128)S(1)}, f32[2,256,128]{2,1,0:T(8,128)S(1)}, u32[]{:S(2)}, u32[]{:S(2)}) %collective-permute-start.10) | collective-permute-done | bytes 262176 | tf_op jit(solution)/shard_map/ppermute | solution.py:374
  99.1 8.9 %collective-permute-done.8 = f32[256,128]{1,0:T(8,128)S(1)} collective-permute-done((f32[256,128]{1,0:T(8,128)S(1)}, f32[256,128]{1,0:T(8,128)S(1)}, u32[]{:S(2)}, u32[]{:S(2)}) %collective-permute-start.8) | collective-permute-done | bytes 131104 | tf_op jit(solution)/shard_map/ppermute | solution.py:377
  110.4 3.0 %gram.1 = f32[8,32,128]{2,1,0:T(8,128)} custom-call(s32[1]{0:T(128)} %dynamic_slice.53.count, f32[1024,128]{1,0:T(8,128)} %pad_maximum_fusion.rows), custom_call_target="tpu_custom_call" | custom-call | tf_op jit(solution)/shard_map/gram/pallas_call | solution.py:190
  113.4 12.4 %all_to_all.35.own = f32[8,32,128]{2,1,0:T(8,128)S(1)} all-to-all(f32[8,32,128]{2,1,0:T(8,128)} %gram.1), channel_id=1, replica_groups=mesh['parts'=2,'tensor'=8,'dp'=2] {'tensor'}, dimensions={0} | all-to-all | bytes 262144 | tf_op jit(solution)/shard_map/all_to_all | solution.py:380
  127.2 3.4 %copy-done.2 = f32[512,4096]{1,0:T(8,128)S(1)} copy-done((f32[512,4096]{1,0:T(8,128)S(1)}, f32[512,4096]{1,0:T(8,128)}, u32[]{:S(2)}) %copy-start.2) | copy-done | bytes 8388632
  133.3 9.1 %all_to_all.36.images = f32[8,8,128]{2,1,0:T(8,128)S(1)} all-to-all(f32[8,8,128]{2,1,0:T(8,128)S(1)} %get-tuple-element.24), channel_id=1, replica_groups=mesh['parts'=2,'tensor'=8,'dp'=2] {'tensor'}, dimensions={0} | all-to-all | bytes 65536 | tf_op jit(solution)/shard_map/all_to_all | solution.py:389
  142.4 3.4 %copy-done.3 = f32[512,4096]{1,0:T(8,128)S(1)} copy-done((f32[512,4096]{1,0:T(8,128)S(1)}, f32[512,4096]{1,0:T(8,128)}, u32[]{:S(2)}) %copy-start.3) | copy-done | bytes 8388632
  148.5 9.1 %all_to_all.37.images = f32[8,8,128]{2,1,0:T(8,128)S(1)} all-to-all(f32[8,8,128]{2,1,0:T(8,128)S(1)} %get-tuple-element.27), channel_id=1, replica_groups=mesh['parts'=2,'tensor'=8,'dp'=2] {'tensor'}, dimensions={0} | all-to-all | bytes 65536 | tf_op jit(solution)/shard_map/all_to_all | solution.py:389
  160.3 9.1 %all_to_all.38.images = f32[8,8,128]{2,1,0:T(8,128)S(1)} all-to-all(f32[8,8,128]{2,1,0:T(8,128)S(1)} %get-tuple-element.31), channel_id=1, replica_groups=mesh['parts'=2,'tensor'=8,'dp'=2] {'tensor'}, dimensions={0} | all-to-all | bytes 65536 | tf_op jit(solution)/shard_map/all_to_all | solution.py:389
  172.2 9.1 %all_to_all.39.images = f32[8,8,128]{2,1,0:T(8,128)S(1)} all-to-all(f32[8,8,128]{2,1,0:T(8,128)S(1)} %get-tuple-element.35), channel_id=1, replica_groups=mesh['parts'=2,'tensor'=8,'dp'=2] {'tensor'}, dimensions={0} | all-to-all | bytes 65536 | tf_op jit(solution)/shard_map/all_to_all | solution.py:389
  184.0 9.1 %all_to_all.40.images = f32[8,8,128]{2,1,0:T(8,128)S(1)} all-to-all(f32[8,8,128]{2,1,0:T(8,128)S(1)} %get-tuple-element.39), channel_id=1, replica_groups=mesh['parts'=2,'tensor'=8,'dp'=2] {'tensor'}, dimensions={0} | all-to-all | bytes 65536 | tf_op jit(solution)/shard_map/all_to_all | solution.py:389
  196.0 9.1 %all_to_all.41.curves = f32[8,8,128]{2,1,0:T(8,128)S(1)} all-to-all(f32[8,8,128]{2,1,0:T(8,128)S(1)} %get-tuple-element.43), channel_id=1, replica_groups=mesh['parts'=2,'tensor'=8,'dp'=2] {'tensor'}, dimensions={0} | all-to-all | bytes 65536 | tf_op jit(solution)/shard_map/all_to_all | solution.py:389
  (67 shorter events, 43.4 us)
Async XLA Ops:
  3.6 4.6 %copy-start = (bf16[6,1024,1024]{2,1,0:T(8,128)(2,1)S(1)}, bf16[6,1024,1024]{2,1,0:T(8,128)(2,1)}, u32[]{:S(2)}) copy-start(bf16[6,1024,1024]{2,1,0:T(8,128)(2,1)} %train_out.9) | copy-start | bytes 37748740
  8.2 2.2 %copy-start.4 = (bf16[2,1024,1024]{2,1,0:T(8,128)(2,1)S(1)}, bf16[2,1024,1024]{2,1,0:T(8,128)(2,1)}, u32[]{:S(2)}) copy-start(bf16[2,1024,1024]{2,1,0:T(8,128)(2,1)} %test_out.9) | copy-start | bytes 12582916
  10.3 0.7 copy-start.6
  11.0 0.7 copy-start.8
  17.0 39.0 %collective-permute-start = (f32[4,256,128]{2,1,0:T(8,128)S(1)}, f32[4,256,128]{2,1,0:T(8,128)}, u32[]{:S(2)}, u32[]{:S(2)}) collective-permute-start(f32[4,256,128]{2,1,0:T(8,128)S(1)} %project_send_0.1), channel_id=1, source_target_pairs={{0,2},{2,0},{4,6},{6,4},{8,10},{10,8},{12,14},{14,12},{1,3},{3,1},... | collective-permute-start | bytes 1572872 | tf_op jit(solution)/shard_map/ppermute | solution.py:367
  25.3 30.6 %collective-permute-start.3 = (f32[4,256,128]{2,1,0:T(8,128)S(1)}, f32[4,256,128]{2,1,0:T(8,128)}, u32[]{:S(2)}, u32[]{:S(2)}) collective-permute-start(f32[4,256,128]{2,1,0:T(8,128)S(1)} %project_send_256.1), channel_id=1, source_target_pairs={{0,2},{2,0},{4,6},{6,4},{8,10},{10,8},{12,14},{14,12},{1,3},{3,1},... | collective-permute-start | bytes 1572872 | tf_op jit(solution)/shard_map/ppermute | solution.py:367
  29.9 5.2 %copy-start.7 = (s32[2]{0:T(128)S(1)}, s32[2]{0:T(128)}, u32[]{:S(2)}) copy-start(s32[2]{0:T(128)} %test_count.9) | copy-start | bytes 28
  29.9 5.2 %copy-start.9 = (s32[6]{0:T(128)S(1)}, s32[6]{0:T(128)}, u32[]{:S(2)}) copy-start(s32[6]{0:T(128)} %train_count.9) | copy-start | bytes 76
  29.9 26.0 %collective-permute-start.6 = (f32[4,256,128]{2,1,0:T(8,128)S(1)}, f32[4,256,128]{2,1,0:T(8,128)}, u32[]{:S(2)}, u32[]{:S(2)}) collective-permute-start(f32[4,256,128]{2,1,0:T(8,128)S(1)} %project_send_512.1), channel_id=1, source_target_pairs={{0,2},{2,0},{4,6},{6,4},{8,10},{10,8},{12,14},{14,12},{1,3},{3,1},... | collective-permute-start | bytes 1572872 | tf_op jit(solution)/shard_map/ppermute | solution.py:367
  35.0 30.7 %collective-permute-start.9 = (f32[4,256,128]{2,1,0:T(8,128)S(1)}, f32[4,256,128]{2,1,0:T(8,128)}, u32[]{:S(2)}, u32[]{:S(2)}) collective-permute-start(f32[4,256,128]{2,1,0:T(8,128)S(1)} %project_send_768.1), channel_id=1, source_target_pairs={{0,2},{2,0},{4,6},{6,4},{8,10},{10,8},{12,14},{14,12},{1,3},{3,1},... | collective-permute-start | bytes 1572872 | tf_op jit(solution)/shard_map/ppermute | solution.py:367
  35.8 4.6 %copy-start.1 = (bf16[6,1024,1024]{2,1,0:T(8,128)(2,1)S(1)}, bf16[6,1024,1024]{2,1,0:T(8,128)(2,1)}, u32[]{:S(2)}) copy-start(bf16[6,1024,1024]{2,1,0:T(8,128)(2,1)} %train_out.9) | copy-start | bytes 37748740
  40.4 2.2 %copy-start.5 = (bf16[2,1024,1024]{2,1,0:T(8,128)(2,1)S(1)}, bf16[2,1024,1024]{2,1,0:T(8,128)(2,1)}, u32[]{:S(2)}) copy-start(bf16[2,1024,1024]{2,1,0:T(8,128)(2,1)} %test_out.9) | copy-start | bytes 12582916
  67.5 9.3 %collective-permute-start.1 = (f32[2,256,128]{2,1,0:T(8,128)S(1)}, f32[2,256,128]{2,1,0:T(8,128)S(1)}, u32[]{:S(2)}, u32[]{:S(2)}) collective-permute-start(f32[2,256,128]{2,1,0:T(8,128)S(1)} %dynamic-slice_bitcast_fusion.3), channel_id=1, source_target_pairs={{0,4},{2,6},{4,0},{6,2},{8,12},{10,14},{12,8},{14,10},{1,5},{3,7},... | collective-permute-start | bytes 786440 | tf_op jit(solution)/shard_map/ppermute | solution.py:374
  69.4 17.3 %collective-permute-start.4 = (f32[2,256,128]{2,1,0:T(8,128)S(1)}, f32[2,256,128]{2,1,0:T(8,128)S(1)}, u32[]{:S(2)}, u32[]{:S(2)}) collective-permute-start(f32[2,256,128]{2,1,0:T(8,128)S(1)} %dynamic-slice_bitcast_fusion.2), channel_id=1, source_target_pairs={{0,4},{2,6},{4,0},{6,2},{8,12},{10,14},{12,8},{14,10},{1,5},{3,7},... | collective-permute-start | bytes 786440 | tf_op jit(solution)/shard_map/ppermute | solution.py:374
  69.7 24.1 %collective-permute-start.7 = (f32[2,256,128]{2,1,0:T(8,128)S(1)}, f32[2,256,128]{2,1,0:T(8,128)S(1)}, u32[]{:S(2)}, u32[]{:S(2)}) collective-permute-start(f32[2,256,128]{2,1,0:T(8,128)S(1)} %dynamic-slice_bitcast_fusion.1), channel_id=1, source_target_pairs={{0,4},{2,6},{4,0},{6,2},{8,12},{10,14},{12,8},{14,10},{1,5},{3,7},... | collective-permute-start | bytes 786440 | tf_op jit(solution)/shard_map/ppermute | solution.py:374
  71.6 27.2 %collective-permute-start.10 = (f32[2,256,128]{2,1,0:T(8,128)S(1)}, f32[2,256,128]{2,1,0:T(8,128)S(1)}, u32[]{:S(2)}, u32[]{:S(2)}) collective-permute-start(f32[2,256,128]{2,1,0:T(8,128)S(1)} %dynamic-slice_bitcast_fusion), channel_id=1, source_target_pairs={{0,4},{2,6},{4,0},{6,2},{8,12},{10,14},{12,8},{14,10},{1,5},{3,7},... | collective-permute-start | bytes 786440 | tf_op jit(solution)/shard_map/ppermute | solution.py:374
  76.9 22.2 %collective-permute-start.2 = (f32[256,128]{1,0:T(8,128)S(1)}, f32[256,128]{1,0:T(8,128)S(1)}, u32[]{:S(2)}, u32[]{:S(2)}) collective-permute-start(f32[256,128]{1,0:T(8,128)S(1)} %dynamic-slice_bitcast_fusion.7), channel_id=1, source_target_pairs={{0,8},{2,10},{4,12},{6,14},{8,0},{10,2},{12,4},{14,6},{1,9},{3,11}... | collective-permute-start | bytes 393224 | tf_op jit(solution)/shard_map/ppermute | solution.py:377
  86.7 12.4 %collective-permute-start.5 = (f32[256,128]{1,0:T(8,128)S(1)}, f32[256,128]{1,0:T(8,128)S(1)}, u32[]{:S(2)}, u32[]{:S(2)}) collective-permute-start(f32[256,128]{1,0:T(8,128)S(1)} %dynamic-slice_bitcast_fusion.6), channel_id=1, source_target_pairs={{0,8},{2,10},{4,12},{6,14},{8,0},{10,2},{12,4},{14,6},{1,9},{3,11}... | collective-permute-start | bytes 393224 | tf_op jit(solution)/shard_map/ppermute | solution.py:377
  93.9 14.2 %collective-permute-start.8 = (f32[256,128]{1,0:T(8,128)S(1)}, f32[256,128]{1,0:T(8,128)S(1)}, u32[]{:S(2)}, u32[]{:S(2)}) collective-permute-start(f32[256,128]{1,0:T(8,128)S(1)} %dynamic-slice_bitcast_fusion.5), channel_id=1, source_target_pairs={{0,8},{2,10},{4,12},{6,14},{8,0},{10,2},{12,4},{14,6},{1,9},{3,11}... | collective-permute-start | bytes 393224 | tf_op jit(solution)/shard_map/ppermute | solution.py:377
  98.9 10.6 %collective-permute-start.11 = (f32[256,128]{1,0:T(8,128)S(1)}, f32[256,128]{1,0:T(8,128)S(1)}, u32[]{:S(2)}, u32[]{:S(2)}) collective-permute-start(f32[256,128]{1,0:T(8,128)S(1)} %dynamic-slice_bitcast_fusion.4), channel_id=1, source_target_pairs={{0,8},{2,10},{4,12},{6,14},{8,0},{10,2},{12,4},{14,6},{1,9},{3,11}... | collective-permute-start | bytes 393224 | tf_op jit(solution)/shard_map/ppermute | solution.py:377
  125.8 1.4 collective-permute-start.12
  127.2 3.4 %copy-start.2 = (f32[512,4096]{1,0:T(8,128)S(1)}, f32[512,4096]{1,0:T(8,128)}, u32[]{:S(2)}) copy-start(f32[512,4096]{1,0:T(8,128)} %prior.11) | copy-start | bytes 25165828
  142.4 3.4 %copy-start.3 = (f32[512,4096]{1,0:T(8,128)S(1)}, f32[512,4096]{1,0:T(8,128)}, u32[]{:S(2)}) copy-start(f32[512,4096]{1,0:T(8,128)} %prior.11) | copy-start | bytes 25165828

commit v2 on v1

--- a/solution.py
+++ b/solution.py
@@ -11,9 +11,9 @@
 RANK = 64
 ITERS = 6
 LANES = 128
-CHUNKS = (256, 256, 256, 256)
-TILE = 256
+FLOOR = 256
 SLOTS = 3
+SMALL = 24 * 2**20
 
 HIGH = lax.Precision.HIGHEST
 VMEM = pl.BlockSpec(memory_space=pltpu.VMEM)
@@ -82,102 +82,212 @@
 
 
 def project_kernel(
-    flip, first, size, tile, train_count, test_count, train_in, train_out, test_in, test_out,
-    basis_in, basis_out, out, held_in, held_out, sems,
+    parts, after, train_count, test_count, train_in, train_out, test_in, test_out,
+    basis_in, basis_out, *rest,
 ):
-    low = lax.rem(lax.axis_index("tensor"), 2)
-    low = 1 - low if flip else low
-    each = size // tile
-    total = 4 * each
+    outs = rest[after : after + len(parts)]
+    held_in, held_out, near_in, near_out, of_train, of_test, sems, more = rest[after + len(parts) :]
+    me = lax.rem(lax.axis_index("tensor"), 2)
     last = train_in.shape[0] // 2
-
-    def place(k):
-        return k // each, first + lax.rem(k, each) * tile
-
-    def live(k):
-        i, row = place(k)
-        count = jnp.where(
-            i < last, train_count[jnp.minimum(2 * i + low, 2 * last - 1)], test_count[low]
-        )
-        return count > row
-
-    def copies(k, train):
-        i, row = place(k)
+    begins = [0]
+    for _, _, size, tile in parts:
+        begins.append(begins[-1] + 4 * (size // tile))
+    dynamic = [max(range(first, first + size, tile)) >= FLOOR for _, first, size, tile in parts]
+
+    def place(part, k):
+        flip, first, size, tile = parts[part]
+        each = size // tile
+        low = 1 - me if flip else me
+        step = k - begins[part]
+        return step // each, first + lax.rem(step, each) * tile, low
+
+    def live(part, k):
+        i, row, low = place(part, k)
+        train = of_train[jnp.minimum(2 * i + low, 2 * last - 1)]
+        return (jnp.where(i < last, train, of_test[low]) > row) | (k == 0)
+
+    def copies(part, k, train):
+        i, row, low = place(part, k)
+        tile = parts[part][3]
         slot = lax.rem(k, SLOTS)
-        rows = pl.ds(row, tile)
+        rows, there = pl.ds(row, tile), pl.ds(0, tile)
         wide, narrow, e = (train_in, train_out, 2 * i + low) if train else (test_in, test_out, low)
         return (
-            pltpu.make_async_copy(wide.at[e, rows], held_in.at[slot], sems.at[slot, 0]),
-            pltpu.make_async_copy(narrow.at[e, rows], held_out.at[slot], sems.at[slot, 1]),
+            pltpu.make_async_copy(wide.at[e, rows], held_in.at[slot, there], sems.at[slot, 0]),
+            pltpu.make_async_copy(narrow.at[e, rows], held_out.at[slot, there], sems.at[slot, 1]),
         )
 
-    def start(k):
-        i, _ = place(k)
-
-        @pl.when(live(k) & (i < last))
-        def _():
-            for copy in copies(k, True):
-                copy.start()
-
-        @pl.when(live(k) & (i == last))
-        def _():
-            for copy in copies(k, False):
-                copy.start()
-
-    for k in range(SLOTS - 1):
-        start(jnp.int32(k))
-
-    @pl.loop(0, total)
-    def _(k):
-        i, row = place(k)
-        slot = lax.rem(k, SLOTS)
-
-        @pl.when(k + SLOTS - 1 < total)
-        def _():
-            start(k + SLOTS - 1)
-
-        there = pl.ds(row - first, tile)
-
-        @pl.when(live(k))
-        def _():
-            for copy in copies(k, False):
-                copy.wait()
-            out[i, there, :] = jnp.dot(
-                held_out[slot], basis_out[...], preferred_element_type=jnp.float32
-            ) + jnp.dot(held_in[slot], basis_in[...], preferred_element_type=jnp.float32)
-
-        @pl.when(jnp.logical_not(live(k)))
-        def _():
-            out[i, there, :] = jnp.zeros((tile, LANES), jnp.float32)
-
-
-def project_rows(flip, first, size, tile, operands):
-    wide, narrow = operands[2], operands[3]
+    def start(k, among):
+        for part in among:
+            mine = (k >= begins[part]) & (k < begins[part + 1])
+            if dynamic[part]:
+                mine = mine & live(part, k)
+            i, _, _ = place(part, k)
+
+            @pl.when(mine & (i < last))
+            def _():
+                for copy in copies(part, k, True):
+                    copy.start()
+
+            @pl.when(mine & (i == last))
+            def _():
+                for copy in copies(part, k, False):
+                    copy.start()
+
+    bases = (
+        pltpu.make_async_copy(basis_in, near_in, more.at[0]),
+        pltpu.make_async_copy(basis_out, near_out, more.at[1]),
+    )
+    lengths = (
+        pltpu.make_async_copy(train_count, of_train, more.at[2]),
+        pltpu.make_async_copy(test_count, of_test, more.at[3]),
+    )
+    if any(dynamic):
+        for copy in lengths:
+            copy.start()
+    for copy in copies(0, jnp.int32(0), True):
+        copy.start()
+    for copy in bases:
+        copy.start()
+    if any(dynamic):
+        for copy in lengths:
+            copy.wait()
+    for k in range(1, SLOTS - 1):
+        start(jnp.int32(k), range(len(parts)))
+    for copy in bases:
+        copy.wait()
+
+    for part, (flip, first, size, tile) in enumerate(parts):
+
+        @pl.loop(begins[part], begins[part + 1])
+        def _(k):
+            i, row, _ = place(part, k)
+            slot = lax.rem(k, SLOTS)
+            start(k + SLOTS - 1, range(part, len(parts)))
+            there, whole = pl.ds(row - first, tile), pl.ds(0, tile)
+
+            def make():
+                for copy in copies(part, k, False):
+                    copy.wait()
+                dims = (((1,), (1,)), ((), ()))
+                left = lax.dot_general(
+                    held_out[slot, whole], near_out[...], dims, preferred_element_type=jnp.float32
+                )
+                right = lax.dot_general(
+                    held_in[slot, whole], near_in[...], dims, preferred_element_type=jnp.float32
+                )
+                outs[part][i, there, :] = jnp.concatenate([left, right], axis=1)
+
+            if dynamic[part]:
+                alive = live(part, k)
+                pl.when(alive)(make)
+
+                @pl.when(jnp.logical_not(alive))
+                def _():
+                    outs[part][i, there, :] = jnp.zeros((tile, LANES), jnp.float32)
+
+            else:
+                make()
+
+
+def in_hbm(arrays):
+    return [pltpu.with_memory_space_constraint(x, pltpu.HBM) for x in arrays]
+
+
+def project_rows(parts, operands, after=()):
+    wide, narrow, basis_in, basis_out = operands[2], operands[3], operands[6], operands[7]
+    tile = max(part[3] for part in parts)
+    rows = 4 * sum(part[2] for part in parts)
+    depth = wide.shape[2] + narrow.shape[2]
     return pl.pallas_call(
-        functools.partial(project_kernel, flip, first, size, tile),
-        out_shape=jax.ShapeDtypeStruct((4, size, LANES), jnp.float32),
-        in_specs=[SMEM, SMEM, ANY, ANY, ANY, ANY, VMEM, VMEM],
-        out_specs=VMEM,
+        functools.partial(project_kernel, parts, len(after)),
+        out_shape=[pltpu.VMEM((4, part[2], LANES), jnp.float32) for part in parts],
+        in_specs=[ANY] * (len(operands) + len(after)),
+        out_specs=[VMEM] * len(parts),
         scratch_shapes=[
             pltpu.VMEM((SLOTS, tile, wide.shape[2]), wide.dtype),
             pltpu.VMEM((SLOTS, tile, narrow.shape[2]), narrow.dtype),
+            pltpu.VMEM(basis_in.shape, basis_in.dtype),
+            pltpu.VMEM(basis_out.shape, basis_out.dtype),
+            pltpu.SMEM(operands[0].shape, jnp.int32),
+            pltpu.SMEM(operands[1].shape, jnp.int32),
             pltpu.SemaphoreType.DMA((SLOTS, 2)),
+            pltpu.SemaphoreType.DMA((4,)),
         ],
-        compiler_params=pltpu.CompilerParams(vmem_limit_bytes=24 * 2**20),
+        compiler_params=pltpu.CompilerParams(vmem_limit_bytes=SMALL),
         cost_estimate=pl.CostEstimate(
-            flops=2 * 4 * size * 4608 * 64, bytes_accessed=4 * size * 4608 * 2, transcendentals=0
+            flops=2 * rows * depth * RANK, bytes_accessed=rows * depth * 2, transcendentals=0
         ),
-        name=f"project_{'send' if flip else 'keep'}_{first}",
-    )(*operands)
-
-
-def gram_kernel(count, rows, out, held):
-    live = lax.broadcasted_iota(jnp.int32, rows.shape, 0) < count[0]
-    vectors = jnp.where(live, rows[...], 0.0)
-    held[...] = lax.dot_general(
-        vectors[:, :RANK], vectors[:, RANK:], (((0,), (0,)), ((), ())), precision=HIGH,
-        preferred_element_type=jnp.float32,
-    ) * (1.0 / math.sqrt(rows.shape[0]))
+        name="project_" + "_".join(f"{'send' if p[0] else 'keep'}{p[1]}" for p in parts),
+    )(*in_hbm(operands), *after)
+
+
+def halve_kernel(offset, bit, pieces, kept, *rest):
+    got, (theirs, ours) = rest[:pieces], rest[-2:]
+    mine = (lax.axis_index("tensor") >> bit) & 1
+    groups = theirs.shape[0]
+    at = 0
+    for piece in got:
+        rows = piece.shape[1]
+        here, there = pl.ds(offset + at, rows), pl.ds(at, rows)
+        for h in range(groups):
+            give = 2 * h + 1 - mine if bit == 1 else 1 - mine
+            take = 2 * h + mine if bit == 1 else mine
+            theirs[h, there, :] = kept[give, here, :] + piece[give, :, :]
+            ours[h, there, :] = kept[take, here, :] + piece[take, :, :]
+        at += rows
+
+
+def halve(offset, bit, kept, got, after=()):
+    rows = sum(piece.shape[1] for piece in got)
+    shape = pltpu.VMEM((kept.shape[0] // 2, rows, LANES), jnp.float32)
+    return pl.pallas_call(
+        functools.partial(halve_kernel, offset, bit, len(got)),
+        out_shape=[shape, shape],
+        in_specs=[VMEM] * (1 + len(got)) + [ANY] * len(after),
+        out_specs=[VMEM, VMEM],
+        compiler_params=pltpu.CompilerParams(vmem_limit_bytes=SMALL),
+        name=f"halve{bit}",
+    )(kept, *got, *after)
+
+
+def gram_kernel(first, pieces, length, final, train_count, test_count, *rest):
+    ours, got = rest[:pieces], rest[pieces : 2 * pieces]
+    rest = rest[2 * pieces :]
+    if final:
+        before, out, held, of_train, of_test, sems = rest
+    else:
+        prior, out, near, of_train, of_test, sems, more = rest
+        fetch = pltpu.make_async_copy(prior, near, more)
+        fetch.start()
+    me = lax.axis_index("tensor")
+    train = train_count.shape[0]
+    lengths = (
+        pltpu.make_async_copy(train_count, of_train, sems.at[0]),
+        pltpu.make_async_copy(test_count, of_test, sems.at[1]),
+    )
+    for copy in lengths:
+        copy.start()
+    for copy in lengths:
+        copy.wait()
+    count = jnp.where(
+        me < train, of_train[jnp.minimum(me, train - 1)], of_test[jnp.maximum(me - train, 0)]
+    )
+    total = before[...] if final else jnp.zeros((RANK, RANK), jnp.float32)
+    for a, b in zip(ours, got):
+        rows = a[0] + b[0]
+        live = lax.broadcasted_iota(jnp.int32, rows.shape, 0) + first < count
+        rows = jnp.where(live, rows, 0.0)
+        total = total + lax.dot_general(
+            rows[:, :RANK], rows[:, RANK:], (((0,), (0,)), ((), ())), precision=HIGH,
+            preferred_element_type=jnp.float32,
+        )
+        first += rows.shape[0]
+    if not final:
+        out[...] = total
+        fetch.wait()
+        return
+    held[...] = total * (1.0 / math.sqrt(length))
     half = RANK // 2
     grad = jnp.concatenate(
         [held[pl.ds(0, half, stride=2), :], held[pl.ds(1, half, stride=2), :]], axis=1
@@ -186,15 +296,26 @@
         out[i] = grad
 
 
-def gram(count, rows, n):
+def gram(first, length, counts, ours, got, prior=None, before=None):
+    final = before is not None
+    square = jax.ShapeDtypeStruct((RANK, RANK), jnp.float32)
+    scratch = [pltpu.SMEM(c.shape, jnp.int32) for c in counts] + [pltpu.SemaphoreType.DMA((2,))]
+    if final:
+        out_shape = jax.ShapeDtypeStruct((8, RANK // 2, LANES), jnp.float32)
+        scratch = [pltpu.VMEM((RANK, RANK), jnp.float32)] + scratch
+    else:
+        out_shape = [square, pltpu.VMEM(prior.shape, prior.dtype)]
+        counts, (prior,) = in_hbm(counts), in_hbm([prior])
+        scratch = scratch + [pltpu.SemaphoreType.DMA]
     return pl.pallas_call(
-        gram_kernel,
-        out_shape=jax.ShapeDtypeStruct((n, RANK // 2, LANES), jnp.float32),
-        in_specs=[SMEM, VMEM],
-        out_specs=VMEM,
-        scratch_shapes=[pltpu.VMEM((RANK, RANK), jnp.float32)],
-        name="gram",
-    )(count, rows)
+        functools.partial(gram_kernel, first, len(ours), length, final),
+        out_shape=out_shape,
+        in_specs=[ANY, ANY] + [VMEM] * (2 * len(ours)) + [VMEM if final else ANY],
+        out_specs=VMEM if final else [VMEM, VMEM],
+        scratch_shapes=scratch,
+        compiler_params=pltpu.CompilerParams(vmem_limit_bytes=SMALL),
+        name="gram_end" if final else "gram_begin",
+    )(*counts, *ours, *got, before if final else prior)
 
 
 def pair_sums(x):
@@ -323,7 +444,7 @@
         scores[pl.ds(j, 1), :] = table[j * 4 : j * 4 + 1, :total]
 
 
-def call(kernel, shapes, operands, scratch=(), limit=16):
+def call(kernel, shapes, operands, scratch=(), limit=24):
     return pl.pallas_call(
         kernel,
         out_shape=[jax.ShapeDtypeStruct(s, jnp.float32) for s in shapes],
@@ -351,32 +472,49 @@
     fisher_prior,
 ):
     n = 8
-    me = lax.axis_index("tensor")
-    near, far = (me >> 1) & 1, me >> 2
     length = train_inputs.shape[1]
-    basis_out = jnp.concatenate([proj_out, jnp.zeros_like(proj_out)], 0).T
-    basis_in = jnp.concatenate([jnp.zeros_like(proj_in), proj_in], 0).T
-    operands = (
-        train_counts, test_counts, train_inputs, train_outgrads, test_inputs, test_outgrads,
-        basis_in, basis_out,
-    )
-    firsts = [sum(CHUNKS[:c]) for c in range(len(CHUNKS))]
-    arrived = []
-    for first, size in zip(firsts, CHUNKS):
-        sent = project_rows(True, first, size, min(TILE, size), operands)
-        arrived.append(lax.ppermute(sent, "tensor", flipped(n, 1)))
-    kept = project_rows(False, 0, length, TILE, operands)
-    whole = []
-    for first, size, got in zip(firsts, CHUNKS, arrived):
-        pair = (kept[:, first : first + size] + got).reshape(2, 2, size, LANES)
-        ours = lax.dynamic_index_in_dim(pair, near, 1, False)
-        theirs = lax.dynamic_index_in_dim(pair, 1 - near, 1, False)
-        quad = ours + lax.ppermute(theirs, "tensor", flipped(n, 2))
-        ours = lax.dynamic_index_in_dim(quad, far, 0, False)
-        theirs = lax.dynamic_index_in_dim(quad, 1 - far, 0, False)
-        whole.append(ours + lax.ppermute(theirs, "tensor", flipped(n, 4)))
-    counts = jnp.concatenate([train_counts, test_counts])
-    grad = gram(lax.dynamic_slice_in_dim(counts, me, 1), jnp.concatenate(whole), n)
+    counts = (train_counts, test_counts)
+    operands = counts + (
+        train_inputs, train_outgrads, test_inputs, test_outgrads, proj_in, proj_out
+    )
+    near = lambda x: lax.ppermute(x, "tensor", flipped(n, 1))
+    next_to = lambda x: lax.ppermute(x, "tensor", flipped(n, 2))
+    beyond = lambda x: lax.ppermute(x, "tensor", flipped(n, 4))
+    (sent0,) = project_rows([(True, 0, 128, 128)], operands)
+    got0 = near(sent0)
+    (sent1,) = project_rows([(True, 128, 256, 256)], operands, (sent0,))
+    got1 = near(sent1)
+    (sent2,) = project_rows([(True, 384, 256, 256)], operands, (sent1,))
+    got2 = near(sent2)
+    kept01, sent3 = project_rows(
+        [(False, 0, 384, 384), (True, 640, 256, 256)], operands, (sent2, got0)
+    )
+    got3 = near(sent3)
+    theirs_a, ours_a = halve(0, 1, kept01, (got0, got1))
+    half_a = next_to(theirs_a)
+    kept2, sent4 = project_rows(
+        [(False, 384, 256, 256), (True, 896, 128, 128)], operands, (sent3, theirs_a)
+    )
+    got4 = near(sent4)
+    theirs_b, ours_b = halve(0, 1, kept2, (got2,))
+    half_b = next_to(theirs_b)
+    send_a, last_a = halve(0, 2, ours_a, (half_a,), (theirs_b,))
+    whole_a = beyond(send_a)
+    (kept34,) = project_rows([(False, 640, 384, 128)], operands, (sent4, theirs_b))
+    theirs_c, ours_c = halve(0, 1, kept34, (got3,), (send_a,))
+    half_c = next_to(theirs_c)
+    send_b, last_b = halve(0, 2, ours_b, (half_b,), (theirs_c,))
+    whole_b = beyond(send_b)
+    theirs_d, ours_d = halve(256, 1, kept34, (got4,), (send_b,))
+    half_d = next_to(theirs_d)
+    send_c, last_c = halve(0, 2, ours_c, (half_c,), (theirs_d,))
+    whole_c = beyond(send_c)
+    send_d, last_d = halve(0, 2, ours_d, (half_d,), (send_c,))
+    whole_d = beyond(send_d)
+    square, prior = gram(
+        0, length, counts, (last_a, last_b), (whole_a, whole_b), prior=fisher_prior
+    )
+    grad = gram(640, length, counts, (last_c, last_d), (whole_c, whole_d), before=square)
     own = lax.all_to_all(grad, "tensor", 0, 0, tiled=True)
     per = train_inputs.shape[0]
     other = lax.ppermute(own[:per], "dp", flipped(2, 1))
@@ -384,23 +522,23 @@
     piece = (8, LANES)
     total = 2 * per
     grads, search, payload = call(
-        begin_kernel, [(total, 8, 8, LANES), state, state], (own, other, fisher_prior), [piece]
+        begin_kernel, [(total, 8, 8, LANES), state, state], (own, other, prior), [piece]
     )
     swap = lambda x: lax.all_to_all(x, "tensor", 0, 0, tiled=True)
     solution, residue, search, payload = call(
-        first_kernel, [state] * 4, (swap(payload), search, grads, fisher_prior), [piece]
+        first_kernel, [state] * 4, (swap(payload), search, grads, prior), [piece]
     )
     for _ in range(ITERS - 3):
         solution, residue, search, payload = call(
             step_kernel,
             [state] * 4,
-            (swap(payload), solution, residue, search, grads, fisher_prior),
+            (swap(payload), solution, residue, search, grads, prior),
             [piece],
         )
     ours, payload, values = call(
         last_kernel,
         [(3, 8, LANES), state, (2, total, 8, LANES)],
-        (swap(payload), solution, residue, search, grads, fisher_prior),
+        (swap(payload), solution, residue, search, grads, prior),
         [state, state, state, piece],
     )
     return tuple(

time: 207 us -> 162 us (0.78)
  waiting for transfers between devices: 42.4 us -> 12.1 us
  local copies, waits for them, and re-layouts: 25.3 us -> 0.02 us
  starting transfers between devices: 14.1 us -> 21.6 us
  Pallas kernels: 53.3 us -> 60.7 us
  other arithmetic: 2.87 us -> 0 us
    ppermute x12 -> x13, waiting for transfers between devices: 41.1 us -> 10.9 us  [the longest x4 5.6 us: per_device(): next_to = lambda x: lax.ppermute(x, 'tensor', flipped(n, 2))]
    unnamed x22 -> x4, local copies, waits for them, and re-layouts: 24.1 us -> 0.01 us
    ppermute x12 -> x13, starting transfers between devices: 14.1 us -> 21.6 us  [the longest x4 9.85 us: per_device(): beyond = lambda x: lax.ppermute(x, 'tensor', flipped(n, 4))]
    pallas_call x6 -> x16, Pallas kernels: 36 us -> 43.4 us  [the longest x6 38.6 us: project_rows(): pl.pallas_call(functools.partial(project_kernel, parts, len(after)), out_...]
  transfers between devices with their start and end apart: 13 -> 14, of which waited for: 8 -> 6; matrix products, arithmetic and copies ran while one was open for 0% -> 0% of each run, Pallas kernels for 13% -> 24%
where the time goes in v2:
time: 162 us; the launch traced here: 161 us
  blocking collectives  65.6 us (40%)
  Pallas kernels  60.7 us (37%)
  starting transfers between devices  21.6 us (13%)
  waiting for transfers between devices  12.1 us (7%)
    all_to_all x6, blocking collectives, per_device(): swap = lambda x: lax.all_to_all(x, 'tensor', 0, 0, tiled=True)  54.4 us
    pallas_call x6, Pallas kernels, project_rows(): pl.pallas_call(functools.partial(project_kernel, parts, len(after)), out_...  38.6 us
    pallas_call x7, Pallas kernels, call(): pl.pallas_call(kernel, out_shape=[jax.ShapeDtypeStruct(s, jnp.float32) fo...  17.3 us
    all_to_all x1, blocking collectives, per_device(): own = lax.all_to_all(grad, 'tensor', 0, 0, tiled=True)  11.2 us
    ppermute x4, starting transfers between devices, per_device(): beyond = lambda x: lax.ppermute(x, 'tensor', flipped(n, 4))  9.85 us
    ppermute x4, starting transfers between devices, per_device(): next_to = lambda x: lax.ppermute(x, 'tensor', flipped(n, 2))  5.95 us
    ppermute x5, starting transfers between devices, per_device(): near = lambda x: lax.ppermute(x, 'tensor', flipped(n, 1))  5.76 us
    ppermute x4, waiting for transfers between devices, per_device(): next_to = lambda x: lax.ppermute(x, 'tensor', flipped(n, 2))  5.6 us
  transfers between devices with their start and end apart: 14, of which 6 were waited for; matrix products, arithmetic and copies ran while one was open for 0% of the time, Pallas kernels for 24%

profile of v2, /device:TPU:0, one launch (start us, length us, event | category | flops | bytes accessed | tf_op | source)
XLA Modules:
  0.0 160.9 jit_solution(7705632509750229055)
XLA Ops:
  0.6 3.9 %project_send0.1.rest_0_ = f32[4,128,128]{2,1,0:T(8,128)S(1)} custom-call(s32[6]{0:T(128)} %train_count.15, s32[2]{0:T(128)} %test_count.15, bf16[6,1024,3584]{2,1,0:T(8,128)(2,1)} %train_in.11, bf16[6,1024,1024]{2,1,0:T(8,128)(2,1)} %train_out.11, bf16[2,1024,3584]{2,1,0:T(8,128)(2,1)} %test_in.11, bf16[2,1024,1024]{2,1,0:T(8,128)(2,1)} %test_out.11, ...), custom_call_target="tpu_custom_call" | custom-call | flops 301989888 | bytes 4718592 | tf_op jit(solution)/shard_map/project_send0/pallas_call | solution.py:202
  4.5 3.0 %collective-permute-start = (f32[4,128,128]{2,1,0:T(8,128)S(1)}, f32[4,128,128]{2,1,0:T(8,128)S(1)}, u32[]{:S(2)}, u32[]{:S(2)}) collective-permute-start(f32[4,128,128]{2,1,0:T(8,128)S(1)} %project_send0.1.rest_0_), channel_id=1, source_target_pairs={{0,2},{2,0},{4,6},{6,4},{8,10},{10,8},{12,14},{14,12},{1,3},{3,1},... | collective-permute-start | bytes 786440 | tf_op jit(solution)/shard_map/ppermute | solution.py:480
  7.6 5.3 %project_send128.1.rest_0_ = f32[4,256,128]{2,1,0:T(8,128)S(1)} custom-call(s32[6]{0:T(128)} %train_count.15, s32[2]{0:T(128)} %test_count.15, bf16[6,1024,3584]{2,1,0:T(8,128)(2,1)} %train_in.11, bf16[6,1024,1024]{2,1,0:T(8,128)(2,1)} %train_out.11, bf16[2,1024,3584]{2,1,0:T(8,128)(2,1)} %test_in.11, bf16[2,1024,1024]{2,1,0:T(8,128)(2,1)} %test_out.11, ...), custom_call_target="tpu_custom_call" | custom-call | flops 603979776 | bytes 9437184 | tf_op jit(solution)/shard_map/project_send128/pallas_call | solution.py:202
  12.9 5.3 %project_send384.1.rest_0_ = f32[4,256,128]{2,1,0:T(8,128)S(1)} custom-call(s32[6]{0:T(128)} %train_count.15, s32[2]{0:T(128)} %test_count.15, bf16[6,1024,3584]{2,1,0:T(8,128)(2,1)} %train_in.11, bf16[6,1024,1024]{2,1,0:T(8,128)(2,1)} %train_out.11, bf16[2,1024,3584]{2,1,0:T(8,128)(2,1)} %test_in.11, bf16[2,1024,1024]{2,1,0:T(8,128)(2,1)} %test_out.11, ...), custom_call_target="tpu_custom_call" | custom-call | flops 603979776 | bytes 9437184 | tf_op jit(solution)/shard_map/project_send384/pallas_call | solution.py:202
  20.3 10.1 %project_keep0_send640.1 = (f32[4,384,128]{2,1,0:T(8,128)S(1)}, f32[4,256,128]{2,1,0:T(8,128)S(1)}) custom-call(s32[6]{0:T(128)} %train_count.15, s32[2]{0:T(128)} %test_count.15, bf16[6,1024,3584]{2,1,0:T(8,128)(2,1)} %train_in.11, bf16[6,1024,1024]{2,1,0:T(8,128)(2,1)} %train_out.11, bf16[2,1024,3584]{2,1,0:T(8,128)(2,1)} %test_in.11, ...), custom_call_target="tpu_custom_call" | custom-call | flops 1509949440 | bytes 23592960 | tf_op jit(solution)/shard_map/project_keep0_send640/pallas_call | solution.py:202
  32.3 7.1 %project_keep384_send896.1 = (f32[4,256,128]{2,1,0:T(8,128)S(1)}, f32[4,128,128]{2,1,0:T(8,128)S(1)}) custom-call(s32[6]{0:T(128)} %train_count.15, s32[2]{0:T(128)} %test_count.15, bf16[6,1024,3584]{2,1,0:T(8,128)(2,1)} %train_in.11, bf16[6,1024,1024]{2,1,0:T(8,128)(2,1)} %train_out.11, bf16[2,1024,3584]{2,1,0:T(8,128)(2,1)} %test_in.11, ...), custom_call_target="tpu_custom_call" | custom-call | flops 905969664 | bytes 14155776 | tf_op jit(solution)/shard_map/project_keep384_send896/pallas_call | solution.py:202
  41.2 6.8 %project_keep640.1.kept = f32[4,384,128]{2,1,0:T(8,128)S(1)} custom-call(s32[6]{0:T(128)} %train_count.15, s32[2]{0:T(128)} %test_count.15, bf16[6,1024,3584]{2,1,0:T(8,128)(2,1)} %train_in.11, bf16[6,1024,1024]{2,1,0:T(8,128)(2,1)} %train_out.11, bf16[2,1024,3584]{2,1,0:T(8,128)(2,1)} %test_in.11, bf16[2,1024,1024]{2,1,0:T(8,128)(2,1)} %test_out.11, ...), custom_call_target="tpu_custom_call" | custom-call | flops 905969664 | bytes 14155776 | tf_op jit(solution)/shard_map/project_keep640/pallas_call | solution.py:202
  58.7 4.7 %collective-permute-done.5.rest_0_ = f32[2,256,128]{2,1,0:T(8,128)S(1)} collective-permute-done((f32[2,256,128]{2,1,0:T(8,128)S(1)}, f32[2,256,128]{2,1,0:T(8,128)S(1)}, u32[]{:S(2)}, u32[]{:S(2)}) %collective-permute-start.5) | collective-permute-done | bytes 262176 | tf_op jit(solution)/shard_map/ppermute | solution.py:481
  65.5 3.5 %collective-permute-start.10 = (f32[1,128,128]{2,1,0:T(8,128)S(1)}, f32[1,128,128]{2,1,0:T(8,128)S(1)}, u32[]{:S(2)}, u32[]{:S(2)}) collective-permute-start(f32[1,128,128]{2,1,0:T(8,128)S(1)} %get-tuple-element.63), channel_id=1, source_target_pairs={{0,8},{2,10},{4,12},{6,14},{8,0},{10,2},{12,4},{14,6},{1,9},{3,11}... | collective-permute-start | bytes 196616 | tf_op jit(solution)/shard_map/ppermute | solution.py:482
  69.0 2.9 %collective-permute-done.12.rest_3_ = f32[1,256,128]{2,1,0:T(8,128)S(1)} collective-permute-done((f32[1,256,128]{2,1,0:T(8,128)S(1)}, f32[1,256,128]{2,1,0:T(8,128)S(1)}, u32[]{:S(2)}, u32[]{:S(2)}) %collective-permute-start.12) | collective-permute-done | bytes 131104 | tf_op jit(solution)/shard_map/ppermute | solution.py:482
  71.9 3.4 %gram_begin.1 = (f32[64,64]{1,0:T(8,128)S(1)}, f32[512,4096]{1,0:T(8,128)S(1)}) custom-call(s32[6]{0:T(128)} %train_count.15, s32[2]{0:T(128)} %test_count.15, f32[1,384,128]{2,1,0:T(8,128)S(1)} %get-tuple-element.64.rest_0_, f32[1,256,128]{2,1,0:T(8,128)S(1)} %get-tuple-element.65.rest_1_, f32[1,384,128]{2,1,0:T(8,128)S(1)} %collective-permute-done.11.rest_2_, ...), custom_call_target="tpu_custom_call" | custom-call | tf_op jit(solution)/shard_map/gram_begin/pallas_call | solution.py:310
  76.6 11.2 %all_to_all.35.own = f32[8,32,128]{2,1,0:T(8,128)S(1)} all-to-all(f32[8,32,128]{2,1,0:T(8,128)S(1)} %gram_end.1), channel_id=1, replica_groups=mesh['parts'=2,'tensor'=8,'dp'=2] {'tensor'}, dimensions={0} | all-to-all | bytes 262144 | tf_op jit(solution)/shard_map/all_to_all | solution.py:518
  89.2 2.7 %begin_kernel.1 = (f32[12,8,8,128]{3,2,1,0:T(8,128)S(1)}, f32[8,8,128]{2,1,0:T(8,128)S(1)}, f32[8,8,128]{2,1,0:T(8,128)S(1)}) custom-call(f32[8,32,128]{2,1,0:T(8,128)S(1)} %all_to_all.35.own, f32[6,32,128]{2,1,0:T(8,128)S(1)} %collective-permute-done.13.other, f32[512,4096]{1,0:T(8,128)S(1)} %get-tuple-element.67.prior), custom_call_target="tpu_custom_call" | custom-call | tf_op jit(solution)/shard_map/begin_kernel/pallas_call | solution.py:448
  91.9 9.1 %all_to_all.36.images = f32[8,8,128]{2,1,0:T(8,128)S(1)} all-to-all(f32[8,8,128]{2,1,0:T(8,128)S(1)} %get-tuple-element.68), channel_id=1, replica_groups=mesh['parts'=2,'tensor'=8,'dp'=2] {'tensor'}, dimensions={0} | all-to-all | bytes 65536 | tf_op jit(solution)/shard_map/all_to_all | solution.py:527
  100.9 2.8 %first_kernel.1 = (f32[8,8,128]{2,1,0:T(8,128)S(1)}, f32[8,8,128]{2,1,0:T(8,128)S(1)}, f32[8,8,128]{2,1,0:T(8,128)S(1)}, f32[8,8,128]{2,1,0:T(8,128)S(1)}) custom-call(f32[8,8,128]{2,1,0:T(8,128)S(1)} %all_to_all.36.images, f32[8,8,128]{2,1,0:T(8,128)S(1)} %get-tuple-element.69.search, f32[12,8,8,128]{3,2,1,0:T(8,128)S(1)} %get-tuple-element.70.grads, ...), custom_call_target="tpu_custom_call" | custom-call | tf_op jit(solution)/shard_map/first_kernel/pallas_call | solution.py:448
  103.7 9.1 %all_to_all.37.images = f32[8,8,128]{2,1,0:T(8,128)S(1)} all-to-all(f32[8,8,128]{2,1,0:T(8,128)S(1)} %get-tuple-element.71), channel_id=1, replica_groups=mesh['parts'=2,'tensor'=8,'dp'=2] {'tensor'}, dimensions={0} | all-to-all | bytes 65536 | tf_op jit(solution)/shard_map/all_to_all | solution.py:527
  112.8 2.8 %step_kernel.3 = (f32[8,8,128]{2,1,0:T(8,128)S(1)}, f32[8,8,128]{2,1,0:T(8,128)S(1)}, f32[8,8,128]{2,1,0:T(8,128)S(1)}, f32[8,8,128]{2,1,0:T(8,128)S(1)}) custom-call(f32[8,8,128]{2,1,0:T(8,128)S(1)} %all_to_all.37.images, f32[8,8,128]{2,1,0:T(8,128)S(1)} %get-tuple-element.72.solution, f32[8,8,128]{2,1,0:T(8,128)S(1)} %get-tuple-element.73.residue, ...), custom_call_target="tpu_custom_call" | custom-call | tf_op jit(solution)/shard_map/step_kernel/pallas_call | solution.py:448
  115.6 9.1 %all_to_all.38.images = f32[8,8,128]{2,1,0:T(8,128)S(1)} all-to-all(f32[8,8,128]{2,1,0:T(8,128)S(1)} %get-tuple-element.75), channel_id=1, replica_groups=mesh['parts'=2,'tensor'=8,'dp'=2] {'tensor'}, dimensions={0} | all-to-all | bytes 65536 | tf_op jit(solution)/shard_map/all_to_all | solution.py:527
  124.6 2.8 %step_kernel.4 = (f32[8,8,128]{2,1,0:T(8,128)S(1)}, f32[8,8,128]{2,1,0:T(8,128)S(1)}, f32[8,8,128]{2,1,0:T(8,128)S(1)}, f32[8,8,128]{2,1,0:T(8,128)S(1)}) custom-call(f32[8,8,128]{2,1,0:T(8,128)S(1)} %all_to_all.38.images, f32[8,8,128]{2,1,0:T(8,128)S(1)} %get-tuple-element.76.solution, f32[8,8,128]{2,1,0:T(8,128)S(1)} %get-tuple-element.77.residue, ...), custom_call_target="tpu_custom_call" | custom-call | tf_op jit(solution)/shard_map/step_kernel/pallas_call | solution.py:448
  127.4 9.1 %all_to_all.39.images = f32[8,8,128]{2,1,0:T(8,128)S(1)} all-to-all(f32[8,8,128]{2,1,0:T(8,128)S(1)} %get-tuple-element.79), channel_id=1, replica_groups=mesh['parts'=2,'tensor'=8,'dp'=2] {'tensor'}, dimensions={0} | all-to-all | bytes 65536 | tf_op jit(solution)/shard_map/all_to_all | solution.py:527
  136.5 2.8 %step_kernel.5 = (f32[8,8,128]{2,1,0:T(8,128)S(1)}, f32[8,8,128]{2,1,0:T(8,128)S(1)}, f32[8,8,128]{2,1,0:T(8,128)S(1)}, f32[8,8,128]{2,1,0:T(8,128)S(1)}) custom-call(f32[8,8,128]{2,1,0:T(8,128)S(1)} %all_to_all.39.images, f32[8,8,128]{2,1,0:T(8,128)S(1)} %get-tuple-element.80.solution, f32[8,8,128]{2,1,0:T(8,128)S(1)} %get-tuple-element.81.residue, ...), custom_call_target="tpu_custom_call" | custom-call | tf_op jit(solution)/shard_map/step_kernel/pallas_call | solution.py:448
  139.2 9.1 %all_to_all.40.images = f32[8,8,128]{2,1,0:T(8,128)S(1)} all-to-all(f32[8,8,128]{2,1,0:T(8,128)S(1)} %get-tuple-element.83), channel_id=1, replica_groups=mesh['parts'=2,'tensor'=8,'dp'=2] {'tensor'}, dimensions={0} | all-to-all | bytes 65536 | tf_op jit(solution)/shard_map/all_to_all | solution.py:527
  148.3 2.9 %last_kernel.1 = (f32[3,8,128]{2,1,0:T(8,128)S(1)}, f32[8,8,128]{2,1,0:T(8,128)S(1)}, f32[2,12,8,128]{3,2,1,0:T(8,128)S(1)}) custom-call(f32[8,8,128]{2,1,0:T(8,128)S(1)} %all_to_all.40.images, f32[8,8,128]{2,1,0:T(8,128)S(1)} %get-tuple-element.84.solution, f32[8,8,128]{2,1,0:T(8,128)S(1)} %get-tuple-element.85.residue, ...), custom_call_target="tpu_custom_call" | custom-call | tf_op jit(solution)/shard_map/last_kernel/pallas_call | solution.py:448
  151.2 9.1 %all_to_all.41.curves = f32[8,8,128]{2,1,0:T(8,128)S(1)} all-to-all(f32[8,8,128]{2,1,0:T(8,128)S(1)} %get-tuple-element.87), channel_id=1, replica_groups=mesh['parts'=2,'tensor'=8,'dp'=2] {'tensor'}, dimensions={0} | all-to-all | bytes 65536 | tf_op jit(solution)/shard_map/all_to_all | solution.py:527
  (39 shorter events, 21.7 us)
Async XLA Ops:
  4.5 15.8 %collective-permute-start = (f32[4,128,128]{2,1,0:T(8,128)S(1)}, f32[4,128,128]{2,1,0:T(8,128)S(1)}, u32[]{:S(2)}, u32[]{:S(2)}) collective-permute-start(f32[4,128,128]{2,1,0:T(8,128)S(1)} %project_send0.1.rest_0_), channel_id=1, source_target_pairs={{0,2},{2,0},{4,6},{6,4},{8,10},{10,8},{12,14},{14,12},{1,3},{3,1},... | collective-permute-start | bytes 786440 | tf_op jit(solution)/shard_map/ppermute | solution.py:480
  12.9 17.7 %collective-permute-start.1 = (f32[4,256,128]{2,1,0:T(8,128)S(1)}, f32[4,256,128]{2,1,0:T(8,128)S(1)}, u32[]{:S(2)}, u32[]{:S(2)}) collective-permute-start(f32[4,256,128]{2,1,0:T(8,128)S(1)} %project_send128.1.rest_0_), channel_id=1, source_target_pairs={{0,2},{2,0},{4,6},{6,4},{8,10},{10,8},{12,14},{14,12},{1,3},{3,1},... | collective-permute-start | bytes 1572872 | tf_op jit(solution)/shard_map/ppermute | solution.py:480
  18.3 21.2 %collective-permute-start.2 = (f32[4,256,128]{2,1,0:T(8,128)S(1)}, f32[4,256,128]{2,1,0:T(8,128)S(1)}, u32[]{:S(2)}, u32[]{:S(2)}) collective-permute-start(f32[4,256,128]{2,1,0:T(8,128)S(1)} %project_send384.1.rest_0_), channel_id=1, source_target_pairs={{0,2},{2,0},{4,6},{6,4},{8,10},{10,8},{12,14},{14,12},{1,3},{3,1},... | collective-permute-start | bytes 1572872 | tf_op jit(solution)/shard_map/ppermute | solution.py:480
  30.5 19.8 %collective-permute-start.3 = (f32[4,256,128]{2,1,0:T(8,128)S(1)}, f32[4,256,128]{2,1,0:T(8,128)S(1)}, u32[]{:S(2)}, u32[]{:S(2)}) collective-permute-start(f32[4,256,128]{2,1,0:T(8,128)S(1)} %get-tuple-element.46.rest_0_), channel_id=1, source_target_pairs={{0,2},{2,0},{4,6},{6,4},{8,10},{10,8},{12,14},{14,12},{1,3},{3,1},... | collective-permute-start | bytes 1572872 | tf_op jit(solution)/shard_map/ppermute | solution.py:480
  30.7 17.4 %collective-permute-start.4 = (f32[2,384,128]{2,1,0:T(8,128)S(1)}, f32[2,384,128]{2,1,0:T(8,128)S(1)}, u32[]{:S(2)}, u32[]{:S(2)}) collective-permute-start(f32[2,384,128]{2,1,0:T(8,128)S(1)} %get-tuple-element.48.rest_1_), channel_id=1, source_target_pairs={{0,4},{2,6},{4,0},{6,2},{8,12},{10,14},{12,8},{14,10},{1,5},{3,7},... | collective-permute-start | bytes 1179656 | tf_op jit(solution)/shard_map/ppermute | solution.py:481
  39.5 15.0 %collective-permute-start.7 = (f32[2,256,128]{2,1,0:T(8,128)S(1)}, f32[2,256,128]{2,1,0:T(8,128)S(1)}, u32[]{:S(2)}, u32[]{:S(2)}) collective-permute-start(f32[2,256,128]{2,1,0:T(8,128)S(1)} %get-tuple-element.51.rest_1_), channel_id=1, source_target_pairs={{0,4},{2,6},{4,0},{6,2},{8,12},{10,14},{12,8},{14,10},{1,5},{3,7},... | collective-permute-start | bytes 786440 | tf_op jit(solution)/shard_map/ppermute | solution.py:481
  40.7 13.9 %collective-permute-start.6 = (f32[4,128,128]{2,1,0:T(8,128)S(1)}, f32[4,128,128]{2,1,0:T(8,128)S(1)}, u32[]{:S(2)}, u32[]{:S(2)}) collective-permute-start(f32[4,128,128]{2,1,0:T(8,128)S(1)} %get-tuple-element.49.rest_0_), channel_id=1, source_target_pairs={{0,2},{2,0},{4,6},{6,4},{8,10},{10,8},{12,14},{14,12},{1,3},{3,1},... | collective-permute-start | bytes 786440 | tf_op jit(solution)/shard_map/ppermute | solution.py:480
  48.1 27.5 %copy-start = (s32[6]{0:T(128)S(1)}, s32[6]{0:T(128)}, u32[]{:S(2)}) copy-start(s32[6]{0:T(128)} %train_count.15) | copy-start | bytes 76
  48.1 27.5 %copy-start.1 = (s32[2]{0:T(128)S(1)}, s32[2]{0:T(128)}, u32[]{:S(2)}) copy-start(s32[2]{0:T(128)} %test_count.15) | copy-start | bytes 28
  50.3 13.1 %collective-permute-start.5 = (f32[2,256,128]{2,1,0:T(8,128)S(1)}, f32[2,256,128]{2,1,0:T(8,128)S(1)}, u32[]{:S(2)}, u32[]{:S(2)}) collective-permute-start(f32[2,256,128]{2,1,0:T(8,128)S(1)} %get-tuple-element.55.rest_1_), channel_id=1, source_target_pairs={{0,4},{2,6},{4,0},{6,2},{8,12},{10,14},{12,8},{14,10},{1,5},{3,7},... | collective-permute-start | bytes 786440 | tf_op jit(solution)/shard_map/ppermute | solution.py:481
  52.0 20.0 %collective-permute-start.11 = (f32[1,384,128]{2,1,0:T(8,128)S(1)}, f32[1,384,128]{2,1,0:T(8,128)S(1)}, u32[]{:S(2)}, u32[]{:S(2)}) collective-permute-start(f32[1,384,128]{2,1,0:T(8,128)S(1)} %get-tuple-element.53.rest_1_), channel_id=1, source_target_pairs={{0,8},{2,10},{4,12},{6,14},{8,0},{10,2},{12,4},{14,6},{1,9},{3,11}... | collective-permute-start | bytes 589832 | tf_op jit(solution)/shard_map/ppermute | solution.py:482
  54.6 10.9 %collective-permute-start.8 = (f32[2,128,128]{2,1,0:T(8,128)S(1)}, f32[2,128,128]{2,1,0:T(8,128)S(1)}, u32[]{:S(2)}, u32[]{:S(2)}) collective-permute-start(f32[2,128,128]{2,1,0:T(8,128)S(1)} %get-tuple-element.58.rest_1_), channel_id=1, source_target_pairs={{0,4},{2,6},{4,0},{6,2},{8,12},{10,14},{12,8},{14,10},{1,5},{3,7},... | collective-permute-start | bytes 393224 | tf_op jit(solution)/shard_map/ppermute | solution.py:481
  56.1 15.9 %collective-permute-start.12 = (f32[1,256,128]{2,1,0:T(8,128)S(1)}, f32[1,256,128]{2,1,0:T(8,128)S(1)}, u32[]{:S(2)}, u32[]{:S(2)}) collective-permute-start(f32[1,256,128]{2,1,0:T(8,128)S(1)} %get-tuple-element.57.rest_1_), channel_id=1, source_target_pairs={{0,8},{2,10},{4,12},{6,14},{8,0},{10,2},{12,4},{14,6},{1,9},{3,11}... | collective-permute-start | bytes 393224 | tf_op jit(solution)/shard_map/ppermute | solution.py:482
  63.4 12.2 %collective-permute-start.9 = (f32[1,256,128]{2,1,0:T(8,128)S(1)}, f32[1,256,128]{2,1,0:T(8,128)S(1)}, u32[]{:S(2)}, u32[]{:S(2)}) collective-permute-start(f32[1,256,128]{2,1,0:T(8,128)S(1)} %get-tuple-element.61.rest_1_), channel_id=1, source_target_pairs={{0,8},{2,10},{4,12},{6,14},{8,0},{10,2},{12,4},{14,6},{1,9},{3,11}... | collective-permute-start | bytes 393224 | tf_op jit(solution)/shard_map/ppermute | solution.py:482
  65.5 10.1 %collective-permute-start.10 = (f32[1,128,128]{2,1,0:T(8,128)S(1)}, f32[1,128,128]{2,1,0:T(8,128)S(1)}, u32[]{:S(2)}, u32[]{:S(2)}) collective-permute-start(f32[1,128,128]{2,1,0:T(8,128)S(1)} %get-tuple-element.63), channel_id=1, source_target_pairs={{0,8},{2,10},{4,12},{6,14},{8,0},{10,2},{12,4},{14,6},{1,9},{3,11}... | collective-permute-start | bytes 196616 | tf_op jit(solution)/shard_map/ppermute | solution.py:482
  87.8 1.4 collective-permute-start.13

commit v3 on v2

--- a/solution.py
+++ b/solution.py
@@ -12,7 +12,7 @@
 ITERS = 6
 LANES = 128
 FLOOR = 256
-SLOTS = 3
+SLOTS = 4
 SMALL = 24 * 2**20
 
 HIGH = lax.Precision.HIGHEST
@@ -82,112 +82,123 @@
 
 
 def project_kernel(
-    parts, after, train_count, test_count, train_in, train_out, test_in, test_out,
+    parts, tile, after, train_count, test_count, train_in, train_out, test_in, test_out,
     basis_in, basis_out, *rest,
 ):
-    outs = rest[after : after + len(parts)]
-    held_in, held_out, near_in, near_out, of_train, of_test, sems, more = rest[after + len(parts) :]
+    outs = rest[after : after + sum(len(part[2]) for part in parts)]
+    held_in, held_out, near_in, near_out, of_train, of_test, sems, more = rest[after + len(outs) :]
     me = lax.rem(lax.axis_index("tensor"), 2)
     last = train_in.shape[0] // 2
-    begins = [0]
-    for _, _, size, tile in parts:
-        begins.append(begins[-1] + 4 * (size // tile))
-    dynamic = [max(range(first, first + size, tile)) >= FLOOR for _, first, size, tile in parts]
-
-    def place(part, k):
-        flip, first, size, tile = parts[part]
-        each = size // tile
-        low = 1 - me if flip else me
-        step = k - begins[part]
-        return step // each, first + lax.rem(step, each) * tile, low
-
-    def live(part, k):
-        i, row, low = place(part, k)
+    total = 4 * len(parts)
+    dynamic = any(first >= FLOOR for _, first, _ in parts)
+
+    def pick(part, values):
+        value = jnp.int32(values[0])
+        for g in range(1, len(values)):
+            value = jnp.where(part == g, values[g], value)
+        return value
+
+    def place(k):
+        part = k // 4
+        low = pick(part, [int(p[0]) for p in parts]) ^ me
+        return lax.rem(k, 4), pl.multiple_of(pick(part, [p[1] for p in parts]), LANES), low
+
+    def live(k):
+        if not dynamic:
+            return jnp.bool_(True)
+        i, row, low = place(k)
         train = of_train[jnp.minimum(2 * i + low, 2 * last - 1)]
         return (jnp.where(i < last, train, of_test[low]) > row) | (k == 0)
 
-    def copies(part, k, train):
-        i, row, low = place(part, k)
-        tile = parts[part][3]
+    def copies(k, train):
+        i, row, low = place(k)
         slot = lax.rem(k, SLOTS)
-        rows, there = pl.ds(row, tile), pl.ds(0, tile)
+        rows = pl.ds(row, tile)
         wide, narrow, e = (train_in, train_out, 2 * i + low) if train else (test_in, test_out, low)
         return (
-            pltpu.make_async_copy(wide.at[e, rows], held_in.at[slot, there], sems.at[slot, 0]),
-            pltpu.make_async_copy(narrow.at[e, rows], held_out.at[slot, there], sems.at[slot, 1]),
+            pltpu.make_async_copy(wide.at[e, rows], held_in.at[slot], sems.at[slot, 0]),
+            pltpu.make_async_copy(narrow.at[e, rows], held_out.at[slot], sems.at[slot, 1]),
         )
 
-    def start(k, among):
-        for part in among:
-            mine = (k >= begins[part]) & (k < begins[part + 1])
-            if dynamic[part]:
-                mine = mine & live(part, k)
-            i, _, _ = place(part, k)
-
-            @pl.when(mine & (i < last))
-            def _():
-                for copy in copies(part, k, True):
-                    copy.start()
-
-            @pl.when(mine & (i == last))
-            def _():
-                for copy in copies(part, k, False):
-                    copy.start()
+    def start(k):
+        mine = (k < total) & live(k)
+        i = lax.rem(k, 4)
+
+        @pl.when(mine & (i < last))
+        def _():
+            for copy in copies(k, True):
+                copy.start()
+
+        @pl.when(mine & (i == last))
+        def _():
+            for copy in copies(k, False):
+                copy.start()
 
     bases = (
         pltpu.make_async_copy(basis_in, near_in, more.at[0]),
         pltpu.make_async_copy(basis_out, near_out, more.at[1]),
     )
-    lengths = (
-        pltpu.make_async_copy(train_count, of_train, more.at[2]),
-        pltpu.make_async_copy(test_count, of_test, more.at[3]),
-    )
-    if any(dynamic):
+    if dynamic:
+        lengths = (
+            pltpu.make_async_copy(train_count, of_train, more.at[2]),
+            pltpu.make_async_copy(test_count, of_test, more.at[3]),
+        )
         for copy in lengths:
             copy.start()
-    for copy in copies(0, jnp.int32(0), True):
+    for copy in copies(jnp.int32(0), True) + bases:
         copy.start()
-    for copy in bases:
-        copy.start()
-    if any(dynamic):
+    if dynamic:
         for copy in lengths:
             copy.wait()
-    for k in range(1, SLOTS - 1):
-        start(jnp.int32(k), range(len(parts)))
+
+    @pl.loop(1, SLOTS - 1)
+    def _(k):
+        start(k)
+
     for copy in bases:
         copy.wait()
 
-    for part, (flip, first, size, tile) in enumerate(parts):
-
-        @pl.loop(begins[part], begins[part + 1])
-        def _(k):
-            i, row, _ = place(part, k)
-            slot = lax.rem(k, SLOTS)
-            start(k + SLOTS - 1, range(part, len(parts)))
-            there, whole = pl.ds(row - first, tile), pl.ds(0, tile)
-
-            def make():
-                for copy in copies(part, k, False):
-                    copy.wait()
-                dims = (((1,), (1,)), ((), ()))
-                left = lax.dot_general(
-                    held_out[slot, whole], near_out[...], dims, preferred_element_type=jnp.float32
-                )
-                right = lax.dot_general(
-                    held_in[slot, whole], near_in[...], dims, preferred_element_type=jnp.float32
-                )
-                outs[part][i, there, :] = jnp.concatenate([left, right], axis=1)
-
-            if dynamic[part]:
-                alive = live(part, k)
-                pl.when(alive)(make)
-
-                @pl.when(jnp.logical_not(alive))
+    @pl.loop(0, total)
+    def _(k):
+        i, _, _ = place(k)
+        slot = lax.rem(k, SLOTS)
+        start(k + SLOTS - 1)
+
+        def keep(rows):
+            at = 0
+            for g, (_, _, pieces) in enumerate(parts):
+
+                @pl.when(k // 4 == g)
                 def _():
-                    outs[part][i, there, :] = jnp.zeros((tile, LANES), jnp.float32)
-
-            else:
-                make()
+                    done = 0
+                    for n, size in enumerate(pieces):
+                        outs[at + n][i] = rows[done : done + size]
+                        done += size
+
+                at += len(pieces)
+
+        def make():
+            for copy in copies(k, False):
+                copy.wait()
+            dims = (((1,), (1,)), ((), ()))
+            left = lax.dot_general(
+                held_out[slot], near_out[...], dims, preferred_element_type=jnp.float32
+            )
+            right = lax.dot_general(
+                held_in[slot], near_in[...], dims, preferred_element_type=jnp.float32
+            )
+            keep(jnp.concatenate([left, right], axis=1))
+
+        if dynamic:
+            alive = live(k)
+            pl.when(alive)(make)
+
+            @pl.when(jnp.logical_not(alive))
+            def _():
+                keep(jnp.zeros((tile, LANES), jnp.float32))
+
+        else:
+            make()
 
 
 def in_hbm(arrays):
@@ -196,14 +207,15 @@
 
 def project_rows(parts, operands, after=()):
     wide, narrow, basis_in, basis_out = operands[2], operands[3], operands[6], operands[7]
-    tile = max(part[3] for part in parts)
-    rows = 4 * sum(part[2] for part in parts)
+    tile = sum(parts[0][2])
+    sizes = [size for part in parts for size in part[2]]
+    rows = 4 * sum(sizes)
     depth = wide.shape[2] + narrow.shape[2]
     return pl.pallas_call(
-        functools.partial(project_kernel, parts, len(after)),
-        out_shape=[pltpu.VMEM((4, part[2], LANES), jnp.float32) for part in parts],
+        functools.partial(project_kernel, parts, tile, len(after)),
+        out_shape=[pltpu.VMEM((4, size, LANES), jnp.float32) for size in sizes],
         in_specs=[ANY] * (len(operands) + len(after)),
-        out_specs=[VMEM] * len(parts),
+        out_specs=[VMEM] * len(sizes),
         scratch_shapes=[
             pltpu.VMEM((SLOTS, tile, wide.shape[2]), wide.dtype),
             pltpu.VMEM((SLOTS, tile, narrow.shape[2]), narrow.dtype),
@@ -338,7 +350,6 @@
 
 def fisher_rows(prior, grads, vector, weights, image):
     me = lax.axis_index("tensor")
-    ones = jnp.ones((8, LANES), jnp.float32)
 
     @pl.loop(0, prior.shape[0] // LANES)
     def _(block):
@@ -349,11 +360,8 @@
             for j in range(2):
                 sums[j] = sums[j] + piece * vector[c // 4, pl.ds(j * 4 + c % 4, 1), :]
         for j in range(2):
-            line = lax.dot_general(
-                ones, sums[j], (((1,), (1,)), ((), ())), precision=HIGH,
-                preferred_element_type=jnp.float32,
-            )
-            image[pl.ds(j * 4 + block, 1), :] = line[:1]
+            line = jnp.sum(sums[j].T, axis=0, keepdims=True)
+            image[pl.ds(j * 4 + block, 1), :] = line
 
     total = grads.shape[0]
     low = weights[0] * grads[0, me]
@@ -480,41 +488,44 @@
     near = lambda x: lax.ppermute(x, "tensor", flipped(n, 1))
     next_to = lambda x: lax.ppermute(x, "tensor", flipped(n, 2))
     beyond = lambda x: lax.ppermute(x, "tensor", flipped(n, 4))
-    (sent0,) = project_rows([(True, 0, 128, 128)], operands)
+    (sent0,) = project_rows([(True, 0, (256,))], operands)
     got0 = near(sent0)
-    (sent1,) = project_rows([(True, 128, 256, 256)], operands, (sent0,))
+    (sent1,) = project_rows([(True, 256, (256,))], operands, (sent0,))
     got1 = near(sent1)
-    (sent2,) = project_rows([(True, 384, 256, 256)], operands, (sent1,))
+    kept0, sent2 = project_rows([(False, 0, (256,)), (True, 512, (256,))], operands, (sent1,))
     got2 = near(sent2)
-    kept01, sent3 = project_rows(
-        [(False, 0, 384, 384), (True, 640, 256, 256)], operands, (sent2, got0)
+    theirs_a, ours_a = halve(0, 1, kept0, (got0,))
+    half_a = next_to(theirs_a)
+    kept1, sent3, sent4 = project_rows(
+        [(False, 256, (256,)), (True, 768, (128, 128))], operands, (sent2, theirs_a)
     )
     got3 = near(sent3)
-    theirs_a, ours_a = halve(0, 1, kept01, (got0, got1))
-    half_a = next_to(theirs_a)
-    kept2, sent4 = project_rows(
-        [(False, 384, 256, 256), (True, 896, 128, 128)], operands, (sent3, theirs_a)
-    )
     got4 = near(sent4)
-    theirs_b, ours_b = halve(0, 1, kept2, (got2,))
+    theirs_b, ours_b = halve(0, 1, kept1, (got1,))
     half_b = next_to(theirs_b)
     send_a, last_a = halve(0, 2, ours_a, (half_a,), (theirs_b,))
     whole_a = beyond(send_a)
-    (kept34,) = project_rows([(False, 640, 384, 128)], operands, (sent4, theirs_b))
-    theirs_c, ours_c = halve(0, 1, kept34, (got3,), (send_a,))
+    kept2, kept3 = project_rows(
+        [(False, 512, (256,)), (False, 768, (256,))], operands, (sent4, send_a)
+    )
+    theirs_c, ours_c = halve(0, 1, kept2, (got2,), (whole_a,))
     half_c = next_to(theirs_c)
     send_b, last_b = halve(0, 2, ours_b, (half_b,), (theirs_c,))
     whole_b = beyond(send_b)
-    theirs_d, ours_d = halve(256, 1, kept34, (got4,), (send_b,))
+    theirs_d, ours_d = halve(0, 1, kept3, (got3,), (send_b,))
     half_d = next_to(theirs_d)
-    send_c, last_c = halve(0, 2, ours_c, (half_c,), (theirs_d,))
+    theirs_e, ours_e = halve(128, 1, kept3, (got4,), (theirs_d,))
+    half_e = next_to(theirs_e)
+    send_c, last_c = halve(0, 2, ours_c, (half_c,), (theirs_e, whole_b))
     whole_c = beyond(send_c)
     send_d, last_d = halve(0, 2, ours_d, (half_d,), (send_c,))
     whole_d = beyond(send_d)
+    send_e, last_e = halve(0, 2, ours_e, (half_e,), (send_d,))
+    whole_e = beyond(send_e)
     square, prior = gram(
-        0, length, counts, (last_a, last_b), (whole_a, whole_b), prior=fisher_prior
-    )
-    grad = gram(640, length, counts, (last_c, last_d), (whole_c, whole_d), before=square)
+        0, length, counts, (last_a, last_b, last_c), (whole_a, whole_b, whole_c), prior=fisher_prior
+    )
+    grad = gram(768, length, counts, (last_d, last_e), (whole_d, whole_e), before=square)
     own = lax.all_to_all(grad, "tensor", 0, 0, tiled=True)
     per = train_inputs.shape[0]
     other = lax.ppermute(own[:per], "dp", flipped(2, 1))

time: 162 us -> 152 us (0.938)
  Pallas kernels: 60.7 us -> 49.2 us
  starting transfers between devices: 21.6 us -> 25.1 us
  waiting for transfers between devices: 12.1 us -> 9.58 us
    pallas_call x6 -> x5, Pallas kernels: 38.6 us -> 32.7 us  [project_rows(): pl.pallas_call(functools.partial(project_kernel, parts, tile, len(after))...]
    pallas_call x7, Pallas kernels: 17.3 us -> 11.7 us  [call(): pl.pallas_call(kernel, out_shape=[jax.ShapeDtypeStruct(s, jnp.float32) fo...]
    ppermute x4 -> x5, waiting for transfers between devices: 3.16 us -> 0.78 us  [per_device(): beyond = lambda x: lax.ppermute(x, 'tensor', flipped(n, 4))]
    ppermute x4 -> x5, starting transfers between devices: 5.95 us -> 7.83 us  [per_device(): next_to = lambda x: lax.ppermute(x, 'tensor', flipped(n, 2))]
    ppermute x4 -> x5, waiting for transfers between devices: 5.6 us -> 4.25 us  [per_device(): next_to = lambda x: lax.ppermute(x, 'tensor', flipped(n, 2))]
    ppermute x4 -> x5, starting transfers between devices: 9.85 us -> 10.2 us  [per_device(): beyond = lambda x: lax.ppermute(x, 'tensor', flipped(n, 4))]
  transfers between devices with their start and end apart: 14 -> 16, of which waited for: 6 -> 7; matrix products, arithmetic and copies ran while one was open for 0% -> 0% of each run, Pallas kernels for 24% -> 21%
where the time goes in v3:
time: 152 us; the launch traced here: 151 us
  blocking collectives  66.4 us (44%)
  Pallas kernels  49.2 us (32%)
  starting transfers between devices  25.1 us (17%)
  waiting for transfers between devices  9.58 us (6%)
    all_to_all x6, blocking collectives, per_device(): swap = lambda x: lax.all_to_all(x, 'tensor', 0, 0, tiled=True)  54.4 us
    pallas_call x5, Pallas kernels, project_rows(): pl.pallas_call(functools.partial(project_kernel, parts, tile, len(after))...  32.7 us
    all_to_all x1, blocking collectives, per_device(): own = lax.all_to_all(grad, 'tensor', 0, 0, tiled=True)  12.1 us
    pallas_call x7, Pallas kernels, call(): pl.pallas_call(kernel, out_shape=[jax.ShapeDtypeStruct(s, jnp.float32) fo...  11.7 us
    ppermute x5, starting transfers between devices, per_device(): beyond = lambda x: lax.ppermute(x, 'tensor', flipped(n, 4))  10.2 us
    ppermute x5, starting transfers between devices, per_device(): next_to = lambda x: lax.ppermute(x, 'tensor', flipped(n, 2))  7.83 us
    ppermute x5, starting transfers between devices, per_device(): near = lambda x: lax.ppermute(x, 'tensor', flipped(n, 1))  6.97 us
    pallas_call x2, Pallas kernels, gram(): pl.pallas_call(functools.partial(gram_kernel, first, len(ours), length, f...  4.4 us
  transfers between devices with their start and end apart: 16, of which 7 were waited for; matrix products, arithmetic and copies ran while one was open for 0% of the time, Pallas kernels for 21%

profile of v3, /device:TPU:0, one launch (start us, length us, event | category | flops | bytes accessed | tf_op | source)
XLA Modules:
  0.0 151.1 jit_solution(8639177651208452672)
XLA Ops:
  0.6 5.2 %project_send0.1.rest_0_ = f32[4,256,128]{2,1,0:T(8,128)S(1)} custom-call(s32[6]{0:T(128)} %train_count.13, s32[2]{0:T(128)} %test_count.13, bf16[6,1024,3584]{2,1,0:T(8,128)(2,1)} %train_in.9, bf16[6,1024,1024]{2,1,0:T(8,128)(2,1)} %train_out.9, bf16[2,1024,3584]{2,1,0:T(8,128)(2,1)} %test_in.9, bf16[2,1024,1024]{2,1,0:T(8,128)(2,1)} %test_out.9, ...), custom_call_target="tpu_custom_call" | custom-call | flops 603979776 | bytes 9437184 | tf_op jit(solution)/shard_map/project_send0/pallas_call | solution.py:214
  5.9 3.0 %collective-permute-start = (f32[4,256,128]{2,1,0:T(8,128)S(1)}, f32[4,256,128]{2,1,0:T(8,128)S(1)}, u32[]{:S(2)}, u32[]{:S(2)}) collective-permute-start(f32[4,256,128]{2,1,0:T(8,128)S(1)} %project_send0.1.rest_0_), channel_id=1, source_target_pairs={{0,2},{2,0},{4,6},{6,4},{8,10},{10,8},{12,14},{14,12},{1,3},{3,1},... | collective-permute-start | bytes 1572872 | tf_op jit(solution)/shard_map/ppermute | solution.py:488
  8.9 5.3 %project_send256.1.rest_0_ = f32[4,256,128]{2,1,0:T(8,128)S(1)} custom-call(s32[6]{0:T(128)} %train_count.13, s32[2]{0:T(128)} %test_count.13, bf16[6,1024,3584]{2,1,0:T(8,128)(2,1)} %train_in.9, bf16[6,1024,1024]{2,1,0:T(8,128)(2,1)} %train_out.9, bf16[2,1024,3584]{2,1,0:T(8,128)(2,1)} %test_in.9, bf16[2,1024,1024]{2,1,0:T(8,128)(2,1)} %test_out.9, ...), custom_call_target="tpu_custom_call" | custom-call | flops 603979776 | bytes 9437184 | tf_op jit(solution)/shard_map/project_send256/pallas_call | solution.py:214
  14.3 8.0 %project_keep0_send512.1 = (f32[4,256,128]{2,1,0:T(8,128)S(1)}, f32[4,256,128]{2,1,0:T(8,128)S(1)}) custom-call(s32[6]{0:T(128)} %train_count.13, s32[2]{0:T(128)} %test_count.13, bf16[6,1024,3584]{2,1,0:T(8,128)(2,1)} %train_in.9, bf16[6,1024,1024]{2,1,0:T(8,128)(2,1)} %train_out.9, bf16[2,1024,3584]{2,1,0:T(8,128)(2,1)} %test_in.9, ...), custom_call_target="tpu_custom_call" | custom-call | flops 1207959552 | bytes 18874368 | tf_op jit(solution)/shard_map/project_keep0_send512/pallas_call | solution.py:214
  25.9 7.8 %project_keep256_send768.1 = (f32[4,256,128]{2,1,0:T(8,128)S(1)}, f32[4,128,128]{2,1,0:T(8,128)S(1)}, f32[4,128,128]{2,1,0:T(8,128)S(1)}) custom-call(s32[6]{0:T(128)} %train_count.13, s32[2]{0:T(128)} %test_count.13, bf16[6,1024,3584]{2,1,0:T(8,128)(2,1)} %train_in.9, bf16[6,1024,1024]{2,1,0:T(8,128)(2,1)} %train_out.9, bf16[2,1024,3584]{2,1,0:T(8,128)(2,1)} %test_in.9, ...), custom_call_target="tpu_custom_call" | custom-call | flops 1207959552 | bytes 18874368 | tf_op jit(solution)/shard_map/project_keep256_send768/pallas_call | solution.py:214
  35.2 2.6 %collective-permute-start.6 = (f32[1,256,128]{2,1,0:T(8,128)S(1)}, f32[1,256,128]{2,1,0:T(8,128)S(1)}, u32[]{:S(2)}, u32[]{:S(2)}) collective-permute-start(f32[1,256,128]{2,1,0:T(8,128)S(1)} %get-tuple-element.60.rest_1_), channel_id=1, source_target_pairs={{0,8},{2,10},{4,12},{6,14},{8,0},{10,2},{12,4},{14,6},{1,9},{3,11}... | collective-permute-start | bytes 393224 | tf_op jit(solution)/shard_map/ppermute | solution.py:490
  39.8 6.4 %project_keep512_keep768.1 = (f32[4,256,128]{2,1,0:T(8,128)S(1)}, f32[4,256,128]{2,1,0:T(8,128)S(1)}) custom-call(s32[6]{0:T(128)} %train_count.13, s32[2]{0:T(128)} %test_count.13, bf16[6,1024,3584]{2,1,0:T(8,128)(2,1)} %train_in.9, bf16[6,1024,1024]{2,1,0:T(8,128)(2,1)} %train_out.9, bf16[2,1024,3584]{2,1,0:T(8,128)(2,1)} %test_in.9, ...), custom_call_target="tpu_custom_call" | custom-call | flops 1207959552 | bytes 18874368 | tf_op jit(solution)/shard_map/project_keep512_keep768/pallas_call | solution.py:214
  47.1 1.9 %collective-permute-start.10 = (f32[1,256,128]{2,1,0:T(8,128)S(1)}, f32[1,256,128]{2,1,0:T(8,128)S(1)}, u32[]{:S(2)}, u32[]{:S(2)}) collective-permute-start(f32[1,256,128]{2,1,0:T(8,128)S(1)} %get-tuple-element.66.rest_1_), channel_id=1, source_target_pairs={{0,8},{2,10},{4,12},{6,14},{8,0},{10,2},{12,4},{14,6},{1,9},{3,11}... | collective-permute-start | bytes 393224 | tf_op jit(solution)/shard_map/ppermute | solution.py:490
  49.8 2.2 %collective-permute-start.7 = (f32[2,128,128]{2,1,0:T(8,128)S(1)}, f32[2,128,128]{2,1,0:T(8,128)S(1)}, u32[]{:S(2)}, u32[]{:S(2)}) collective-permute-start(f32[2,128,128]{2,1,0:T(8,128)S(1)} %get-tuple-element.68.rest_1_), channel_id=1, source_target_pairs={{0,4},{2,6},{4,0},{6,2},{8,12},{10,14},{12,8},{14,10},{1,5},{3,7},... | collective-permute-start | bytes 393224 | tf_op jit(solution)/shard_map/ppermute | solution.py:489
  52.0 2.6 %collective-permute-done.9.rest_0_ = f32[4,128,128]{2,1,0:T(8,128)S(1)} collective-permute-done((f32[4,128,128]{2,1,0:T(8,128)S(1)}, f32[4,128,128]{2,1,0:T(8,128)S(1)}, u32[]{:S(2)}, u32[]{:S(2)}) %collective-permute-start.9) | collective-permute-done | bytes 262176 | tf_op jit(solution)/shard_map/ppermute | solution.py:488
  54.6 1.9 %collective-permute-start.11 = (f32[2,128,128]{2,1,0:T(8,128)S(1)}, f32[2,128,128]{2,1,0:T(8,128)S(1)}, u32[]{:S(2)}, u32[]{:S(2)}) collective-permute-start(f32[2,128,128]{2,1,0:T(8,128)S(1)} %get-tuple-element.70.rest_1_), channel_id=1, source_target_pairs={{0,4},{2,6},{4,0},{6,2},{8,12},{10,14},{12,8},{14,10},{1,5},{3,7},... | collective-permute-start | bytes 393224 | tf_op jit(solution)/shard_map/ppermute | solution.py:489
  56.6 2.7 %collective-permute-start.14 = (f32[1,256,128]{2,1,0:T(8,128)S(1)}, f32[1,256,128]{2,1,0:T(8,128)S(1)}, u32[]{:S(2)}, u32[]{:S(2)}) collective-permute-start(f32[1,256,128]{2,1,0:T(8,128)S(1)} %get-tuple-element.71.rest_1_), channel_id=1, source_target_pairs={{0,8},{2,10},{4,12},{6,14},{8,0},{10,2},{12,4},{14,6},{1,9},{3,11}... | collective-permute-start | bytes 393224 | tf_op jit(solution)/shard_map/ppermute | solution.py:490
  60.6 2.8 %collective-permute-done.11.rest_0_ = f32[2,128,128]{2,1,0:T(8,128)S(1)} collective-permute-done((f32[2,128,128]{2,1,0:T(8,128)S(1)}, f32[2,128,128]{2,1,0:T(8,128)S(1)}, u32[]{:S(2)}, u32[]{:S(2)}) %collective-permute-start.11) | collective-permute-done | bytes 131104 | tf_op jit(solution)/shard_map/ppermute | solution.py:489
  63.5 2.9 %collective-permute-start.12 = (f32[1,128,128]{2,1,0:T(8,128)S(1)}, f32[1,128,128]{2,1,0:T(8,128)S(1)}, u32[]{:S(2)}, u32[]{:S(2)}) collective-permute-start(f32[1,128,128]{2,1,0:T(8,128)S(1)} %get-tuple-element.74.rest_1_), channel_id=1, source_target_pairs={{0,8},{2,10},{4,12},{6,14},{8,0},{10,2},{12,4},{14,6},{1,9},{3,11}... | collective-permute-start | bytes 196616 | tf_op jit(solution)/shard_map/ppermute | solution.py:490
  66.4 3.4 %gram_begin.1 = (f32[64,64]{1,0:T(8,128)S(1)}, f32[512,4096]{1,0:T(8,128)S(1)}) custom-call(s32[6]{0:T(128)} %train_count.13, s32[2]{0:T(128)} %test_count.13, f32[1,256,128]{2,1,0:T(8,128)S(1)} %get-tuple-element.77.rest_0_, f32[1,256,128]{2,1,0:T(8,128)S(1)} %get-tuple-element.78.rest_1_, f32[1,256,128]{2,1,0:T(8,128)S(1)} %get-tuple-element.79.rest_2_, ...), custom_call_target="tpu_custom_call" | custom-call | tf_op jit(solution)/shard_map/gram_begin/pallas_call | solution.py:322
  71.6 12.1 %all_to_all.35.own = f32[8,32,128]{2,1,0:T(8,128)S(1)} all-to-all(f32[8,32,128]{2,1,0:T(8,128)S(1)} %gram_end.1), channel_id=1, replica_groups=mesh['parts'=2,'tensor'=8,'dp'=2] {'tensor'}, dimensions={0} | all-to-all | bytes 262144 | tf_op jit(solution)/shard_map/all_to_all | solution.py:529
  86.8 9.1 %all_to_all.36.images = f32[8,8,128]{2,1,0:T(8,128)S(1)} all-to-all(f32[8,8,128]{2,1,0:T(8,128)S(1)} %get-tuple-element.82), channel_id=1, replica_groups=mesh['parts'=2,'tensor'=8,'dp'=2] {'tensor'}, dimensions={0} | all-to-all | bytes 65536 | tf_op jit(solution)/shard_map/all_to_all | solution.py:538
  97.7 9.1 %all_to_all.37.images = f32[8,8,128]{2,1,0:T(8,128)S(1)} all-to-all(f32[8,8,128]{2,1,0:T(8,128)S(1)} %get-tuple-element.85), channel_id=1, replica_groups=mesh['parts'=2,'tensor'=8,'dp'=2] {'tensor'}, dimensions={0} | all-to-all | bytes 65536 | tf_op jit(solution)/shard_map/all_to_all | solution.py:538
  106.8 1.8 %step_kernel.3 = (f32[8,8,128]{2,1,0:T(8,128)S(1)}, f32[8,8,128]{2,1,0:T(8,128)S(1)}, f32[8,8,128]{2,1,0:T(8,128)S(1)}, f32[8,8,128]{2,1,0:T(8,128)S(1)}) custom-call(f32[8,8,128]{2,1,0:T(8,128)S(1)} %all_to_all.37.images, f32[8,8,128]{2,1,0:T(8,128)S(1)} %get-tuple-element.86.solution, f32[8,8,128]{2,1,0:T(8,128)S(1)} %get-tuple-element.87.residue, ...), custom_call_target="tpu_custom_call" | custom-call | tf_op jit(solution)/shard_map/step_kernel/pallas_call | solution.py:456
  108.6 9.1 %all_to_all.38.images = f32[8,8,128]{2,1,0:T(8,128)S(1)} all-to-all(f32[8,8,128]{2,1,0:T(8,128)S(1)} %get-tuple-element.89), channel_id=1, replica_groups=mesh['parts'=2,'tensor'=8,'dp'=2] {'tensor'}, dimensions={0} | all-to-all | bytes 65536 | tf_op jit(solution)/shard_map/all_to_all | solution.py:538
  119.5 9.1 %all_to_all.39.images = f32[8,8,128]{2,1,0:T(8,128)S(1)} all-to-all(f32[8,8,128]{2,1,0:T(8,128)S(1)} %get-tuple-element.93), channel_id=1, replica_groups=mesh['parts'=2,'tensor'=8,'dp'=2] {'tensor'}, dimensions={0} | all-to-all | bytes 65536 | tf_op jit(solution)/shard_map/all_to_all | solution.py:538
  130.4 9.1 %all_to_all.40.images = f32[8,8,128]{2,1,0:T(8,128)S(1)} all-to-all(f32[8,8,128]{2,1,0:T(8,128)S(1)} %get-tuple-element.97), channel_id=1, replica_groups=mesh['parts'=2,'tensor'=8,'dp'=2] {'tensor'}, dimensions={0} | all-to-all | bytes 65536 | tf_op jit(solution)/shard_map/all_to_all | solution.py:538
  139.5 1.9 %last_kernel.1 = (f32[3,8,128]{2,1,0:T(8,128)S(1)}, f32[8,8,128]{2,1,0:T(8,128)S(1)}, f32[2,12,8,128]{3,2,1,0:T(8,128)S(1)}) custom-call(f32[8,8,128]{2,1,0:T(8,128)S(1)} %all_to_all.40.images, f32[8,8,128]{2,1,0:T(8,128)S(1)} %get-tuple-element.98.solution, f32[8,8,128]{2,1,0:T(8,128)S(1)} %get-tuple-element.99.residue, ...), custom_call_target="tpu_custom_call" | custom-call | tf_op jit(solution)/shard_map/last_kernel/pallas_call | solution.py:456
  141.4 9.1 %all_to_all.41.curves = f32[8,8,128]{2,1,0:T(8,128)S(1)} all-to-all(f32[8,8,128]{2,1,0:T(8,128)S(1)} %get-tuple-element.101), channel_id=1, replica_groups=mesh['parts'=2,'tensor'=8,'dp'=2] {'tensor'}, dimensions={0} | all-to-all | bytes 65536 | tf_op jit(solution)/shard_map/all_to_all | solution.py:538
  (44 shorter events, 21.4 us)
Async XLA Ops:
  5.9 18.3 %collective-permute-start = (f32[4,256,128]{2,1,0:T(8,128)S(1)}, f32[4,256,128]{2,1,0:T(8,128)S(1)}, u32[]{:S(2)}, u32[]{:S(2)}) collective-permute-start(f32[4,256,128]{2,1,0:T(8,128)S(1)} %project_send0.1.rest_0_), channel_id=1, source_target_pairs={{0,2},{2,0},{4,6},{6,4},{8,10},{10,8},{12,14},{14,12},{1,3},{3,1},... | collective-permute-start | bytes 1572872 | tf_op jit(solution)/shard_map/ppermute | solution.py:488
  14.2 19.5 %collective-permute-start.2 = (f32[4,256,128]{2,1,0:T(8,128)S(1)}, f32[4,256,128]{2,1,0:T(8,128)S(1)}, u32[]{:S(2)}, u32[]{:S(2)}) collective-permute-start(f32[4,256,128]{2,1,0:T(8,128)S(1)} %project_send256.1.rest_0_), channel_id=1, source_target_pairs={{0,2},{2,0},{4,6},{6,4},{8,10},{10,8},{12,14},{14,12},{1,3},{3,1},... | collective-permute-start | bytes 1572872 | tf_op jit(solution)/shard_map/ppermute | solution.py:488
  22.3 23.9 %collective-permute-start.5 = (f32[4,256,128]{2,1,0:T(8,128)S(1)}, f32[4,256,128]{2,1,0:T(8,128)S(1)}, u32[]{:S(2)}, u32[]{:S(2)}) collective-permute-start(f32[4,256,128]{2,1,0:T(8,128)S(1)} %get-tuple-element.53.rest_0_), channel_id=1, source_target_pairs={{0,2},{2,0},{4,6},{6,4},{8,10},{10,8},{12,14},{14,12},{1,3},{3,1},... | collective-permute-start | bytes 1572872 | tf_op jit(solution)/shard_map/ppermute | solution.py:488
  24.2 10.9 %collective-permute-start.1 = (f32[2,256,128]{2,1,0:T(8,128)S(1)}, f32[2,256,128]{2,1,0:T(8,128)S(1)}, u32[]{:S(2)}, u32[]{:S(2)}) collective-permute-start(f32[2,256,128]{2,1,0:T(8,128)S(1)} %get-tuple-element.55.rest_1_), channel_id=1, source_target_pairs={{0,4},{2,6},{4,0},{6,2},{8,12},{10,14},{12,8},{14,10},{1,5},{3,7},... | collective-permute-start | bytes 786440 | tf_op jit(solution)/shard_map/ppermute | solution.py:489
  33.7 13.4 %collective-permute-start.4 = (f32[2,256,128]{2,1,0:T(8,128)S(1)}, f32[2,256,128]{2,1,0:T(8,128)S(1)}, u32[]{:S(2)}, u32[]{:S(2)}) collective-permute-start(f32[2,256,128]{2,1,0:T(8,128)S(1)} %get-tuple-element.59.rest_1_), channel_id=1, source_target_pairs={{0,4},{2,6},{4,0},{6,2},{8,12},{10,14},{12,8},{14,10},{1,5},{3,7},... | collective-permute-start | bytes 786440 | tf_op jit(solution)/shard_map/ppermute | solution.py:489
  35.2 11.1 %collective-permute-start.6 = (f32[1,256,128]{2,1,0:T(8,128)S(1)}, f32[1,256,128]{2,1,0:T(8,128)S(1)}, u32[]{:S(2)}, u32[]{:S(2)}) collective-permute-start(f32[1,256,128]{2,1,0:T(8,128)S(1)} %get-tuple-element.60.rest_1_), channel_id=1, source_target_pairs={{0,8},{2,10},{4,12},{6,14},{8,0},{10,2},{12,4},{14,6},{1,9},{3,11}... | collective-permute-start | bytes 393224 | tf_op jit(solution)/shard_map/ppermute | solution.py:490
  37.8 11.9 %collective-permute-start.3 = (f32[4,128,128]{2,1,0:T(8,128)S(1)}, f32[4,128,128]{2,1,0:T(8,128)S(1)}, u32[]{:S(2)}, u32[]{:S(2)}) collective-permute-start(f32[4,128,128]{2,1,0:T(8,128)S(1)} %get-tuple-element.62), channel_id=1, source_target_pairs={{0,2},{2,0},{4,6},{6,4},{8,10},{10,8},{12,14},{14,12},{1,3},{3,1},... | collective-permute-start | bytes 786440 | tf_op jit(solution)/shard_map/ppermute | solution.py:488
  39.3 15.2 %collective-permute-start.9 = (f32[4,128,128]{2,1,0:T(8,128)S(1)}, f32[4,128,128]{2,1,0:T(8,128)S(1)}, u32[]{:S(2)}, u32[]{:S(2)}) collective-permute-start(f32[4,128,128]{2,1,0:T(8,128)S(1)} %get-tuple-element.56.rest_0_), channel_id=1, source_target_pairs={{0,2},{2,0},{4,6},{6,4},{8,10},{10,8},{12,14},{14,12},{1,3},{3,1},... | collective-permute-start | bytes 786440 | tf_op jit(solution)/shard_map/ppermute | solution.py:488
  46.2 24.4 %copy-start = (s32[6]{0:T(128)S(1)}, s32[6]{0:T(128)}, u32[]{:S(2)}) copy-start(s32[6]{0:T(128)} %train_count.13) | copy-start | bytes 76
  46.2 24.4 %copy-start.1 = (s32[2]{0:T(128)S(1)}, s32[2]{0:T(128)}, u32[]{:S(2)}) copy-start(s32[2]{0:T(128)} %test_count.13) | copy-start | bytes 28
  46.3 10.2 %collective-permute-start.8 = (f32[2,256,128]{2,1,0:T(8,128)S(1)}, f32[2,256,128]{2,1,0:T(8,128)S(1)}, u32[]{:S(2)}, u32[]{:S(2)}) collective-permute-start(f32[2,256,128]{2,1,0:T(8,128)S(1)} %get-tuple-element.65.rest_1_), channel_id=1, source_target_pairs={{0,4},{2,6},{4,0},{6,2},{8,12},{10,14},{12,8},{14,10},{1,5},{3,7},... | collective-permute-start | bytes 786440 | tf_op jit(solution)/shard_map/ppermute | solution.py:489
  47.1 9.3 %collective-permute-start.10 = (f32[1,256,128]{2,1,0:T(8,128)S(1)}, f32[1,256,128]{2,1,0:T(8,128)S(1)}, u32[]{:S(2)}, u32[]{:S(2)}) collective-permute-start(f32[1,256,128]{2,1,0:T(8,128)S(1)} %get-tuple-element.66.rest_1_), channel_id=1, source_target_pairs={{0,8},{2,10},{4,12},{6,14},{8,0},{10,2},{12,4},{14,6},{1,9},{3,11}... | collective-permute-start | bytes 393224 | tf_op jit(solution)/shard_map/ppermute | solution.py:490
  49.8 10.8 %collective-permute-start.7 = (f32[2,128,128]{2,1,0:T(8,128)S(1)}, f32[2,128,128]{2,1,0:T(8,128)S(1)}, u32[]{:S(2)}, u32[]{:S(2)}) collective-permute-start(f32[2,128,128]{2,1,0:T(8,128)S(1)} %get-tuple-element.68.rest_1_), channel_id=1, source_target_pairs={{0,4},{2,6},{4,0},{6,2},{8,12},{10,14},{12,8},{14,10},{1,5},{3,7},... | collective-permute-start | bytes 393224 | tf_op jit(solution)/shard_map/ppermute | solution.py:489
  54.6 8.8 %collective-permute-start.11 = (f32[2,128,128]{2,1,0:T(8,128)S(1)}, f32[2,128,128]{2,1,0:T(8,128)S(1)}, u32[]{:S(2)}, u32[]{:S(2)}) collective-permute-start(f32[2,128,128]{2,1,0:T(8,128)S(1)} %get-tuple-element.70.rest_1_), channel_id=1, source_target_pairs={{0,4},{2,6},{4,0},{6,2},{8,12},{10,14},{12,8},{14,10},{1,5},{3,7},... | collective-permute-start | bytes 393224 | tf_op jit(solution)/shard_map/ppermute | solution.py:489
  56.6 9.8 %collective-permute-start.14 = (f32[1,256,128]{2,1,0:T(8,128)S(1)}, f32[1,256,128]{2,1,0:T(8,128)S(1)}, u32[]{:S(2)}, u32[]{:S(2)}) collective-permute-start(f32[1,256,128]{2,1,0:T(8,128)S(1)} %get-tuple-element.71.rest_1_), channel_id=1, source_target_pairs={{0,8},{2,10},{4,12},{6,14},{8,0},{10,2},{12,4},{14,6},{1,9},{3,11}... | collective-permute-start | bytes 393224 | tf_op jit(solution)/shard_map/ppermute | solution.py:490
  63.4 6.4 %collective-permute-start.13 = (f32[1,128,128]{2,1,0:T(8,128)S(1)}, f32[1,128,128]{2,1,0:T(8,128)S(1)}, u32[]{:S(2)}, u32[]{:S(2)}) collective-permute-start(f32[1,128,128]{2,1,0:T(8,128)S(1)} %get-tuple-element.76), channel_id=1, source_target_pairs={{0,8},{2,10},{4,12},{6,14},{8,0},{10,2},{12,4},{14,6},{1,9},{3,11}... | collective-permute-start | bytes 196616 | tf_op jit(solution)/shard_map/ppermute | solution.py:490
  63.5 7.1 %collective-permute-start.12 = (f32[1,128,128]{2,1,0:T(8,128)S(1)}, f32[1,128,128]{2,1,0:T(8,128)S(1)}, u32[]{:S(2)}, u32[]{:S(2)}) collective-permute-start(f32[1,128,128]{2,1,0:T(8,128)S(1)} %get-tuple-element.74.rest_1_), channel_id=1, source_target_pairs={{0,8},{2,10},{4,12},{6,14},{8,0},{10,2},{12,4},{14,6},{1,9},{3,11}... | collective-permute-start | bytes 196616 | tf_op jit(solution)/shard_map/ppermute | solution.py:490
  83.7 1.4 collective-permute-start.15

commit v4 on v3

--- a/solution.py
+++ b/solution.py
@@ -234,33 +234,34 @@
     )(*in_hbm(operands), *after)
 
 
-def halve_kernel(offset, bit, pieces, kept, *rest):
-    got, (theirs, ours) = rest[:pieces], rest[-2:]
+def halve_kernel(offsets, bit, *refs):
+    pairs = len(offsets)
+    kept, got, (theirs, ours) = refs[:pairs], refs[pairs : 2 * pairs], refs[-2:]
     mine = (lax.axis_index("tensor") >> bit) & 1
-    groups = theirs.shape[0]
     at = 0
-    for piece in got:
+    for offset, base, piece in zip(offsets, kept, got):
         rows = piece.shape[1]
-        here, there = pl.ds(offset + at, rows), pl.ds(at, rows)
-        for h in range(groups):
+        here, there = pl.ds(offset, rows), pl.ds(at, rows)
+        for h in range(theirs.shape[0]):
             give = 2 * h + 1 - mine if bit == 1 else 1 - mine
             take = 2 * h + mine if bit == 1 else mine
-            theirs[h, there, :] = kept[give, here, :] + piece[give, :, :]
-            ours[h, there, :] = kept[take, here, :] + piece[take, :, :]
+            theirs[h, there, :] = base[give, here, :] + piece[give, :, :]
+            ours[h, there, :] = base[take, here, :] + piece[take, :, :]
         at += rows
 
 
-def halve(offset, bit, kept, got, after=()):
+def halve(bit, pairs, after=()):
+    kept, offsets, got = zip(*pairs)
     rows = sum(piece.shape[1] for piece in got)
-    shape = pltpu.VMEM((kept.shape[0] // 2, rows, LANES), jnp.float32)
+    shape = pltpu.VMEM((kept[0].shape[0] // 2, rows, LANES), jnp.float32)
     return pl.pallas_call(
-        functools.partial(halve_kernel, offset, bit, len(got)),
+        functools.partial(halve_kernel, offsets, bit),
         out_shape=[shape, shape],
-        in_specs=[VMEM] * (1 + len(got)) + [ANY] * len(after),
+        in_specs=[VMEM] * (2 * len(pairs)) + [ANY] * len(after),
         out_specs=[VMEM, VMEM],
         compiler_params=pltpu.CompilerParams(vmem_limit_bytes=SMALL),
         name=f"halve{bit}",
-    )(kept, *got, *after)
+    )(*kept, *got, *after)
 
 
 def gram_kernel(first, pieces, length, final, train_count, test_count, *rest):
@@ -372,15 +373,17 @@
 
 def begin_kernel(own, other, prior, grads, search, payload, image):
     me = lax.axis_index("dp")
-    per = other.shape[0]
+    per = grads.shape[0] // 2
     for i in range(per):
+        at = ORDER.index(i)
         for s in range(8):
             for half in range(2):
-                grads[me * per + i, s, pl.ds(half * 4, 4), :] = own[i, pl.ds(s * 4, 4), :]
-                grads[(1 - me) * per + i, s, pl.ds(half * 4, 4), :] = other[i, pl.ds(s * 4, 4), :]
+                there, here = pl.ds(half * 4, 4), pl.ds(s * 4, 4)
+                grads[me * per + i, s, there, :] = own[at, here, :]
+                grads[(1 - me) * per + i, s, there, :] = other[at, here, :]
     for j in range(2):
         for s in range(8):
-            search[s, pl.ds(j * 4, 4), :] = own[per + j, pl.ds(s * 4, 4), :]
+            search[s, pl.ds(j * 4, 4), :] = own[ORDER.index(per + j), pl.ds(s * 4, 4), :]
     fisher_rows(prior, grads, search, weights_of(grads, search[...]), image)
     for s in range(8):
         payload[s] = image[...]
@@ -389,7 +392,7 @@
 def advance(first, images, solution, residue, search, new_solution, new_residue, new_search):
     old = search[...]
     rest = old if first else residue[...]
-    image = images[...]
+    image = jnp.stack([images[ORDER.index(s)] for s in range(8)])
     norm = inner(rest, rest)
     alpha = norm / inner(old, image)
     new_solution[...] = alpha * old if first else solution[...] + alpha * old
@@ -464,6 +467,14 @@
     )(*operands)
 
 
+def nearest_first(n, first):
+    far = lambda i: abs((i >> 1) - (first >> 1)) + abs((i & 1) - (first & 1))
+    return sorted(range(n), key=lambda i: (far(i), i))
+
+
+ORDER = nearest_first(8, 2)
+
+
 def flipped(n, bit):
     return [(i, i ^ bit) for i in range(n)]
 
@@ -494,48 +505,48 @@
     got1 = near(sent1)
     kept0, sent2 = project_rows([(False, 0, (256,)), (True, 512, (256,))], operands, (sent1,))
     got2 = near(sent2)
-    theirs_a, ours_a = halve(0, 1, kept0, (got0,))
+    theirs_a, ours_a = halve(1, [(kept0, 0, got0)])
     half_a = next_to(theirs_a)
     kept1, sent3, sent4 = project_rows(
         [(False, 256, (256,)), (True, 768, (128, 128))], operands, (sent2, theirs_a)
     )
     got3 = near(sent3)
     got4 = near(sent4)
-    theirs_b, ours_b = halve(0, 1, kept1, (got1,))
+    theirs_b, ours_b = halve(1, [(kept1, 0, got1)])
     half_b = next_to(theirs_b)
-    send_a, last_a = halve(0, 2, ours_a, (half_a,), (theirs_b,))
+    send_a, last_a = halve(2, [(ours_a, 0, half_a)], (theirs_b,))
     whole_a = beyond(send_a)
     kept2, kept3 = project_rows(
         [(False, 512, (256,)), (False, 768, (256,))], operands, (sent4, send_a)
     )
-    theirs_c, ours_c = halve(0, 1, kept2, (got2,), (whole_a,))
+    theirs_c, ours_c = halve(1, [(kept2, 0, got2)], (whole_a,))
     half_c = next_to(theirs_c)
-    send_b, last_b = halve(0, 2, ours_b, (half_b,), (theirs_c,))
+    send_b, last_b = halve(2, [(ours_b, 0, half_b)], (theirs_c,))
     whole_b = beyond(send_b)
-    theirs_d, ours_d = halve(0, 1, kept3, (got3,), (send_b,))
+    theirs_d, ours_d = halve(1, [(kept3, 0, got3)], (send_b,))
     half_d = next_to(theirs_d)
-    theirs_e, ours_e = halve(128, 1, kept3, (got4,), (theirs_d,))
+    theirs_e, ours_e = halve(1, [(kept3, 128, got4)], (theirs_d,))
     half_e = next_to(theirs_e)
-    send_c, last_c = halve(0, 2, ours_c, (half_c,), (theirs_e, whole_b))
+    send_c, last_c = halve(2, [(ours_c, 0, half_c)], (theirs_e, whole_b))
     whole_c = beyond(send_c)
-    send_d, last_d = halve(0, 2, ours_d, (half_d,), (send_c,))
+    send_d, last_d = halve(2, [(ours_d, 0, half_d)], (send_c,))
     whole_d = beyond(send_d)
-    send_e, last_e = halve(0, 2, ours_e, (half_e,), (send_d,))
+    send_e, last_e = halve(2, [(ours_e, 0, half_e)], (send_d,))
     whole_e = beyond(send_e)
     square, prior = gram(
         0, length, counts, (last_a, last_b, last_c), (whole_a, whole_b, whole_c), prior=fisher_prior
     )
     grad = gram(768, length, counts, (last_d, last_e), (whole_d, whole_e), before=square)
-    own = lax.all_to_all(grad, "tensor", 0, 0, tiled=True)
+    own = lax.all_to_all(grad, "tensor", 0, 0, tiled=True, axis_index_groups=[ORDER])
+    other = lax.ppermute(own, "dp", flipped(2, 1))
     per = train_inputs.shape[0]
-    other = lax.ppermute(own[:per], "dp", flipped(2, 1))
     state = (8, 8, LANES)
     piece = (8, LANES)
     total = 2 * per
     grads, search, payload = call(
         begin_kernel, [(total, 8, 8, LANES), state, state], (own, other, prior), [piece]
     )
-    swap = lambda x: lax.all_to_all(x, "tensor", 0, 0, tiled=True)
+    swap = lambda x: lax.all_to_all(x, "tensor", 0, 0, tiled=True, axis_index_groups=[ORDER])
     solution, residue, search, payload = call(
         first_kernel, [state] * 4, (swap(payload), search, grads, prior), [piece]
     )

time: 152 us -> 145 us (0.954)
  blocking collectives: 66.4 us -> 61 us
    all_to_all x7, blocking collectives: 66.4 us -> 61 us  [the longest x6 49.8 us: per_device(): lax.all_to_all(x, 'tensor', 0, 0, tiled=True, axis_index_groups=[ORDER])]
  transfers between devices with their start and end apart: 16 -> 16, of which waited for: 7 -> 7; matrix products, arithmetic and copies ran while one was open for 0% -> 0% of each run, Pallas kernels for 21% -> 22%
where the time goes in v4:
time: 145 us
  blocking collectives  61 us (42%)
  Pallas kernels  49.4 us (34%)
  starting transfers between devices  24.3 us (17%)
  waiting for transfers between devices  9.3 us (6%)
    all_to_all x6, blocking collectives, per_device(): lax.all_to_all(x, 'tensor', 0, 0, tiled=True, axis_index_groups=[ORDER])  49.8 us
    pallas_call x5, Pallas kernels, project_rows(): pl.pallas_call(functools.partial(project_kernel, parts, tile, len(after))...  33 us
    pallas_call x7, Pallas kernels, call(): pl.pallas_call(kernel, out_shape=[jax.ShapeDtypeStruct(s, jnp.float32) fo...  11.7 us
    all_to_all x1, blocking collectives, per_device(): lax.all_to_all(grad, 'tensor', 0, 0, tiled=True, axis_index_groups=[ORDER])  11.2 us
    ppermute x5, starting transfers between devices, per_device(): beyond = lambda x: lax.ppermute(x, 'tensor', flipped(n, 4))  8.75 us
    ppermute x5, starting transfers between devices, per_device(): next_to = lambda x: lax.ppermute(x, 'tensor', flipped(n, 2))  8.38 us
    ppermute x5, starting transfers between devices, per_device(): near = lambda x: lax.ppermute(x, 'tensor', flipped(n, 1))  7.2 us
    pallas_call x2, Pallas kernels, gram(): pl.pallas_call(functools.partial(gram_kernel, first, len(ours), length, f...  4.4 us
  transfers between devices with their start and end apart: 16, of which 7 were waited for; matrix products, arithmetic and copies ran while one was open for 0% of the time, Pallas kernels for 22%

profile of v4, /device:TPU:0, one launch (start us, length us, event | category | flops | bytes accessed | tf_op | source)
XLA Modules:
  0.0 144.9 jit_solution(695069865299616198)
XLA Ops:
  0.6 5.2 %project_send0.1.rest_0_ = f32[4,256,128]{2,1,0:T(8,128)S(1)} custom-call(s32[6]{0:T(128)} %train_count.13, s32[2]{0:T(128)} %test_count.13, bf16[6,1024,3584]{2,1,0:T(8,128)(2,1)} %train_in.9, bf16[6,1024,1024]{2,1,0:T(8,128)(2,1)} %train_out.9, bf16[2,1024,3584]{2,1,0:T(8,128)(2,1)} %test_in.9, bf16[2,1024,1024]{2,1,0:T(8,128)(2,1)} %test_out.9, ...), custom_call_target="tpu_custom_call" | custom-call | flops 603979776 | bytes 9437184 | tf_op jit(solution)/shard_map/project_send0/pallas_call | solution.py:214
  5.9 3.0 %collective-permute-start = (f32[4,256,128]{2,1,0:T(8,128)S(1)}, f32[4,256,128]{2,1,0:T(8,128)S(1)}, u32[]{:S(2)}, u32[]{:S(2)}) collective-permute-start(f32[4,256,128]{2,1,0:T(8,128)S(1)} %project_send0.1.rest_0_), channel_id=1, source_target_pairs={{0,2},{2,0},{4,6},{6,4},{8,10},{10,8},{12,14},{14,12},{1,3},{3,1},... | collective-permute-start | bytes 1572872 | tf_op jit(solution)/shard_map/ppermute | solution.py:499
  8.9 5.3 %project_send256.1.rest_0_ = f32[4,256,128]{2,1,0:T(8,128)S(1)} custom-call(s32[6]{0:T(128)} %train_count.13, s32[2]{0:T(128)} %test_count.13, bf16[6,1024,3584]{2,1,0:T(8,128)(2,1)} %train_in.9, bf16[6,1024,1024]{2,1,0:T(8,128)(2,1)} %train_out.9, bf16[2,1024,3584]{2,1,0:T(8,128)(2,1)} %test_in.9, bf16[2,1024,1024]{2,1,0:T(8,128)(2,1)} %test_out.9, ...), custom_call_target="tpu_custom_call" | custom-call | flops 603979776 | bytes 9437184 | tf_op jit(solution)/shard_map/project_send256/pallas_call | solution.py:214
  14.3 8.0 %project_keep0_send512.1 = (f32[4,256,128]{2,1,0:T(8,128)S(1)}, f32[4,256,128]{2,1,0:T(8,128)S(1)}) custom-call(s32[6]{0:T(128)} %train_count.13, s32[2]{0:T(128)} %test_count.13, bf16[6,1024,3584]{2,1,0:T(8,128)(2,1)} %train_in.9, bf16[6,1024,1024]{2,1,0:T(8,128)(2,1)} %train_out.9, bf16[2,1024,3584]{2,1,0:T(8,128)(2,1)} %test_in.9, ...), custom_call_target="tpu_custom_call" | custom-call | flops 1207959552 | bytes 18874368 | tf_op jit(solution)/shard_map/project_keep0_send512/pallas_call | solution.py:214
  22.3 2.1 %collective-permute-start.5 = (f32[4,256,128]{2,1,0:T(8,128)S(1)}, f32[4,256,128]{2,1,0:T(8,128)S(1)}, u32[]{:S(2)}, u32[]{:S(2)}) collective-permute-start(f32[4,256,128]{2,1,0:T(8,128)S(1)} %get-tuple-element.53.rest_0_), channel_id=1, source_target_pairs={{0,2},{2,0},{4,6},{6,4},{8,10},{10,8},{12,14},{14,12},{1,3},{3,1},... | collective-permute-start | bytes 1572872 | tf_op jit(solution)/shard_map/ppermute | solution.py:499
  26.1 6.4 %project_keep256_send768.1 = (f32[4,256,128]{2,1,0:T(8,128)S(1)}, f32[4,128,128]{2,1,0:T(8,128)S(1)}, f32[4,128,128]{2,1,0:T(8,128)S(1)}) custom-call(s32[6]{0:T(128)} %train_count.13, s32[2]{0:T(128)} %test_count.13, bf16[6,1024,3584]{2,1,0:T(8,128)(2,1)} %train_in.9, bf16[6,1024,1024]{2,1,0:T(8,128)(2,1)} %train_out.9, bf16[2,1024,3584]{2,1,0:T(8,128)(2,1)} %test_in.9, ...), custom_call_target="tpu_custom_call" | custom-call | flops 1207959552 | bytes 18874368 | tf_op jit(solution)/shard_map/project_keep256_send768/pallas_call | solution.py:214
  33.0 2.2 %collective-permute-start.4 = (f32[2,256,128]{2,1,0:T(8,128)S(1)}, f32[2,256,128]{2,1,0:T(8,128)S(1)}, u32[]{:S(2)}, u32[]{:S(2)}) collective-permute-start(f32[2,256,128]{2,1,0:T(8,128)S(1)} %get-tuple-element.59.refs_2_), channel_id=1, source_target_pairs={{0,4},{2,6},{4,0},{6,2},{8,12},{10,14},{12,8},{14,10},{1,5},{3,7},... | collective-permute-start | bytes 786440 | tf_op jit(solution)/shard_map/ppermute | solution.py:500
  35.2 2.6 %collective-permute-start.6 = (f32[1,256,128]{2,1,0:T(8,128)S(1)}, f32[1,256,128]{2,1,0:T(8,128)S(1)}, u32[]{:S(2)}, u32[]{:S(2)}) collective-permute-start(f32[1,256,128]{2,1,0:T(8,128)S(1)} %get-tuple-element.60.rest_1_), channel_id=1, source_target_pairs={{0,8},{2,10},{4,12},{6,14},{8,0},{10,2},{12,4},{14,6},{1,9},{3,11}... | collective-permute-start | bytes 393224 | tf_op jit(solution)/shard_map/ppermute | solution.py:501
  39.8 8.0 %project_keep512_keep768.1 = (f32[4,256,128]{2,1,0:T(8,128)S(1)}, f32[4,256,128]{2,1,0:T(8,128)S(1)}) custom-call(s32[6]{0:T(128)} %train_count.13, s32[2]{0:T(128)} %test_count.13, bf16[6,1024,3584]{2,1,0:T(8,128)(2,1)} %train_in.9, bf16[6,1024,1024]{2,1,0:T(8,128)(2,1)} %train_out.9, bf16[2,1024,3584]{2,1,0:T(8,128)(2,1)} %test_in.9, ...), custom_call_target="tpu_custom_call" | custom-call | flops 1207959552 | bytes 18874368 | tf_op jit(solution)/shard_map/project_keep512_keep768/pallas_call | solution.py:214
  49.8 2.2 %collective-permute-start.7 = (f32[2,128,128]{2,1,0:T(8,128)S(1)}, f32[2,128,128]{2,1,0:T(8,128)S(1)}, u32[]{:S(2)}, u32[]{:S(2)}) collective-permute-start(f32[2,128,128]{2,1,0:T(8,128)S(1)} %get-tuple-element.68.refs_2_), channel_id=1, source_target_pairs={{0,4},{2,6},{4,0},{6,2},{8,12},{10,14},{12,8},{14,10},{1,5},{3,7},... | collective-permute-start | bytes 393224 | tf_op jit(solution)/shard_map/ppermute | solution.py:500
  52.0 2.6 %collective-permute-done.9.refs_1_ = f32[4,128,128]{2,1,0:T(8,128)S(1)} collective-permute-done((f32[4,128,128]{2,1,0:T(8,128)S(1)}, f32[4,128,128]{2,1,0:T(8,128)S(1)}, u32[]{:S(2)}, u32[]{:S(2)}) %collective-permute-start.9) | collective-permute-done | bytes 262176 | tf_op jit(solution)/shard_map/ppermute | solution.py:499
  54.6 1.9 %collective-permute-start.11 = (f32[2,128,128]{2,1,0:T(8,128)S(1)}, f32[2,128,128]{2,1,0:T(8,128)S(1)}, u32[]{:S(2)}, u32[]{:S(2)}) collective-permute-start(f32[2,128,128]{2,1,0:T(8,128)S(1)} %get-tuple-element.70.refs_2_), channel_id=1, source_target_pairs={{0,4},{2,6},{4,0},{6,2},{8,12},{10,14},{12,8},{14,10},{1,5},{3,7},... | collective-permute-start | bytes 393224 | tf_op jit(solution)/shard_map/ppermute | solution.py:500
  56.5 2.6 %collective-permute-start.14 = (f32[1,256,128]{2,1,0:T(8,128)S(1)}, f32[1,256,128]{2,1,0:T(8,128)S(1)}, u32[]{:S(2)}, u32[]{:S(2)}) collective-permute-start(f32[1,256,128]{2,1,0:T(8,128)S(1)} %get-tuple-element.71.refs_2_), channel_id=1, source_target_pairs={{0,8},{2,10},{4,12},{6,14},{8,0},{10,2},{12,4},{14,6},{1,9},{3,11}... | collective-permute-start | bytes 393224 | tf_op jit(solution)/shard_map/ppermute | solution.py:501
  60.5 2.9 %collective-permute-done.11.refs_1_ = f32[2,128,128]{2,1,0:T(8,128)S(1)} collective-permute-done((f32[2,128,128]{2,1,0:T(8,128)S(1)}, f32[2,128,128]{2,1,0:T(8,128)S(1)}, u32[]{:S(2)}, u32[]{:S(2)}) %collective-permute-start.11) | collective-permute-done | bytes 131104 | tf_op jit(solution)/shard_map/ppermute | solution.py:500
  63.4 2.9 %collective-permute-start.12 = (f32[1,128,128]{2,1,0:T(8,128)S(1)}, f32[1,128,128]{2,1,0:T(8,128)S(1)}, u32[]{:S(2)}, u32[]{:S(2)}) collective-permute-start(f32[1,128,128]{2,1,0:T(8,128)S(1)} %get-tuple-element.74.refs_2_), channel_id=1, source_target_pairs={{0,8},{2,10},{4,12},{6,14},{8,0},{10,2},{12,4},{14,6},{1,9},{3,11}... | collective-permute-start | bytes 196616 | tf_op jit(solution)/shard_map/ppermute | solution.py:501
  66.4 3.4 %gram_begin.1 = (f32[64,64]{1,0:T(8,128)S(1)}, f32[512,4096]{1,0:T(8,128)S(1)}) custom-call(s32[6]{0:T(128)} %train_count.13, s32[2]{0:T(128)} %test_count.13, f32[1,256,128]{2,1,0:T(8,128)S(1)} %get-tuple-element.77.rest_0_, f32[1,256,128]{2,1,0:T(8,128)S(1)} %get-tuple-element.78.rest_1_, f32[1,256,128]{2,1,0:T(8,128)S(1)} %get-tuple-element.79.rest_2_, ...), custom_call_target="tpu_custom_call" | custom-call | tf_op jit(solution)/shard_map/gram_begin/pallas_call | solution.py:323
  70.8 11.2 %all_to_all.35.own = f32[8,32,128]{2,1,0:T(8,128)S(1)} all-to-all(f32[8,32,128]{2,1,0:T(8,128)S(1)} %gram_end.1), channel_id=1, replica_groups={{4,0,6,8,2,10,12,14},{5,1,7,9,3,11,13,15},{20,16,22,24,18,26,28,30},{21..., dimensions={0} | all-to-all | bytes 262144 | tf_op jit(solution)/shard_map/all_to_all | solution.py:540
  85.1 8.4 %all_to_all.36.images = f32[8,8,128]{2,1,0:T(8,128)S(1)} all-to-all(f32[8,8,128]{2,1,0:T(8,128)S(1)} %get-tuple-element.82), channel_id=1, replica_groups={{4,0,6,8,2,10,12,14},{5,1,7,9,3,11,13,15},{20,16,22,24,18,26,28,30},{21..., dimensions={0} | all-to-all | bytes 65536 | tf_op jit(solution)/shard_map/all_to_all | solution.py:549
  95.4 8.3 %all_to_all.37.images = f32[8,8,128]{2,1,0:T(8,128)S(1)} all-to-all(f32[8,8,128]{2,1,0:T(8,128)S(1)} %get-tuple-element.85), channel_id=1, replica_groups={{4,0,6,8,2,10,12,14},{5,1,7,9,3,11,13,15},{20,16,22,24,18,26,28,30},{21..., dimensions={0} | all-to-all | bytes 65536 | tf_op jit(solution)/shard_map/all_to_all | solution.py:549
  105.5 8.3 %all_to_all.38.images = f32[8,8,128]{2,1,0:T(8,128)S(1)} all-to-all(f32[8,8,128]{2,1,0:T(8,128)S(1)} %get-tuple-element.89), channel_id=1, replica_groups={{4,0,6,8,2,10,12,14},{5,1,7,9,3,11,13,15},{20,16,22,24,18,26,28,30},{21..., dimensions={0} | all-to-all | bytes 65536 | tf_op jit(solution)/shard_map/all_to_all | solution.py:549
  115.7 8.3 %all_to_all.39.images = f32[8,8,128]{2,1,0:T(8,128)S(1)} all-to-all(f32[8,8,128]{2,1,0:T(8,128)S(1)} %get-tuple-element.93), channel_id=1, replica_groups={{4,0,6,8,2,10,12,14},{5,1,7,9,3,11,13,15},{20,16,22,24,18,26,28,30},{21..., dimensions={0} | all-to-all | bytes 65536 | tf_op jit(solution)/shard_map/all_to_all | solution.py:549
  125.8 8.3 %all_to_all.40.images = f32[8,8,128]{2,1,0:T(8,128)S(1)} all-to-all(f32[8,8,128]{2,1,0:T(8,128)S(1)} %get-tuple-element.97), channel_id=1, replica_groups={{4,0,6,8,2,10,12,14},{5,1,7,9,3,11,13,15},{20,16,22,24,18,26,28,30},{21..., dimensions={0} | all-to-all | bytes 65536 | tf_op jit(solution)/shard_map/all_to_all | solution.py:549
  134.1 1.9 %last_kernel.1 = (f32[3,8,128]{2,1,0:T(8,128)S(1)}, f32[8,8,128]{2,1,0:T(8,128)S(1)}, f32[2,12,8,128]{3,2,1,0:T(8,128)S(1)}) custom-call(f32[8,8,128]{2,1,0:T(8,128)S(1)} %all_to_all.40.images, f32[8,8,128]{2,1,0:T(8,128)S(1)} %get-tuple-element.98.solution, f32[8,8,128]{2,1,0:T(8,128)S(1)} %get-tuple-element.99.residue, ...), custom_call_target="tpu_custom_call" | custom-call | tf_op jit(solution)/shard_map/last_kernel/pallas_call | solution.py:459
  136.0 8.3 %all_to_all.41.curves = f32[8,8,128]{2,1,0:T(8,128)S(1)} all-to-all(f32[8,8,128]{2,1,0:T(8,128)S(1)} %get-tuple-element.101), channel_id=1, replica_groups={{4,0,6,8,2,10,12,14},{5,1,7,9,3,11,13,15},{20,16,22,24,18,26,28,30},{21..., dimensions={0} | all-to-all | bytes 65536 | tf_op jit(solution)/shard_map/all_to_all | solution.py:549
  (43 shorter events, 19.9 us)
Async XLA Ops:
  5.9 18.5 %collective-permute-start = (f32[4,256,128]{2,1,0:T(8,128)S(1)}, f32[4,256,128]{2,1,0:T(8,128)S(1)}, u32[]{:S(2)}, u32[]{:S(2)}) collective-permute-start(f32[4,256,128]{2,1,0:T(8,128)S(1)} %project_send0.1.rest_0_), channel_id=1, source_target_pairs={{0,2},{2,0},{4,6},{6,4},{8,10},{10,8},{12,14},{14,12},{1,3},{3,1},... | collective-permute-start | bytes 1572872 | tf_op jit(solution)/shard_map/ppermute | solution.py:499
  14.2 18.7 %collective-permute-start.2 = (f32[4,256,128]{2,1,0:T(8,128)S(1)}, f32[4,256,128]{2,1,0:T(8,128)S(1)}, u32[]{:S(2)}, u32[]{:S(2)}) collective-permute-start(f32[4,256,128]{2,1,0:T(8,128)S(1)} %project_send256.1.rest_0_), channel_id=1, source_target_pairs={{0,2},{2,0},{4,6},{6,4},{8,10},{10,8},{12,14},{14,12},{1,3},{3,1},... | collective-permute-start | bytes 1572872 | tf_op jit(solution)/shard_map/ppermute | solution.py:499
  22.3 25.6 %collective-permute-start.5 = (f32[4,256,128]{2,1,0:T(8,128)S(1)}, f32[4,256,128]{2,1,0:T(8,128)S(1)}, u32[]{:S(2)}, u32[]{:S(2)}) collective-permute-start(f32[4,256,128]{2,1,0:T(8,128)S(1)} %get-tuple-element.53.rest_0_), channel_id=1, source_target_pairs={{0,2},{2,0},{4,6},{6,4},{8,10},{10,8},{12,14},{14,12},{1,3},{3,1},... | collective-permute-start | bytes 1572872 | tf_op jit(solution)/shard_map/ppermute | solution.py:499
  24.4 10.7 %collective-permute-start.1 = (f32[2,256,128]{2,1,0:T(8,128)S(1)}, f32[2,256,128]{2,1,0:T(8,128)S(1)}, u32[]{:S(2)}, u32[]{:S(2)}) collective-permute-start(f32[2,256,128]{2,1,0:T(8,128)S(1)} %get-tuple-element.55.rest_1_), channel_id=1, source_target_pairs={{0,4},{2,6},{4,0},{6,2},{8,12},{10,14},{12,8},{14,10},{1,5},{3,7},... | collective-permute-start | bytes 786440 | tf_op jit(solution)/shard_map/ppermute | solution.py:500
  33.0 15.5 %collective-permute-start.4 = (f32[2,256,128]{2,1,0:T(8,128)S(1)}, f32[2,256,128]{2,1,0:T(8,128)S(1)}, u32[]{:S(2)}, u32[]{:S(2)}) collective-permute-start(f32[2,256,128]{2,1,0:T(8,128)S(1)} %get-tuple-element.59.refs_2_), channel_id=1, source_target_pairs={{0,4},{2,6},{4,0},{6,2},{8,12},{10,14},{12,8},{14,10},{1,5},{3,7},... | collective-permute-start | bytes 786440 | tf_op jit(solution)/shard_map/ppermute | solution.py:500
  35.2 12.7 %collective-permute-start.6 = (f32[1,256,128]{2,1,0:T(8,128)S(1)}, f32[1,256,128]{2,1,0:T(8,128)S(1)}, u32[]{:S(2)}, u32[]{:S(2)}) collective-permute-start(f32[1,256,128]{2,1,0:T(8,128)S(1)} %get-tuple-element.60.rest_1_), channel_id=1, source_target_pairs={{0,8},{2,10},{4,12},{6,14},{8,0},{10,2},{12,4},{14,6},{1,9},{3,11}... | collective-permute-start | bytes 393224 | tf_op jit(solution)/shard_map/ppermute | solution.py:501
  37.8 11.9 %collective-permute-start.3 = (f32[4,128,128]{2,1,0:T(8,128)S(1)}, f32[4,128,128]{2,1,0:T(8,128)S(1)}, u32[]{:S(2)}, u32[]{:S(2)}) collective-permute-start(f32[4,128,128]{2,1,0:T(8,128)S(1)} %get-tuple-element.62), channel_id=1, source_target_pairs={{0,2},{2,0},{4,6},{6,4},{8,10},{10,8},{12,14},{14,12},{1,3},{3,1},... | collective-permute-start | bytes 786440 | tf_op jit(solution)/shard_map/ppermute | solution.py:499
  39.3 15.2 %collective-permute-start.9 = (f32[4,128,128]{2,1,0:T(8,128)S(1)}, f32[4,128,128]{2,1,0:T(8,128)S(1)}, u32[]{:S(2)}, u32[]{:S(2)}) collective-permute-start(f32[4,128,128]{2,1,0:T(8,128)S(1)} %get-tuple-element.56.rest_0_), channel_id=1, source_target_pairs={{0,2},{2,0},{4,6},{6,4},{8,10},{10,8},{12,14},{14,12},{1,3},{3,1},... | collective-permute-start | bytes 786440 | tf_op jit(solution)/shard_map/ppermute | solution.py:499
  47.9 21.9 %copy-start = (s32[6]{0:T(128)S(1)}, s32[6]{0:T(128)}, u32[]{:S(2)}) copy-start(s32[6]{0:T(128)} %train_count.13) | copy-start | bytes 76
  47.9 21.9 %copy-start.1 = (s32[2]{0:T(128)S(1)}, s32[2]{0:T(128)}, u32[]{:S(2)}) copy-start(s32[2]{0:T(128)} %test_count.13) | copy-start | bytes 28
  48.0 8.5 %collective-permute-start.8 = (f32[2,256,128]{2,1,0:T(8,128)S(1)}, f32[2,256,128]{2,1,0:T(8,128)S(1)}, u32[]{:S(2)}, u32[]{:S(2)}) collective-permute-start(f32[2,256,128]{2,1,0:T(8,128)S(1)} %get-tuple-element.65.refs_2_), channel_id=1, source_target_pairs={{0,4},{2,6},{4,0},{6,2},{8,12},{10,14},{12,8},{14,10},{1,5},{3,7},... | collective-permute-start | bytes 786440 | tf_op jit(solution)/shard_map/ppermute | solution.py:500
  48.5 7.9 %collective-permute-start.10 = (f32[1,256,128]{2,1,0:T(8,128)S(1)}, f32[1,256,128]{2,1,0:T(8,128)S(1)}, u32[]{:S(2)}, u32[]{:S(2)}) collective-permute-start(f32[1,256,128]{2,1,0:T(8,128)S(1)} %get-tuple-element.66.refs_2_), channel_id=1, source_target_pairs={{0,8},{2,10},{4,12},{6,14},{8,0},{10,2},{12,4},{14,6},{1,9},{3,11}... | collective-permute-start | bytes 393224 | tf_op jit(solution)/shard_map/ppermute | solution.py:501
  49.8 10.7 %collective-permute-start.7 = (f32[2,128,128]{2,1,0:T(8,128)S(1)}, f32[2,128,128]{2,1,0:T(8,128)S(1)}, u32[]{:S(2)}, u32[]{:S(2)}) collective-permute-start(f32[2,128,128]{2,1,0:T(8,128)S(1)} %get-tuple-element.68.refs_2_), channel_id=1, source_target_pairs={{0,4},{2,6},{4,0},{6,2},{8,12},{10,14},{12,8},{14,10},{1,5},{3,7},... | collective-permute-start | bytes 393224 | tf_op jit(solution)/shard_map/ppermute | solution.py:500
  54.6 8.8 %collective-permute-start.11 = (f32[2,128,128]{2,1,0:T(8,128)S(1)}, f32[2,128,128]{2,1,0:T(8,128)S(1)}, u32[]{:S(2)}, u32[]{:S(2)}) collective-permute-start(f32[2,128,128]{2,1,0:T(8,128)S(1)} %get-tuple-element.70.refs_2_), channel_id=1, source_target_pairs={{0,4},{2,6},{4,0},{6,2},{8,12},{10,14},{12,8},{14,10},{1,5},{3,7},... | collective-permute-start | bytes 393224 | tf_op jit(solution)/shard_map/ppermute | solution.py:500
  56.5 9.8 %collective-permute-start.14 = (f32[1,256,128]{2,1,0:T(8,128)S(1)}, f32[1,256,128]{2,1,0:T(8,128)S(1)}, u32[]{:S(2)}, u32[]{:S(2)}) collective-permute-start(f32[1,256,128]{2,1,0:T(8,128)S(1)} %get-tuple-element.71.refs_2_), channel_id=1, source_target_pairs={{0,8},{2,10},{4,12},{6,14},{8,0},{10,2},{12,4},{14,6},{1,9},{3,11}... | collective-permute-start | bytes 393224 | tf_op jit(solution)/shard_map/ppermute | solution.py:501
  63.4 6.4 %collective-permute-start.13 = (f32[1,128,128]{2,1,0:T(8,128)S(1)}, f32[1,128,128]{2,1,0:T(8,128)S(1)}, u32[]{:S(2)}, u32[]{:S(2)}) collective-permute-start(f32[1,128,128]{2,1,0:T(8,128)S(1)} %get-tuple-element.76), channel_id=1, source_target_pairs={{0,8},{2,10},{4,12},{6,14},{8,0},{10,2},{12,4},{14,6},{1,9},{3,11}... | collective-permute-start | bytes 196616 | tf_op jit(solution)/shard_map/ppermute | solution.py:501
  63.4 6.3 %collective-permute-start.12 = (f32[1,128,128]{2,1,0:T(8,128)S(1)}, f32[1,128,128]{2,1,0:T(8,128)S(1)}, u32[]{:S(2)}, u32[]{:S(2)}) collective-permute-start(f32[1,128,128]{2,1,0:T(8,128)S(1)} %get-tuple-element.74.refs_2_), channel_id=1, source_target_pairs={{0,8},{2,10},{4,12},{6,14},{8,0},{10,2},{12,4},{14,6},{1,9},{3,11}... | collective-permute-start | bytes 196616 | tf_op jit(solution)/shard_map/ppermute | solution.py:501
  82.0 1.3 collective-permute-start.15

commit v5 on v4

--- a/solution.py
+++ b/solution.py
@@ -264,28 +264,32 @@
     )(*kept, *got, *after)
 
 
-def gram_kernel(first, pieces, length, final, train_count, test_count, *rest):
+def gram_kernel(first, pieces, length, final, *rest):
     ours, got = rest[:pieces], rest[pieces : 2 * pieces]
     rest = rest[2 * pieces :]
     if final:
-        before, out, held, of_train, of_test, sems = rest
+        before, limit, out, held = rest
+        count = limit[:1, :]
     else:
-        prior, out, near, of_train, of_test, sems, more = rest
+        train_count, test_count, prior, out, near, limit, of_train, of_test, sems, more = rest
         fetch = pltpu.make_async_copy(prior, near, more)
         fetch.start()
-    me = lax.axis_index("tensor")
-    train = train_count.shape[0]
-    lengths = (
-        pltpu.make_async_copy(train_count, of_train, sems.at[0]),
-        pltpu.make_async_copy(test_count, of_test, sems.at[1]),
-    )
-    for copy in lengths:
-        copy.start()
-    for copy in lengths:
-        copy.wait()
-    count = jnp.where(
-        me < train, of_train[jnp.minimum(me, train - 1)], of_test[jnp.maximum(me - train, 0)]
-    )
+        me = lax.axis_index("tensor")
+        train = train_count.shape[0]
+        lengths = (
+            pltpu.make_async_copy(train_count, of_train, sems.at[0]),
+            pltpu.make_async_copy(test_count, of_test, sems.at[1]),
+        )
+        for copy in lengths:
+            copy.start()
+        for copy in lengths:
+            copy.wait()
+        count = jnp.where(
+            me < train,
+            of_train[jnp.minimum(me, train - 1)],
+            of_test[jnp.maximum(me - train, 0)],
+        )
+        limit[...] = jnp.full(limit.shape, count, jnp.int32)
     total = before[...] if final else jnp.zeros((RANK, RANK), jnp.float32)
     for a, b in zip(ours, got):
         rows = a[0] + b[0]
@@ -309,26 +313,30 @@
         out[i] = grad
 
 
-def gram(first, length, counts, ours, got, prior=None, before=None):
+def gram(first, length, ours, got, counts=None, prior=None, before=None):
     final = before is not None
-    square = jax.ShapeDtypeStruct((RANK, RANK), jnp.float32)
-    scratch = [pltpu.SMEM(c.shape, jnp.int32) for c in counts] + [pltpu.SemaphoreType.DMA((2,))]
     if final:
+        others, other_specs = before, [VMEM, VMEM]
         out_shape = jax.ShapeDtypeStruct((8, RANK // 2, LANES), jnp.float32)
-        scratch = [pltpu.VMEM((RANK, RANK), jnp.float32)] + scratch
+        scratch = [pltpu.VMEM((RANK, RANK), jnp.float32)]
     else:
-        out_shape = [square, pltpu.VMEM(prior.shape, prior.dtype)]
-        counts, (prior,) = in_hbm(counts), in_hbm([prior])
-        scratch = scratch + [pltpu.SemaphoreType.DMA]
+        others, other_specs = in_hbm(counts + (prior,)), [ANY, ANY, ANY]
+        out_shape = [
+            jax.ShapeDtypeStruct((RANK, RANK), jnp.float32),
+            pltpu.VMEM(prior.shape, prior.dtype),
+            jax.ShapeDtypeStruct((8, LANES), jnp.int32),
+        ]
+        scratch = [pltpu.SMEM(c.shape, jnp.int32) for c in counts]
+        scratch += [pltpu.SemaphoreType.DMA((2,)), pltpu.SemaphoreType.DMA]
     return pl.pallas_call(
         functools.partial(gram_kernel, first, len(ours), length, final),
         out_shape=out_shape,
-        in_specs=[ANY, ANY] + [VMEM] * (2 * len(ours)) + [VMEM if final else ANY],
-        out_specs=VMEM if final else [VMEM, VMEM],
+        in_specs=[VMEM] * (2 * len(ours)) + other_specs,
+        out_specs=VMEM if final else [VMEM] * 3,
         scratch_shapes=scratch,
         compiler_params=pltpu.CompilerParams(vmem_limit_bytes=SMALL),
         name="gram_end" if final else "gram_begin",
-    )(*counts, *ours, *got, before if final else prior)
+    )(*ours, *got, *others)
 
 
 def pair_sums(x):
@@ -364,6 +372,8 @@
             line = jnp.sum(sums[j].T, axis=0, keepdims=True)
             image[pl.ds(j * 4 + block, 1), :] = line
 
+    if grads is None:
+        return
     total = grads.shape[0]
     low = weights[0] * grads[0, me]
     for i in range(1, total):
@@ -371,28 +381,23 @@
     image[...] = image[...] + low * (1.0 / total)
 
 
-def begin_kernel(own, other, prior, grads, search, payload, image):
-    me = lax.axis_index("dp")
-    per = grads.shape[0] // 2
-    for i in range(per):
-        at = ORDER.index(i)
-        for s in range(8):
-            for half in range(2):
-                there, here = pl.ds(half * 4, 4), pl.ds(s * 4, 4)
-                grads[me * per + i, s, there, :] = own[at, here, :]
-                grads[(1 - me) * per + i, s, there, :] = other[at, here, :]
+def begin_kernel(own, prior, search, payload, image):
+    first = own.shape[0] - 2
     for j in range(2):
         for s in range(8):
-            search[s, pl.ds(j * 4, 4), :] = own[ORDER.index(per + j), pl.ds(s * 4, 4), :]
-    fisher_rows(prior, grads, search, weights_of(grads, search[...]), image)
+            search[s, pl.ds(j * 4, 4), :] = own[ORDER.index(first + j), pl.ds(s * 4, 4), :]
+    fisher_rows(prior, None, search, None, image)
     for s in range(8):
         payload[s] = image[...]
 
 
-def advance(first, images, solution, residue, search, new_solution, new_residue, new_search):
+def in_order(images):
+    return jnp.stack([images[ORDER.index(s)] for s in range(8)])
+
+
+def advance(first, image, solution, residue, search, new_solution, new_residue, new_search):
     old = search[...]
     rest = old if first else residue[...]
-    image = jnp.stack([images[ORDER.index(s)] for s in range(8)])
     norm = inner(rest, rest)
     alpha = norm / inner(old, image)
     new_solution[...] = alpha * old if first else solution[...] + alpha * old
@@ -403,20 +408,36 @@
     return norm_next
 
 
+def first_kernel(
+    images, search, own, other, prior,
+    new_solution, new_residue, new_search, payload, grads, image,
+):
+    me = lax.axis_index("dp")
+    total = grads.shape[0]
+    per = total // 2
+    for i in range(per):
+        at = ORDER.index(i)
+        for s in range(8):
+            for half in range(2):
+                there, here = pl.ds(half * 4, 4), pl.ds(s * 4, 4)
+                grads[me * per + i, s, there, :] = own[at, here, :]
+                grads[(1 - me) * per + i, s, there, :] = other[at, here, :]
+    weights = weights_of(grads, search[...])
+    low = weights[0] * grads[0]
+    for i in range(1, total):
+        low = low + weights[i] * grads[i]
+    whole = in_order(images) + low * (1.0 / total)
+    advance(True, whole, None, None, search, new_solution, new_residue, new_search)
+    fisher_rows(prior, grads, new_search, weights_of(grads, new_search[...]), image)
+    for s in range(8):
+        payload[s] = image[...]
+
+
 def step_kernel(
     images, solution, residue, search, grads, prior,
     new_solution, new_residue, new_search, payload, image,
 ):
-    advance(False, images, solution, residue, search, new_solution, new_residue, new_search)
-    fisher_rows(prior, grads, new_search, weights_of(grads, new_search[...]), image)
-    for s in range(8):
-        payload[s] = image[...]
-
-
-def first_kernel(
-    images, search, grads, prior, new_solution, new_residue, new_search, payload, image
-):
-    advance(True, images, None, None, search, new_solution, new_residue, new_search)
+    advance(False, in_order(images), solution, residue, search, new_solution, new_residue, new_search)
     fisher_rows(prior, grads, new_search, weights_of(grads, new_search[...]), image)
     for s in range(8):
         payload[s] = image[...]
@@ -427,7 +448,7 @@
     own, payload, values, new_solution, new_residue, new_search, image,
 ):
     me = lax.axis_index("tensor")
-    norm = advance(False, images, solution, residue, search, new_solution, new_residue, new_search)
+    norm = advance(False, in_order(images), solution, residue, search, new_solution, new_residue, new_search)
     weights = weights_of(grads, new_search[...])
     fisher_rows(prior, grads, new_search, weights, image)
     curve = pair_sums(new_search[me] * image[...])
@@ -516,13 +537,12 @@
     half_b = next_to(theirs_b)
     send_a, last_a = halve(2, [(ours_a, 0, half_a)], (theirs_b,))
     whole_a = beyond(send_a)
-    kept2, kept3 = project_rows(
-        [(False, 512, (256,)), (False, 768, (256,))], operands, (sent4, send_a)
-    )
+    (kept2,) = project_rows([(False, 512, (256,))], operands, (sent4, send_a))
     theirs_c, ours_c = halve(1, [(kept2, 0, got2)], (whole_a,))
     half_c = next_to(theirs_c)
     send_b, last_b = halve(2, [(ours_b, 0, half_b)], (theirs_c,))
     whole_b = beyond(send_b)
+    (kept3,) = project_rows([(False, 768, (256,))], operands, (kept2, send_b))
     theirs_d, ours_d = halve(1, [(kept3, 0, got3)], (send_b,))
     half_d = next_to(theirs_d)
     theirs_e, ours_e = halve(1, [(kept3, 128, got4)], (theirs_d,))
@@ -533,22 +553,23 @@
     whole_d = beyond(send_d)
     send_e, last_e = halve(2, [(ours_e, 0, half_e)], (send_d,))
     whole_e = beyond(send_e)
-    square, prior = gram(
-        0, length, counts, (last_a, last_b, last_c), (whole_a, whole_b, whole_c), prior=fisher_prior
-    )
-    grad = gram(768, length, counts, (last_d, last_e), (whole_d, whole_e), before=square)
+    square, prior, limit = gram(
+        0, length, (last_a, last_b, last_c), (whole_a, whole_b, whole_c), counts, fisher_prior
+    )
+    grad = gram(768, length, (last_d, last_e), (whole_d, whole_e), before=(square, limit))
     own = lax.all_to_all(grad, "tensor", 0, 0, tiled=True, axis_index_groups=[ORDER])
     other = lax.ppermute(own, "dp", flipped(2, 1))
     per = train_inputs.shape[0]
     state = (8, 8, LANES)
     piece = (8, LANES)
     total = 2 * per
-    grads, search, payload = call(
-        begin_kernel, [(total, 8, 8, LANES), state, state], (own, other, prior), [piece]
-    )
+    search, payload = call(begin_kernel, [state, state], (own, prior), [piece])
     swap = lambda x: lax.all_to_all(x, "tensor", 0, 0, tiled=True, axis_index_groups=[ORDER])
-    solution, residue, search, payload = call(
-        first_kernel, [state] * 4, (swap(payload), search, grads, prior), [piece]
+    solution, residue, search, payload, grads = call(
+        first_kernel,
+        [state] * 4 + [(total,) + state],
+        (swap(payload), search, own, other, prior),
+        [piece],
     )
     for _ in range(ITERS - 3):
         solution, residue, search, payload = call(

time: 145 us -> 144 us (level)
  waiting for transfers between devices: 9.3 us -> 5.38 us
    ppermute x5, waiting for transfers between devices: 3.66 us -> 1.26 us  [per_device(): near = lambda x: lax.ppermute(x, 'tensor', flipped(n, 1))]
    ppermute x5, starting transfers between devices: 8.75 us -> 10.9 us  [per_device(): beyond = lambda x: lax.ppermute(x, 'tensor', flipped(n, 4))]
    pallas_call x5 -> x6, Pallas kernels: 33 us -> 34.7 us  [project_rows(): pl.pallas_call(functools.partial(project_kernel, parts, tile, len(after))...]
    ppermute x5, starting transfers between devices: 8.38 us -> 6.9 us  [per_device(): next_to = lambda x: lax.ppermute(x, 'tensor', flipped(n, 2))]
  transfers between devices with their start and end apart: 16 -> 16, of which waited for: 7 -> 3; matrix products, arithmetic and copies ran while one was open for 0% -> 0% of each run, Pallas kernels for 22% -> 24%
where the time goes in v5:
time: 144 us
  blocking collectives  61.6 us (43%)
  Pallas kernels  50.8 us (35%)
  starting transfers between devices  25 us (17%)
  waiting for transfers between devices  5.38 us (4%)
    all_to_all x6, blocking collectives, per_device(): lax.all_to_all(x, 'tensor', 0, 0, tiled=True, axis_index_groups=[ORDER])  49.8 us
    pallas_call x6, Pallas kernels, project_rows(): pl.pallas_call(functools.partial(project_kernel, parts, tile, len(after))...  34.7 us
    pallas_call x7, Pallas kernels, call(): pl.pallas_call(kernel, out_shape=[jax.ShapeDtypeStruct(s, jnp.float32) fo...  11.9 us
    all_to_all x1, blocking collectives, per_device(): lax.all_to_all(grad, 'tensor', 0, 0, tiled=True, axis_index_groups=[ORDER])  11.8 us
    ppermute x5, starting transfers between devices, per_device(): beyond = lambda x: lax.ppermute(x, 'tensor', flipped(n, 4))  10.9 us
    ppermute x5, starting transfers between devices, per_device(): near = lambda x: lax.ppermute(x, 'tensor', flipped(n, 1))  7.21 us
    ppermute x5, starting transfers between devices, per_device(): next_to = lambda x: lax.ppermute(x, 'tensor', flipped(n, 2))  6.9 us
    ppermute x5, waiting for transfers between devices, per_device(): next_to = lambda x: lax.ppermute(x, 'tensor', flipped(n, 2))  4.11 us
  transfers between devices with their start and end apart: 16, of which 3 were waited for; matrix products, arithmetic and copies ran while one was open for 0% of the time, Pallas kernels for 24%

profile of v5, /device:TPU:0, one launch (start us, length us, event | category | flops | bytes accessed | tf_op | source)
XLA Modules:
  0.0 143.6 jit_solution(10955231603267536745)
XLA Ops:
  0.6 5.2 %project_send0.1.rest_0_ = f32[4,256,128]{2,1,0:T(8,128)S(1)} custom-call(s32[6]{0:T(128)} %rest_6_.1, s32[2]{0:T(128)} %rest_7_.1, bf16[6,1024,3584]{2,1,0:T(8,128)(2,1)} %train_in.11, bf16[6,1024,1024]{2,1,0:T(8,128)(2,1)} %train_out.11, bf16[2,1024,3584]{2,1,0:T(8,128)(2,1)} %test_in.11, bf16[2,1024,1024]{2,1,0:T(8,128)(2,1)} %test_out.11, ...), custom_call_target="tpu_custom_call" | custom-call | flops 603979776 | bytes 9437184 | tf_op jit(solution)/shard_map/project_send0/pallas_call | solution.py:214
  5.9 3.0 %collective-permute-start = (f32[4,256,128]{2,1,0:T(8,128)S(1)}, f32[4,256,128]{2,1,0:T(8,128)S(1)}, u32[]{:S(2)}, u32[]{:S(2)}) collective-permute-start(f32[4,256,128]{2,1,0:T(8,128)S(1)} %project_send0.1.rest_0_), channel_id=1, source_target_pairs={{0,2},{2,0},{4,6},{6,4},{8,10},{10,8},{12,14},{14,12},{1,3},{3,1},... | collective-permute-start | bytes 1572872 | tf_op jit(solution)/shard_map/ppermute | solution.py:520
  8.9 5.3 %project_send256.1.rest_0_ = f32[4,256,128]{2,1,0:T(8,128)S(1)} custom-call(s32[6]{0:T(128)} %rest_6_.1, s32[2]{0:T(128)} %rest_7_.1, bf16[6,1024,3584]{2,1,0:T(8,128)(2,1)} %train_in.11, bf16[6,1024,1024]{2,1,0:T(8,128)(2,1)} %train_out.11, bf16[2,1024,3584]{2,1,0:T(8,128)(2,1)} %test_in.11, bf16[2,1024,1024]{2,1,0:T(8,128)(2,1)} %test_out.11, ...), custom_call_target="tpu_custom_call" | custom-call | flops 603979776 | bytes 9437184 | tf_op jit(solution)/shard_map/project_send256/pallas_call | solution.py:214
  14.3 8.0 %project_keep0_send512.1 = (f32[4,256,128]{2,1,0:T(8,128)S(1)}, f32[4,256,128]{2,1,0:T(8,128)S(1)}) custom-call(s32[6]{0:T(128)} %rest_6_.1, s32[2]{0:T(128)} %rest_7_.1, bf16[6,1024,3584]{2,1,0:T(8,128)(2,1)} %train_in.11, bf16[6,1024,1024]{2,1,0:T(8,128)(2,1)} %train_out.11, bf16[2,1024,3584]{2,1,0:T(8,128)(2,1)} %test_in.11, ...), custom_call_target="tpu_custom_call" | custom-call | flops 1207959552 | bytes 18874368 | tf_op jit(solution)/shard_map/project_keep0_send512/pallas_call | solution.py:214
  22.3 2.1 %collective-permute-start.4 = (f32[4,256,128]{2,1,0:T(8,128)S(1)}, f32[4,256,128]{2,1,0:T(8,128)S(1)}, u32[]{:S(2)}, u32[]{:S(2)}) collective-permute-start(f32[4,256,128]{2,1,0:T(8,128)S(1)} %get-tuple-element.52.rest_0_), channel_id=1, source_target_pairs={{0,2},{2,0},{4,6},{6,4},{8,10},{10,8},{12,14},{14,12},{1,3},{3,1},... | collective-permute-start | bytes 1572872 | tf_op jit(solution)/shard_map/ppermute | solution.py:520
  26.1 8.0 %project_keep256_send768.1 = (f32[4,256,128]{2,1,0:T(8,128)S(1)}, f32[4,128,128]{2,1,0:T(8,128)S(1)}, f32[4,128,128]{2,1,0:T(8,128)S(1)}) custom-call(s32[6]{0:T(128)} %rest_6_.1, s32[2]{0:T(128)} %rest_7_.1, bf16[6,1024,3584]{2,1,0:T(8,128)(2,1)} %train_in.11, bf16[6,1024,1024]{2,1,0:T(8,128)(2,1)} %train_out.11, bf16[2,1024,3584]{2,1,0:T(8,128)(2,1)} %test_in.11, ...), custom_call_target="tpu_custom_call" | custom-call | flops 1207959552 | bytes 18874368 | tf_op jit(solution)/shard_map/project_keep256_send768/pallas_call | solution.py:214
  35.2 2.6 %collective-permute-start.5 = (f32[1,256,128]{2,1,0:T(8,128)S(1)}, f32[1,256,128]{2,1,0:T(8,128)S(1)}, u32[]{:S(2)}, u32[]{:S(2)}) collective-permute-start(f32[1,256,128]{2,1,0:T(8,128)S(1)} %get-tuple-element.59.rest_1_), channel_id=1, source_target_pairs={{0,8},{2,10},{4,12},{6,14},{8,0},{10,2},{12,4},{14,6},{1,9},{3,11}... | collective-permute-start | bytes 393224 | tf_op jit(solution)/shard_map/ppermute | solution.py:522
  39.8 4.5 %project_keep512.1.refs_0_.rest_0_ = f32[4,256,128]{2,1,0:T(8,128)S(1)} custom-call(s32[6]{0:T(128)} %rest_6_.1, s32[2]{0:T(128)} %rest_7_.1, bf16[6,1024,3584]{2,1,0:T(8,128)(2,1)} %train_in.11, bf16[6,1024,1024]{2,1,0:T(8,128)(2,1)} %train_out.11, bf16[2,1024,3584]{2,1,0:T(8,128)(2,1)} %test_in.11, bf16[2,1024,1024]{2,1,0:T(8,128)(2,1)} %test_out.11, ...), custom_call_target="tpu_custom_call" | custom-call | flops 603979776 | bytes 9437184 | tf_op jit(solution)/shard_map/project_keep512/pallas_call | solution.py:214
  44.4 2.0 %collective-permute-start.8 = (f32[2,256,128]{2,1,0:T(8,128)S(1)}, f32[2,256,128]{2,1,0:T(8,128)S(1)}, u32[]{:S(2)}, u32[]{:S(2)}) collective-permute-start(f32[2,256,128]{2,1,0:T(8,128)S(1)} %get-tuple-element.61.refs_2_), channel_id=1, source_target_pairs={{0,4},{2,6},{4,0},{6,2},{8,12},{10,14},{12,8},{14,10},{1,5},{3,7},... | collective-permute-start | bytes 786440 | tf_op jit(solution)/shard_map/ppermute | solution.py:521
  46.4 2.6 %collective-permute-start.10 = (f32[1,256,128]{2,1,0:T(8,128)S(1)}, f32[1,256,128]{2,1,0:T(8,128)S(1)}, u32[]{:S(2)}, u32[]{:S(2)}) collective-permute-start(f32[1,256,128]{2,1,0:T(8,128)S(1)} %get-tuple-element.62.rest_1_.refs_2_), channel_id=1, source_target_pairs={{0,8},{2,10},{4,12},{6,14},{8,0},{10,2},{12,4},{14,6},{1,9},{3,11}... | collective-permute-start | bytes 393224 | tf_op jit(solution)/shard_map/ppermute | solution.py:522
  49.1 3.6 %project_keep768.1.refs_0_ = f32[4,256,128]{2,1,0:T(8,128)S(1)} custom-call(s32[6]{0:T(128)} %rest_6_.1, s32[2]{0:T(128)} %rest_7_.1, bf16[6,1024,3584]{2,1,0:T(8,128)(2,1)} %train_in.11, bf16[6,1024,1024]{2,1,0:T(8,128)(2,1)} %train_out.11, bf16[2,1024,3584]{2,1,0:T(8,128)(2,1)} %test_in.11, bf16[2,1024,1024]{2,1,0:T(8,128)(2,1)} %test_out.11, ...), custom_call_target="tpu_custom_call" | custom-call | flops 603979776 | bytes 9437184 | tf_op jit(solution)/shard_map/project_keep768/pallas_call | solution.py:214
  56.5 2.7 %collective-permute-start.14 = (f32[1,256,128]{2,1,0:T(8,128)S(1)}, f32[1,256,128]{2,1,0:T(8,128)S(1)}, u32[]{:S(2)}, u32[]{:S(2)}) collective-permute-start(f32[1,256,128]{2,1,0:T(8,128)S(1)} %get-tuple-element.68.refs_2_), channel_id=1, source_target_pairs={{0,8},{2,10},{4,12},{6,14},{8,0},{10,2},{12,4},{14,6},{1,9},{3,11}... | collective-permute-start | bytes 393224 | tf_op jit(solution)/shard_map/ppermute | solution.py:522
  60.4 2.9 %collective-permute-done.11.refs_1_ = f32[2,128,128]{2,1,0:T(8,128)S(1)} collective-permute-done((f32[2,128,128]{2,1,0:T(8,128)S(1)}, f32[2,128,128]{2,1,0:T(8,128)S(1)}, u32[]{:S(2)}, u32[]{:S(2)}) %collective-permute-start.11) | collective-permute-done | bytes 131104 | tf_op jit(solution)/shard_map/ppermute | solution.py:521
  63.3 2.9 %collective-permute-start.12 = (f32[1,128,128]{2,1,0:T(8,128)S(1)}, f32[1,128,128]{2,1,0:T(8,128)S(1)}, u32[]{:S(2)}, u32[]{:S(2)}) collective-permute-start(f32[1,128,128]{2,1,0:T(8,128)S(1)} %get-tuple-element.71.refs_2_), channel_id=1, source_target_pairs={{0,8},{2,10},{4,12},{6,14},{8,0},{10,2},{12,4},{14,6},{1,9},{3,11}... | collective-permute-start | bytes 196616 | tf_op jit(solution)/shard_map/ppermute | solution.py:522
  66.3 3.4 %gram_begin.1 = (f32[64,64]{1,0:T(8,128)S(1)}, f32[512,4096]{1,0:T(8,128)S(1)}, s32[8,128]{1,0:T(8,128)S(1)}) custom-call(f32[1,256,128]{2,1,0:T(8,128)S(1)} %get-tuple-element.74.rest_0_, f32[1,256,128]{2,1,0:T(8,128)S(1)} %get-tuple-element.75.rest_1_, f32[1,256,128]{2,1,0:T(8,128)S(1)} %get-tuple-element.76.rest_2_, ...), custom_call_target="tpu_custom_call" | custom-call | tf_op jit(solution)/shard_map/gram_begin/pallas_call | solution.py:331
  70.1 11.8 %all_to_all.35.own = f32[8,32,128]{2,1,0:T(8,128)S(1)} all-to-all(f32[8,32,128]{2,1,0:T(8,128)S(1)} %gram_end.1), channel_id=1, replica_groups={{4,0,6,8,2,10,12,14},{5,1,7,9,3,11,13,15},{20,16,22,24,18,26,28,30},{21..., dimensions={0} | all-to-all | bytes 262144 | tf_op jit(solution)/shard_map/all_to_all | solution.py:560
  83.5 8.4 %all_to_all.36.images = f32[8,8,128]{2,1,0:T(8,128)S(1)} all-to-all(f32[8,8,128]{2,1,0:T(8,128)S(1)} %get-tuple-element.80), channel_id=1, replica_groups={{4,0,6,8,2,10,12,14},{5,1,7,9,3,11,13,15},{20,16,22,24,18,26,28,30},{21..., dimensions={0} | all-to-all | bytes 65536 | tf_op jit(solution)/shard_map/all_to_all | solution.py:567
  91.9 2.1 %first_kernel.1 = (f32[8,8,128]{2,1,0:T(8,128)S(1)}, f32[8,8,128]{2,1,0:T(8,128)S(1)}, f32[8,8,128]{2,1,0:T(8,128)S(1)}, f32[8,8,128]{2,1,0:T(8,128)S(1)}, f32[12,8,8,128]{3,2,1,0:T(8,128)S(1)}) custom-call(f32[8,8,128]{2,1,0:T(8,128)S(1)} %all_to_all.36.images, f32[8,8,128]{2,1,0:T(8,128)S(1)} %get-tuple-element.81.search, ...), custom_call_target="tpu_custom_call" | custom-call | tf_op jit(solution)/shard_map/first_kernel/pallas_call | solution.py:480
  94.0 8.3 %all_to_all.37.images = f32[8,8,128]{2,1,0:T(8,128)S(1)} all-to-all(f32[8,8,128]{2,1,0:T(8,128)S(1)} %get-tuple-element.82), channel_id=1, replica_groups={{4,0,6,8,2,10,12,14},{5,1,7,9,3,11,13,15},{20,16,22,24,18,26,28,30},{21..., dimensions={0} | all-to-all | bytes 65536 | tf_op jit(solution)/shard_map/all_to_all | solution.py:567
  104.1 8.3 %all_to_all.38.images = f32[8,8,128]{2,1,0:T(8,128)S(1)} all-to-all(f32[8,8,128]{2,1,0:T(8,128)S(1)} %get-tuple-element.87), channel_id=1, replica_groups={{4,0,6,8,2,10,12,14},{5,1,7,9,3,11,13,15},{20,16,22,24,18,26,28,30},{21..., dimensions={0} | all-to-all | bytes 65536 | tf_op jit(solution)/shard_map/all_to_all | solution.py:567
  114.2 8.3 %all_to_all.39.images = f32[8,8,128]{2,1,0:T(8,128)S(1)} all-to-all(f32[8,8,128]{2,1,0:T(8,128)S(1)} %get-tuple-element.91), channel_id=1, replica_groups={{4,0,6,8,2,10,12,14},{5,1,7,9,3,11,13,15},{20,16,22,24,18,26,28,30},{21..., dimensions={0} | all-to-all | bytes 65536 | tf_op jit(solution)/shard_map/all_to_all | solution.py:567
  122.5 2.0 %step_kernel.5 = (f32[8,8,128]{2,1,0:T(8,128)S(1)}, f32[8,8,128]{2,1,0:T(8,128)S(1)}, f32[8,8,128]{2,1,0:T(8,128)S(1)}, f32[8,8,128]{2,1,0:T(8,128)S(1)}) custom-call(f32[8,8,128]{2,1,0:T(8,128)S(1)} %all_to_all.39.images, f32[8,8,128]{2,1,0:T(8,128)S(1)} %get-tuple-element.92.solution, f32[8,8,128]{2,1,0:T(8,128)S(1)} %get-tuple-element.93.residue, ...), custom_call_target="tpu_custom_call" | custom-call | tf_op jit(solution)/shard_map/step_kernel/pallas_call | solution.py:480
  124.5 8.3 %all_to_all.40.images = f32[8,8,128]{2,1,0:T(8,128)S(1)} all-to-all(f32[8,8,128]{2,1,0:T(8,128)S(1)} %get-tuple-element.95), channel_id=1, replica_groups={{4,0,6,8,2,10,12,14},{5,1,7,9,3,11,13,15},{20,16,22,24,18,26,28,30},{21..., dimensions={0} | all-to-all | bytes 65536 | tf_op jit(solution)/shard_map/all_to_all | solution.py:567
  134.7 8.3 %all_to_all.41.curves = f32[8,8,128]{2,1,0:T(8,128)S(1)} all-to-all(f32[8,8,128]{2,1,0:T(8,128)S(1)} %get-tuple-element.99), channel_id=1, replica_groups={{4,0,6,8,2,10,12,14},{5,1,7,9,3,11,13,15},{20,16,22,24,18,26,28,30},{21..., dimensions={0} | all-to-all | bytes 65536 | tf_op jit(solution)/shard_map/all_to_all | solution.py:567
  (40 shorter events, 18.2 us)
Async XLA Ops:
  5.9 18.5 %collective-permute-start = (f32[4,256,128]{2,1,0:T(8,128)S(1)}, f32[4,256,128]{2,1,0:T(8,128)S(1)}, u32[]{:S(2)}, u32[]{:S(2)}) collective-permute-start(f32[4,256,128]{2,1,0:T(8,128)S(1)} %project_send0.1.rest_0_), channel_id=1, source_target_pairs={{0,2},{2,0},{4,6},{6,4},{8,10},{10,8},{12,14},{14,12},{1,3},{3,1},... | collective-permute-start | bytes 1572872 | tf_op jit(solution)/shard_map/ppermute | solution.py:520
  14.2 20.0 %collective-permute-start.2 = (f32[4,256,128]{2,1,0:T(8,128)S(1)}, f32[4,256,128]{2,1,0:T(8,128)S(1)}, u32[]{:S(2)}, u32[]{:S(2)}) collective-permute-start(f32[4,256,128]{2,1,0:T(8,128)S(1)} %project_send256.1.rest_0_), channel_id=1, source_target_pairs={{0,2},{2,0},{4,6},{6,4},{8,10},{10,8},{12,14},{14,12},{1,3},{3,1},... | collective-permute-start | bytes 1572872 | tf_op jit(solution)/shard_map/ppermute | solution.py:520
  22.3 22.0 %collective-permute-start.4 = (f32[4,256,128]{2,1,0:T(8,128)S(1)}, f32[4,256,128]{2,1,0:T(8,128)S(1)}, u32[]{:S(2)}, u32[]{:S(2)}) collective-permute-start(f32[4,256,128]{2,1,0:T(8,128)S(1)} %get-tuple-element.52.rest_0_), channel_id=1, source_target_pairs={{0,2},{2,0},{4,6},{6,4},{8,10},{10,8},{12,14},{14,12},{1,3},{3,1},... | collective-permute-start | bytes 1572872 | tf_op jit(solution)/shard_map/ppermute | solution.py:520
  24.4 10.7 %collective-permute-start.1 = (f32[2,256,128]{2,1,0:T(8,128)S(1)}, f32[2,256,128]{2,1,0:T(8,128)S(1)}, u32[]{:S(2)}, u32[]{:S(2)}) collective-permute-start(f32[2,256,128]{2,1,0:T(8,128)S(1)} %get-tuple-element.54.rest_1_), channel_id=1, source_target_pairs={{0,4},{2,6},{4,0},{6,2},{8,12},{10,14},{12,8},{14,10},{1,5},{3,7},... | collective-permute-start | bytes 786440 | tf_op jit(solution)/shard_map/ppermute | solution.py:521
  34.2 12.2 %collective-permute-start.3 = (f32[2,256,128]{2,1,0:T(8,128)S(1)}, f32[2,256,128]{2,1,0:T(8,128)S(1)}, u32[]{:S(2)}, u32[]{:S(2)}) collective-permute-start(f32[2,256,128]{2,1,0:T(8,128)S(1)} %get-tuple-element.58.refs_2_), channel_id=1, source_target_pairs={{0,4},{2,6},{4,0},{6,2},{8,12},{10,14},{12,8},{14,10},{1,5},{3,7},... | collective-permute-start | bytes 786440 | tf_op jit(solution)/shard_map/ppermute | solution.py:521
  35.2 9.2 %collective-permute-start.5 = (f32[1,256,128]{2,1,0:T(8,128)S(1)}, f32[1,256,128]{2,1,0:T(8,128)S(1)}, u32[]{:S(2)}, u32[]{:S(2)}) collective-permute-start(f32[1,256,128]{2,1,0:T(8,128)S(1)} %get-tuple-element.59.rest_1_), channel_id=1, source_target_pairs={{0,8},{2,10},{4,12},{6,14},{8,0},{10,2},{12,4},{14,6},{1,9},{3,11}... | collective-permute-start | bytes 393224 | tf_op jit(solution)/shard_map/ppermute | solution.py:522
  37.8 14.9 %collective-permute-start.6 = (f32[4,128,128]{2,1,0:T(8,128)S(1)}, f32[4,128,128]{2,1,0:T(8,128)S(1)}, u32[]{:S(2)}, u32[]{:S(2)}) collective-permute-start(f32[4,128,128]{2,1,0:T(8,128)S(1)} %get-tuple-element.63), channel_id=1, source_target_pairs={{0,2},{2,0},{4,6},{6,4},{8,10},{10,8},{12,14},{14,12},{1,3},{3,1},... | collective-permute-start | bytes 786440 | tf_op jit(solution)/shard_map/ppermute | solution.py:520
  39.3 15.2 %collective-permute-start.9 = (f32[4,128,128]{2,1,0:T(8,128)S(1)}, f32[4,128,128]{2,1,0:T(8,128)S(1)}, u32[]{:S(2)}, u32[]{:S(2)}) collective-permute-start(f32[4,128,128]{2,1,0:T(8,128)S(1)} %get-tuple-element.55.rest_0_), channel_id=1, source_target_pairs={{0,2},{2,0},{4,6},{6,4},{8,10},{10,8},{12,14},{14,12},{1,3},{3,1},... | collective-permute-start | bytes 786440 | tf_op jit(solution)/shard_map/ppermute | solution.py:520
  44.4 12.0 %collective-permute-start.8 = (f32[2,256,128]{2,1,0:T(8,128)S(1)}, f32[2,256,128]{2,1,0:T(8,128)S(1)}, u32[]{:S(2)}, u32[]{:S(2)}) collective-permute-start(f32[2,256,128]{2,1,0:T(8,128)S(1)} %get-tuple-element.61.refs_2_), channel_id=1, source_target_pairs={{0,4},{2,6},{4,0},{6,2},{8,12},{10,14},{12,8},{14,10},{1,5},{3,7},... | collective-permute-start | bytes 786440 | tf_op jit(solution)/shard_map/ppermute | solution.py:521
  46.4 10.0 %collective-permute-start.10 = (f32[1,256,128]{2,1,0:T(8,128)S(1)}, f32[1,256,128]{2,1,0:T(8,128)S(1)}, u32[]{:S(2)}, u32[]{:S(2)}) collective-permute-start(f32[1,256,128]{2,1,0:T(8,128)S(1)} %get-tuple-element.62.rest_1_.refs_2_), channel_id=1, source_target_pairs={{0,8},{2,10},{4,12},{6,14},{8,0},{10,2},{12,4},{14,6},{1,9},{3,11}... | collective-permute-start | bytes 393224 | tf_op jit(solution)/shard_map/ppermute | solution.py:522
  52.8 7.6 %collective-permute-start.7 = (f32[2,128,128]{2,1,0:T(8,128)S(1)}, f32[2,128,128]{2,1,0:T(8,128)S(1)}, u32[]{:S(2)}, u32[]{:S(2)}) collective-permute-start(f32[2,128,128]{2,1,0:T(8,128)S(1)} %get-tuple-element.65.refs_2_), channel_id=1, source_target_pairs={{0,4},{2,6},{4,0},{6,2},{8,12},{10,14},{12,8},{14,10},{1,5},{3,7},... | collective-permute-start | bytes 393224 | tf_op jit(solution)/shard_map/ppermute | solution.py:521
  54.6 8.7 %collective-permute-start.11 = (f32[2,128,128]{2,1,0:T(8,128)S(1)}, f32[2,128,128]{2,1,0:T(8,128)S(1)}, u32[]{:S(2)}, u32[]{:S(2)}) collective-permute-start(f32[2,128,128]{2,1,0:T(8,128)S(1)} %get-tuple-element.67.refs_2_), channel_id=1, source_target_pairs={{0,4},{2,6},{4,0},{6,2},{8,12},{10,14},{12,8},{14,10},{1,5},{3,7},... | collective-permute-start | bytes 393224 | tf_op jit(solution)/shard_map/ppermute | solution.py:521
  56.5 9.8 %collective-permute-start.14 = (f32[1,256,128]{2,1,0:T(8,128)S(1)}, f32[1,256,128]{2,1,0:T(8,128)S(1)}, u32[]{:S(2)}, u32[]{:S(2)}) collective-permute-start(f32[1,256,128]{2,1,0:T(8,128)S(1)} %get-tuple-element.68.refs_2_), channel_id=1, source_target_pairs={{0,8},{2,10},{4,12},{6,14},{8,0},{10,2},{12,4},{14,6},{1,9},{3,11}... | collective-permute-start | bytes 393224 | tf_op jit(solution)/shard_map/ppermute | solution.py:522
  63.3 6.4 %collective-permute-start.13 = (f32[1,128,128]{2,1,0:T(8,128)S(1)}, f32[1,128,128]{2,1,0:T(8,128)S(1)}, u32[]{:S(2)}, u32[]{:S(2)}) collective-permute-start(f32[1,128,128]{2,1,0:T(8,128)S(1)} %get-tuple-element.73), channel_id=1, source_target_pairs={{0,8},{2,10},{4,12},{6,14},{8,0},{10,2},{12,4},{14,6},{1,9},{3,11}... | collective-permute-start | bytes 196616 | tf_op jit(solution)/shard_map/ppermute | solution.py:522
  63.3 6.3 %collective-permute-start.12 = (f32[1,128,128]{2,1,0:T(8,128)S(1)}, f32[1,128,128]{2,1,0:T(8,128)S(1)}, u32[]{:S(2)}, u32[]{:S(2)}) collective-permute-start(f32[1,128,128]{2,1,0:T(8,128)S(1)} %get-tuple-element.71.refs_2_), channel_id=1, source_target_pairs={{0,8},{2,10},{4,12},{6,14},{8,0},{10,2},{12,4},{14,6},{1,9},{3,11}... | collective-permute-start | bytes 196616 | tf_op jit(solution)/shard_map/ppermute | solution.py:522
  81.9 10.0 %collective-permute-start.15 = (f32[8,32,128]{2,1,0:T(8,128)S(1)}, f32[8,32,128]{2,1,0:T(8,128)S(1)}, u32[]{:S(2)}, u32[]{:S(2)}) collective-permute-start(f32[8,32,128]{2,1,0:T(8,128)S(1)} %all_to_all.35.own), channel_id=1, source_target_pairs={{0,1},{1,0},{2,3},{3,2},{4,5},{5,4},{6,7},{7,6},{8,9},{9,8},{10,11... | collective-permute-start | bytes 393224 | tf_op jit(solution)/shard_map/ppermute | solution.py:561

commit v6 on v5

--- a/solution.py
+++ b/solution.py
@@ -12,7 +12,7 @@
 ITERS = 6
 LANES = 128
 FLOOR = 256
-SLOTS = 4
+SLOTS = 3
 SMALL = 24 * 2**20
 
 HIGH = lax.Precision.HIGHEST
@@ -86,11 +86,15 @@
     basis_in, basis_out, *rest,
 ):
     outs = rest[after : after + sum(len(part[2]) for part in parts)]
-    held_in, held_out, near_in, near_out, of_train, of_test, sems, more = rest[after + len(outs) :]
+    held, basis, of_train, of_test, sems, more = rest[after + len(outs) :]
+    width, depth = basis_in.shape[1], basis.shape[1]
+    front, back = pl.ds(0, width), pl.ds(width, depth - width)
+    upper, lower = pl.ds(0, RANK), pl.ds(RANK, RANK)
     me = lax.rem(lax.axis_index("tensor"), 2)
     last = train_in.shape[0] // 2
     total = 4 * len(parts)
-    dynamic = any(first >= FLOOR for _, first, _ in parts)
+    always = [first <= FLOOR for _, first, _ in parts]
+    dynamic = not all(always)
 
     def pick(part, values):
         value = jnp.int32(values[0])
@@ -108,7 +112,8 @@
             return jnp.bool_(True)
         i, row, low = place(k)
         train = of_train[jnp.minimum(2 * i + low, 2 * last - 1)]
-        return (jnp.where(i < last, train, of_test[low]) > row) | (k == 0)
+        kept = (pick(k // 4, [int(flag) for flag in always]) == 1) | (k == 0)
+        return (jnp.where(i < last, train, of_test[low]) > row) | kept
 
     def copies(k, train):
         i, row, low = place(k)
@@ -116,12 +121,12 @@
         rows = pl.ds(row, tile)
         wide, narrow, e = (train_in, train_out, 2 * i + low) if train else (test_in, test_out, low)
         return (
-            pltpu.make_async_copy(wide.at[e, rows], held_in.at[slot], sems.at[slot, 0]),
-            pltpu.make_async_copy(narrow.at[e, rows], held_out.at[slot], sems.at[slot, 1]),
+            pltpu.make_async_copy(wide.at[e, rows], held.at[slot, :, front], sems.at[slot, 0]),
+            pltpu.make_async_copy(narrow.at[e, rows], held.at[slot, :, back], sems.at[slot, 1]),
         )
 
-    def start(k):
-        mine = (k < total) & live(k)
+    def start(k, sure=False):
+        mine = k < total if sure else (k < total) & live(k)
         i = lax.rem(k, 4)
 
         @pl.when(mine & (i < last))
@@ -135,8 +140,8 @@
                 copy.start()
 
     bases = (
-        pltpu.make_async_copy(basis_in, near_in, more.at[0]),
-        pltpu.make_async_copy(basis_out, near_out, more.at[1]),
+        pltpu.make_async_copy(basis_in, basis.at[lower, front], more.at[0]),
+        pltpu.make_async_copy(basis_out, basis.at[upper, back], more.at[1]),
     )
     if dynamic:
         lengths = (
@@ -147,14 +152,19 @@
             copy.start()
     for copy in copies(jnp.int32(0), True) + bases:
         copy.start()
-    if dynamic:
+    basis[upper, front] = jnp.zeros((RANK, width), basis.dtype)
+    basis[lower, back] = jnp.zeros((RANK, depth - width), basis.dtype)
+    if dynamic and not always[0]:
         for copy in lengths:
             copy.wait()
 
     @pl.loop(1, SLOTS - 1)
     def _(k):
-        start(k)
-
+        start(k, always[0])
+
+    if dynamic and always[0]:
+        for copy in lengths:
+            copy.wait()
     for copy in bases:
         copy.wait()
 
@@ -180,14 +190,12 @@
         def make():
             for copy in copies(k, False):
                 copy.wait()
-            dims = (((1,), (1,)), ((), ()))
-            left = lax.dot_general(
-                held_out[slot], near_out[...], dims, preferred_element_type=jnp.float32
+            keep(
+                lax.dot_general(
+                    held[slot], basis[...], (((1,), (1,)), ((), ())),
+                    preferred_element_type=jnp.float32,
+                )
             )
-            right = lax.dot_general(
-                held_in[slot], near_in[...], dims, preferred_element_type=jnp.float32
-            )
-            keep(jnp.concatenate([left, right], axis=1))
 
         if dynamic:
             alive = live(k)
@@ -217,10 +225,8 @@
         in_specs=[ANY] * (len(operands) + len(after)),
         out_specs=[VMEM] * len(sizes),
         scratch_shapes=[
-            pltpu.VMEM((SLOTS, tile, wide.shape[2]), wide.dtype),
-            pltpu.VMEM((SLOTS, tile, narrow.shape[2]), narrow.dtype),
-            pltpu.VMEM(basis_in.shape, basis_in.dtype),
-            pltpu.VMEM(basis_out.shape, basis_out.dtype),
+            pltpu.VMEM((SLOTS, tile, depth), wide.dtype),
+            pltpu.VMEM((2 * RANK, depth), basis_in.dtype),
             pltpu.SMEM(operands[0].shape, jnp.int32),
             pltpu.SMEM(operands[1].shape, jnp.int32),
             pltpu.SemaphoreType.DMA((SLOTS, 2)),
@@ -360,7 +366,7 @@
 def fisher_rows(prior, grads, vector, weights, image):
     me = lax.axis_index("tensor")
 
-    @pl.loop(0, prior.shape[0] // LANES)
+    @pl.loop(0, prior.shape[0] // LANES, unroll=2)
     def _(block):
         rows = pl.ds(pl.multiple_of(block * LANES, LANES), LANES)
         sums = [jnp.zeros((LANES, LANES), jnp.float32)] * 2

time: 144 us -> 143 us (level)
  waiting for transfers between devices: 5.38 us -> 7.12 us
  blocking collectives: 61.6 us -> 59.9 us
    ppermute x5, starting transfers between devices: 6.9 us -> 8.76 us  [per_device(): next_to = lambda x: lax.ppermute(x, 'tensor', flipped(n, 2))]
    all_to_all x1, blocking collectives: 11.8 us -> 10.1 us  [per_device(): lax.all_to_all(grad, 'tensor', 0, 0, tiled=True, axis_index_groups=[ORDER])]
    ppermute x5, waiting for transfers between devices: 0.01 us -> 1.6 us  [per_device(): beyond = lambda x: lax.ppermute(x, 'tensor', flipped(n, 4))]
  transfers between devices with their start and end apart: 16 -> 16, of which waited for: 3 -> 6; matrix products, arithmetic and copies ran while one was open for 0% -> 0% of each run, Pallas kernels for 24% -> 24%
where the time goes in v6:
time: 143 us
  blocking collectives  59.9 us (42%)
  Pallas kernels  49.5 us (35%)
  starting transfers between devices  25.9 us (18%)
  waiting for transfers between devices  7.12 us (5%)
    all_to_all x6, blocking collectives, per_device(): lax.all_to_all(x, 'tensor', 0, 0, tiled=True, axis_index_groups=[ORDER])  49.8 us
    pallas_call x6, Pallas kernels, project_rows(): pl.pallas_call(functools.partial(project_kernel, parts, tile, len(after))...  34.7 us
    pallas_call x7, Pallas kernels, call(): pl.pallas_call(kernel, out_shape=[jax.ShapeDtypeStruct(s, jnp.float32) fo...  10.6 us
    all_to_all x1, blocking collectives, per_device(): lax.all_to_all(grad, 'tensor', 0, 0, tiled=True, axis_index_groups=[ORDER])  10.1 us
    ppermute x5, starting transfers between devices, per_device(): beyond = lambda x: lax.ppermute(x, 'tensor', flipped(n, 4))  9.87 us
    ppermute x5, starting transfers between devices, per_device(): next_to = lambda x: lax.ppermute(x, 'tensor', flipped(n, 2))  8.76 us
    ppermute x5, starting transfers between devices, per_device(): near = lambda x: lax.ppermute(x, 'tensor', flipped(n, 1))  7.21 us
    ppermute x5, waiting for transfers between devices, per_device(): next_to = lambda x: lax.ppermute(x, 'tensor', flipped(n, 2))  4.69 us
  transfers between devices with their start and end apart: 16, of which 6 were waited for; matrix products, arithmetic and copies ran while one was open for 0% of the time, Pallas kernels for 24%

profile of v6, /device:TPU:0, one launch (start us, length us, event | category | flops | bytes accessed | tf_op | source)
XLA Modules:
  0.0 143.2 jit_solution(6857696373002927163)
XLA Ops:
  0.6 5.2 %project_send0.1.rest_0_ = f32[4,256,128]{2,1,0:T(8,128)S(1)} custom-call(s32[6]{0:T(128)} %rest_6_.1, s32[2]{0:T(128)} %rest_7_.1, bf16[6,1024,3584]{2,1,0:T(8,128)(2,1)} %train_in.11, bf16[6,1024,1024]{2,1,0:T(8,128)(2,1)} %train_out.11, bf16[2,1024,3584]{2,1,0:T(8,128)(2,1)} %test_in.11, bf16[2,1024,1024]{2,1,0:T(8,128)(2,1)} %test_out.11, ...), custom_call_target="tpu_custom_call" | custom-call | flops 603979776 | bytes 9437184 | tf_op jit(solution)/shard_map/project_send0/pallas_call | solution.py:222
  5.8 3.0 %collective-permute-start = (f32[4,256,128]{2,1,0:T(8,128)S(1)}, f32[4,256,128]{2,1,0:T(8,128)S(1)}, u32[]{:S(2)}, u32[]{:S(2)}) collective-permute-start(f32[4,256,128]{2,1,0:T(8,128)S(1)} %project_send0.1.rest_0_), channel_id=1, source_target_pairs={{0,2},{2,0},{4,6},{6,4},{8,10},{10,8},{12,14},{14,12},{1,3},{3,1},... | collective-permute-start | bytes 1572872 | tf_op jit(solution)/shard_map/ppermute | solution.py:526
  8.9 5.2 %project_send256.1.rest_0_ = f32[4,256,128]{2,1,0:T(8,128)S(1)} custom-call(s32[6]{0:T(128)} %rest_6_.1, s32[2]{0:T(128)} %rest_7_.1, bf16[6,1024,3584]{2,1,0:T(8,128)(2,1)} %train_in.11, bf16[6,1024,1024]{2,1,0:T(8,128)(2,1)} %train_out.11, bf16[2,1024,3584]{2,1,0:T(8,128)(2,1)} %test_in.11, bf16[2,1024,1024]{2,1,0:T(8,128)(2,1)} %test_out.11, ...), custom_call_target="tpu_custom_call" | custom-call | flops 603979776 | bytes 9437184 | tf_op jit(solution)/shard_map/project_send256/pallas_call | solution.py:222
  14.2 8.6 %project_keep0_send512.1 = (f32[4,256,128]{2,1,0:T(8,128)S(1)}, f32[4,256,128]{2,1,0:T(8,128)S(1)}) custom-call(s32[6]{0:T(128)} %rest_6_.1, s32[2]{0:T(128)} %rest_7_.1, bf16[6,1024,3584]{2,1,0:T(8,128)(2,1)} %train_in.11, bf16[6,1024,1024]{2,1,0:T(8,128)(2,1)} %train_out.11, bf16[2,1024,3584]{2,1,0:T(8,128)(2,1)} %test_in.11, ...), custom_call_target="tpu_custom_call" | custom-call | flops 1207959552 | bytes 18874368 | tf_op jit(solution)/shard_map/project_keep0_send512/pallas_call | solution.py:222
  22.8 2.1 %collective-permute-start.4 = (f32[4,256,128]{2,1,0:T(8,128)S(1)}, f32[4,256,128]{2,1,0:T(8,128)S(1)}, u32[]{:S(2)}, u32[]{:S(2)}) collective-permute-start(f32[4,256,128]{2,1,0:T(8,128)S(1)} %get-tuple-element.52.rest_0_), channel_id=1, source_target_pairs={{0,2},{2,0},{4,6},{6,4},{8,10},{10,8},{12,14},{14,12},{1,3},{3,1},... | collective-permute-start | bytes 1572872 | tf_op jit(solution)/shard_map/ppermute | solution.py:526
  26.6 5.5 %project_keep256_send768.1 = (f32[4,256,128]{2,1,0:T(8,128)S(1)}, f32[4,128,128]{2,1,0:T(8,128)S(1)}, f32[4,128,128]{2,1,0:T(8,128)S(1)}) custom-call(s32[6]{0:T(128)} %rest_6_.1, s32[2]{0:T(128)} %rest_7_.1, bf16[6,1024,3584]{2,1,0:T(8,128)(2,1)} %train_in.11, bf16[6,1024,1024]{2,1,0:T(8,128)(2,1)} %train_out.11, bf16[2,1024,3584]{2,1,0:T(8,128)(2,1)} %test_in.11, ...), custom_call_target="tpu_custom_call" | custom-call | flops 1207959552 | bytes 18874368 | tf_op jit(solution)/shard_map/project_keep256_send768/pallas_call | solution.py:222
  32.9 2.2 %collective-permute-start.3 = (f32[2,256,128]{2,1,0:T(8,128)S(1)}, f32[2,256,128]{2,1,0:T(8,128)S(1)}, u32[]{:S(2)}, u32[]{:S(2)}) collective-permute-start(f32[2,256,128]{2,1,0:T(8,128)S(1)} %get-tuple-element.58.refs_2_), channel_id=1, source_target_pairs={{0,4},{2,6},{4,0},{6,2},{8,12},{10,14},{12,8},{14,10},{1,5},{3,7},... | collective-permute-start | bytes 786440 | tf_op jit(solution)/shard_map/ppermute | solution.py:527
  35.1 2.7 %collective-permute-start.5 = (f32[1,256,128]{2,1,0:T(8,128)S(1)}, f32[1,256,128]{2,1,0:T(8,128)S(1)}, u32[]{:S(2)}, u32[]{:S(2)}) collective-permute-start(f32[1,256,128]{2,1,0:T(8,128)S(1)} %get-tuple-element.59.rest_1_), channel_id=1, source_target_pairs={{0,8},{2,10},{4,12},{6,14},{8,0},{10,2},{12,4},{14,6},{1,9},{3,11}... | collective-permute-start | bytes 393224 | tf_op jit(solution)/shard_map/ppermute | solution.py:528
  39.8 5.1 %project_keep512.1.refs_0_.rest_0_ = f32[4,256,128]{2,1,0:T(8,128)S(1)} custom-call(s32[6]{0:T(128)} %rest_6_.1, s32[2]{0:T(128)} %rest_7_.1, bf16[6,1024,3584]{2,1,0:T(8,128)(2,1)} %train_in.11, bf16[6,1024,1024]{2,1,0:T(8,128)(2,1)} %train_out.11, bf16[2,1024,3584]{2,1,0:T(8,128)(2,1)} %test_in.11, bf16[2,1024,1024]{2,1,0:T(8,128)(2,1)} %test_out.11, ...), custom_call_target="tpu_custom_call" | custom-call | flops 603979776 | bytes 9437184 | tf_op jit(solution)/shard_map/project_keep512/pallas_call | solution.py:222
  45.0 2.8 %collective-permute-start.8 = (f32[2,256,128]{2,1,0:T(8,128)S(1)}, f32[2,256,128]{2,1,0:T(8,128)S(1)}, u32[]{:S(2)}, u32[]{:S(2)}) collective-permute-start(f32[2,256,128]{2,1,0:T(8,128)S(1)} %get-tuple-element.61.refs_2_), channel_id=1, source_target_pairs={{0,4},{2,6},{4,0},{6,2},{8,12},{10,14},{12,8},{14,10},{1,5},{3,7},... | collective-permute-start | bytes 786440 | tf_op jit(solution)/shard_map/ppermute | solution.py:527
  49.0 5.1 %project_keep768.1.refs_0_ = f32[4,256,128]{2,1,0:T(8,128)S(1)} custom-call(s32[6]{0:T(128)} %rest_6_.1, s32[2]{0:T(128)} %rest_7_.1, bf16[6,1024,3584]{2,1,0:T(8,128)(2,1)} %train_in.11, bf16[6,1024,1024]{2,1,0:T(8,128)(2,1)} %train_out.11, bf16[2,1024,3584]{2,1,0:T(8,128)(2,1)} %test_in.11, bf16[2,1024,1024]{2,1,0:T(8,128)(2,1)} %test_out.11, ...), custom_call_target="tpu_custom_call" | custom-call | flops 603979776 | bytes 9437184 | tf_op jit(solution)/shard_map/project_keep768/pallas_call | solution.py:222
  57.8 3.0 %collective-permute-start.14 = (f32[1,256,128]{2,1,0:T(8,128)S(1)}, f32[1,256,128]{2,1,0:T(8,128)S(1)}, u32[]{:S(2)}, u32[]{:S(2)}) collective-permute-start(f32[1,256,128]{2,1,0:T(8,128)S(1)} %get-tuple-element.68.refs_2_), channel_id=1, source_target_pairs={{0,8},{2,10},{4,12},{6,14},{8,0},{10,2},{12,4},{14,6},{1,9},{3,11}... | collective-permute-start | bytes 393224 | tf_op jit(solution)/shard_map/ppermute | solution.py:528
  62.1 3.0 %collective-permute-done.11.refs_1_ = f32[2,128,128]{2,1,0:T(8,128)S(1)} collective-permute-done((f32[2,128,128]{2,1,0:T(8,128)S(1)}, f32[2,128,128]{2,1,0:T(8,128)S(1)}, u32[]{:S(2)}, u32[]{:S(2)}) %collective-permute-start.11) | collective-permute-done | bytes 131104 | tf_op jit(solution)/shard_map/ppermute | solution.py:527
  65.2 2.9 %collective-permute-start.12 = (f32[1,128,128]{2,1,0:T(8,128)S(1)}, f32[1,128,128]{2,1,0:T(8,128)S(1)}, u32[]{:S(2)}, u32[]{:S(2)}) collective-permute-start(f32[1,128,128]{2,1,0:T(8,128)S(1)} %get-tuple-element.71.refs_2_), channel_id=1, source_target_pairs={{0,8},{2,10},{4,12},{6,14},{8,0},{10,2},{12,4},{14,6},{1,9},{3,11}... | collective-permute-start | bytes 196616 | tf_op jit(solution)/shard_map/ppermute | solution.py:528
  68.1 3.4 %gram_begin.1 = (f32[64,64]{1,0:T(8,128)S(1)}, f32[512,4096]{1,0:T(8,128)S(1)}, s32[8,128]{1,0:T(8,128)S(1)}) custom-call(f32[1,256,128]{2,1,0:T(8,128)S(1)} %get-tuple-element.74.rest_0_, f32[1,256,128]{2,1,0:T(8,128)S(1)} %get-tuple-element.75.rest_1_, f32[1,256,128]{2,1,0:T(8,128)S(1)} %get-tuple-element.76.rest_2_, ...), custom_call_target="tpu_custom_call" | custom-call | tf_op jit(solution)/shard_map/gram_begin/pallas_call | solution.py:337
  72.6 10.1 %all_to_all.35.own = f32[8,32,128]{2,1,0:T(8,128)S(1)} all-to-all(f32[8,32,128]{2,1,0:T(8,128)S(1)} %gram_end.1), channel_id=1, replica_groups={{4,0,6,8,2,10,12,14},{5,1,7,9,3,11,13,15},{20,16,22,24,18,26,28,30},{21..., dimensions={0} | all-to-all | bytes 262144 | tf_op jit(solution)/shard_map/all_to_all | solution.py:566
  84.0 8.4 %all_to_all.36.images = f32[8,8,128]{2,1,0:T(8,128)S(1)} all-to-all(f32[8,8,128]{2,1,0:T(8,128)S(1)} %get-tuple-element.80), channel_id=1, replica_groups={{4,0,6,8,2,10,12,14},{5,1,7,9,3,11,13,15},{20,16,22,24,18,26,28,30},{21..., dimensions={0} | all-to-all | bytes 65536 | tf_op jit(solution)/shard_map/all_to_all | solution.py:573
  92.5 1.9 %first_kernel.1 = (f32[8,8,128]{2,1,0:T(8,128)S(1)}, f32[8,8,128]{2,1,0:T(8,128)S(1)}, f32[8,8,128]{2,1,0:T(8,128)S(1)}, f32[8,8,128]{2,1,0:T(8,128)S(1)}, f32[12,8,8,128]{3,2,1,0:T(8,128)S(1)}) custom-call(f32[8,8,128]{2,1,0:T(8,128)S(1)} %all_to_all.36.images, f32[8,8,128]{2,1,0:T(8,128)S(1)} %get-tuple-element.81.search, ...), custom_call_target="tpu_custom_call" | custom-call | tf_op jit(solution)/shard_map/first_kernel/pallas_call | solution.py:486
  94.3 8.3 %all_to_all.37.images = f32[8,8,128]{2,1,0:T(8,128)S(1)} all-to-all(f32[8,8,128]{2,1,0:T(8,128)S(1)} %get-tuple-element.82), channel_id=1, replica_groups={{4,0,6,8,2,10,12,14},{5,1,7,9,3,11,13,15},{20,16,22,24,18,26,28,30},{21..., dimensions={0} | all-to-all | bytes 65536 | tf_op jit(solution)/shard_map/all_to_all | solution.py:573
  104.3 8.3 %all_to_all.38.images = f32[8,8,128]{2,1,0:T(8,128)S(1)} all-to-all(f32[8,8,128]{2,1,0:T(8,128)S(1)} %get-tuple-element.87), channel_id=1, replica_groups={{4,0,6,8,2,10,12,14},{5,1,7,9,3,11,13,15},{20,16,22,24,18,26,28,30},{21..., dimensions={0} | all-to-all | bytes 65536 | tf_op jit(solution)/shard_map/all_to_all | solution.py:573
  114.2 8.3 %all_to_all.39.images = f32[8,8,128]{2,1,0:T(8,128)S(1)} all-to-all(f32[8,8,128]{2,1,0:T(8,128)S(1)} %get-tuple-element.91), channel_id=1, replica_groups={{4,0,6,8,2,10,12,14},{5,1,7,9,3,11,13,15},{20,16,22,24,18,26,28,30},{21..., dimensions={0} | all-to-all | bytes 65536 | tf_op jit(solution)/shard_map/all_to_all | solution.py:573
  122.5 1.8 %step_kernel.5 = (f32[8,8,128]{2,1,0:T(8,128)S(1)}, f32[8,8,128]{2,1,0:T(8,128)S(1)}, f32[8,8,128]{2,1,0:T(8,128)S(1)}, f32[8,8,128]{2,1,0:T(8,128)S(1)}) custom-call(f32[8,8,128]{2,1,0:T(8,128)S(1)} %all_to_all.39.images, f32[8,8,128]{2,1,0:T(8,128)S(1)} %get-tuple-element.92.solution, f32[8,8,128]{2,1,0:T(8,128)S(1)} %get-tuple-element.93.residue, ...), custom_call_target="tpu_custom_call" | custom-call | tf_op jit(solution)/shard_map/step_kernel/pallas_call | solution.py:486
  124.3 8.3 %all_to_all.40.images = f32[8,8,128]{2,1,0:T(8,128)S(1)} all-to-all(f32[8,8,128]{2,1,0:T(8,128)S(1)} %get-tuple-element.95), channel_id=1, replica_groups={{4,0,6,8,2,10,12,14},{5,1,7,9,3,11,13,15},{20,16,22,24,18,26,28,30},{21..., dimensions={0} | all-to-all | bytes 65536 | tf_op jit(solution)/shard_map/all_to_all | solution.py:573
  134.3 8.3 %all_to_all.41.curves = f32[8,8,128]{2,1,0:T(8,128)S(1)} all-to-all(f32[8,8,128]{2,1,0:T(8,128)S(1)} %get-tuple-element.99), channel_id=1, replica_groups={{4,0,6,8,2,10,12,14},{5,1,7,9,3,11,13,15},{20,16,22,24,18,26,28,30},{21..., dimensions={0} | all-to-all | bytes 65536 | tf_op jit(solution)/shard_map/all_to_all | solution.py:573
  (40 shorter events, 19.1 us)
Async XLA Ops:
  5.8 19.0 %collective-permute-start = (f32[4,256,128]{2,1,0:T(8,128)S(1)}, f32[4,256,128]{2,1,0:T(8,128)S(1)}, u32[]{:S(2)}, u32[]{:S(2)}) collective-permute-start(f32[4,256,128]{2,1,0:T(8,128)S(1)} %project_send0.1.rest_0_), channel_id=1, source_target_pairs={{0,2},{2,0},{4,6},{6,4},{8,10},{10,8},{12,14},{14,12},{1,3},{3,1},... | collective-permute-start | bytes 1572872 | tf_op jit(solution)/shard_map/ppermute | solution.py:526
  14.1 18.8 %collective-permute-start.2 = (f32[4,256,128]{2,1,0:T(8,128)S(1)}, f32[4,256,128]{2,1,0:T(8,128)S(1)}, u32[]{:S(2)}, u32[]{:S(2)}) collective-permute-start(f32[4,256,128]{2,1,0:T(8,128)S(1)} %project_send256.1.rest_0_), channel_id=1, source_target_pairs={{0,2},{2,0},{4,6},{6,4},{8,10},{10,8},{12,14},{14,12},{1,3},{3,1},... | collective-permute-start | bytes 1572872 | tf_op jit(solution)/shard_map/ppermute | solution.py:526
  22.8 22.1 %collective-permute-start.4 = (f32[4,256,128]{2,1,0:T(8,128)S(1)}, f32[4,256,128]{2,1,0:T(8,128)S(1)}, u32[]{:S(2)}, u32[]{:S(2)}) collective-permute-start(f32[4,256,128]{2,1,0:T(8,128)S(1)} %get-tuple-element.52.rest_0_), channel_id=1, source_target_pairs={{0,2},{2,0},{4,6},{6,4},{8,10},{10,8},{12,14},{14,12},{1,3},{3,1},... | collective-permute-start | bytes 1572872 | tf_op jit(solution)/shard_map/ppermute | solution.py:526
  24.9 10.2 %collective-permute-start.1 = (f32[2,256,128]{2,1,0:T(8,128)S(1)}, f32[2,256,128]{2,1,0:T(8,128)S(1)}, u32[]{:S(2)}, u32[]{:S(2)}) collective-permute-start(f32[2,256,128]{2,1,0:T(8,128)S(1)} %get-tuple-element.54.rest_1_), channel_id=1, source_target_pairs={{0,4},{2,6},{4,0},{6,2},{8,12},{10,14},{12,8},{14,10},{1,5},{3,7},... | collective-permute-start | bytes 786440 | tf_op jit(solution)/shard_map/ppermute | solution.py:527
  32.9 14.9 %collective-permute-start.3 = (f32[2,256,128]{2,1,0:T(8,128)S(1)}, f32[2,256,128]{2,1,0:T(8,128)S(1)}, u32[]{:S(2)}, u32[]{:S(2)}) collective-permute-start(f32[2,256,128]{2,1,0:T(8,128)S(1)} %get-tuple-element.58.refs_2_), channel_id=1, source_target_pairs={{0,4},{2,6},{4,0},{6,2},{8,12},{10,14},{12,8},{14,10},{1,5},{3,7},... | collective-permute-start | bytes 786440 | tf_op jit(solution)/shard_map/ppermute | solution.py:527
  35.1 9.8 %collective-permute-start.5 = (f32[1,256,128]{2,1,0:T(8,128)S(1)}, f32[1,256,128]{2,1,0:T(8,128)S(1)}, u32[]{:S(2)}, u32[]{:S(2)}) collective-permute-start(f32[1,256,128]{2,1,0:T(8,128)S(1)} %get-tuple-element.59.rest_1_), channel_id=1, source_target_pairs={{0,8},{2,10},{4,12},{6,14},{8,0},{10,2},{12,4},{14,6},{1,9},{3,11}... | collective-permute-start | bytes 393224 | tf_op jit(solution)/shard_map/ppermute | solution.py:528
  37.8 16.4 %collective-permute-start.6 = (f32[4,128,128]{2,1,0:T(8,128)S(1)}, f32[4,128,128]{2,1,0:T(8,128)S(1)}, u32[]{:S(2)}, u32[]{:S(2)}) collective-permute-start(f32[4,128,128]{2,1,0:T(8,128)S(1)} %get-tuple-element.63), channel_id=1, source_target_pairs={{0,2},{2,0},{4,6},{6,4},{8,10},{10,8},{12,14},{14,12},{1,3},{3,1},... | collective-permute-start | bytes 786440 | tf_op jit(solution)/shard_map/ppermute | solution.py:526
  39.3 15.4 %collective-permute-start.9 = (f32[4,128,128]{2,1,0:T(8,128)S(1)}, f32[4,128,128]{2,1,0:T(8,128)S(1)}, u32[]{:S(2)}, u32[]{:S(2)}) collective-permute-start(f32[4,128,128]{2,1,0:T(8,128)S(1)} %get-tuple-element.55.rest_0_), channel_id=1, source_target_pairs={{0,2},{2,0},{4,6},{6,4},{8,10},{10,8},{12,14},{14,12},{1,3},{3,1},... | collective-permute-start | bytes 786440 | tf_op jit(solution)/shard_map/ppermute | solution.py:526
  45.0 12.7 %collective-permute-start.8 = (f32[2,256,128]{2,1,0:T(8,128)S(1)}, f32[2,256,128]{2,1,0:T(8,128)S(1)}, u32[]{:S(2)}, u32[]{:S(2)}) collective-permute-start(f32[2,256,128]{2,1,0:T(8,128)S(1)} %get-tuple-element.61.refs_2_), channel_id=1, source_target_pairs={{0,4},{2,6},{4,0},{6,2},{8,12},{10,14},{12,8},{14,10},{1,5},{3,7},... | collective-permute-start | bytes 786440 | tf_op jit(solution)/shard_map/ppermute | solution.py:527
  47.8 9.5 %collective-permute-start.10 = (f32[1,256,128]{2,1,0:T(8,128)S(1)}, f32[1,256,128]{2,1,0:T(8,128)S(1)}, u32[]{:S(2)}, u32[]{:S(2)}) collective-permute-start(f32[1,256,128]{2,1,0:T(8,128)S(1)} %get-tuple-element.62.rest_1_.refs_2_), channel_id=1, source_target_pairs={{0,8},{2,10},{4,12},{6,14},{8,0},{10,2},{12,4},{14,6},{1,9},{3,11}... | collective-permute-start | bytes 393224 | tf_op jit(solution)/shard_map/ppermute | solution.py:528
  54.2 7.9 %collective-permute-start.7 = (f32[2,128,128]{2,1,0:T(8,128)S(1)}, f32[2,128,128]{2,1,0:T(8,128)S(1)}, u32[]{:S(2)}, u32[]{:S(2)}) collective-permute-start(f32[2,128,128]{2,1,0:T(8,128)S(1)} %get-tuple-element.65.refs_2_), channel_id=1, source_target_pairs={{0,4},{2,6},{4,0},{6,2},{8,12},{10,14},{12,8},{14,10},{1,5},{3,7},... | collective-permute-start | bytes 393224 | tf_op jit(solution)/shard_map/ppermute | solution.py:527
  54.8 10.3 %collective-permute-start.11 = (f32[2,128,128]{2,1,0:T(8,128)S(1)}, f32[2,128,128]{2,1,0:T(8,128)S(1)}, u32[]{:S(2)}, u32[]{:S(2)}) collective-permute-start(f32[2,128,128]{2,1,0:T(8,128)S(1)} %get-tuple-element.67.refs_2_), channel_id=1, source_target_pairs={{0,4},{2,6},{4,0},{6,2},{8,12},{10,14},{12,8},{14,10},{1,5},{3,7},... | collective-permute-start | bytes 393224 | tf_op jit(solution)/shard_map/ppermute | solution.py:527
  57.8 10.3 %collective-permute-start.14 = (f32[1,256,128]{2,1,0:T(8,128)S(1)}, f32[1,256,128]{2,1,0:T(8,128)S(1)}, u32[]{:S(2)}, u32[]{:S(2)}) collective-permute-start(f32[1,256,128]{2,1,0:T(8,128)S(1)} %get-tuple-element.68.refs_2_), channel_id=1, source_target_pairs={{0,8},{2,10},{4,12},{6,14},{8,0},{10,2},{12,4},{14,6},{1,9},{3,11}... | collective-permute-start | bytes 393224 | tf_op jit(solution)/shard_map/ppermute | solution.py:528
  65.1 6.4 %collective-permute-start.13 = (f32[1,128,128]{2,1,0:T(8,128)S(1)}, f32[1,128,128]{2,1,0:T(8,128)S(1)}, u32[]{:S(2)}, u32[]{:S(2)}) collective-permute-start(f32[1,128,128]{2,1,0:T(8,128)S(1)} %get-tuple-element.73), channel_id=1, source_target_pairs={{0,8},{2,10},{4,12},{6,14},{8,0},{10,2},{12,4},{14,6},{1,9},{3,11}... | collective-permute-start | bytes 196616 | tf_op jit(solution)/shard_map/ppermute | solution.py:528
  65.2 7.0 %collective-permute-start.12 = (f32[1,128,128]{2,1,0:T(8,128)S(1)}, f32[1,128,128]{2,1,0:T(8,128)S(1)}, u32[]{:S(2)}, u32[]{:S(2)}) collective-permute-start(f32[1,128,128]{2,1,0:T(8,128)S(1)} %get-tuple-element.71.refs_2_), channel_id=1, source_target_pairs={{0,8},{2,10},{4,12},{6,14},{8,0},{10,2},{12,4},{14,6},{1,9},{3,11}... | collective-permute-start | bytes 196616 | tf_op jit(solution)/shard_map/ppermute | solution.py:528
  82.7 9.8 %collective-permute-start.15 = (f32[8,32,128]{2,1,0:T(8,128)S(1)}, f32[8,32,128]{2,1,0:T(8,128)S(1)}, u32[]{:S(2)}, u32[]{:S(2)}) collective-permute-start(f32[8,32,128]{2,1,0:T(8,128)S(1)} %all_to_all.35.own), channel_id=1, source_target_pairs={{0,1},{1,0},{2,3},{3,2},{4,5},{5,4},{6,7},{7,6},{8,9},{9,8},{10,11... | collective-permute-start | bytes 393224 | tf_op jit(solution)/shard_map/ppermute | solution.py:567
